TPU v7x, 512 devices: a whole 4x4x16 slice. The times are simulated.
512 devices in a mesh: row: 16 (over y, x), col: 32 (over z, core).
Axes of the slice: x: 4, y: 4, z: 16, core: 2. Of those that a mesh axis runs over, the one named last changes fastest.
Arguments:
- kernel: float32 [8192, 8192], P('row', 'col'), as said below
Outputs:
- factored: float32 [8192, 8192], P('row', 'col')
Inputs may be any that keep to these rules, and one draw needn't show every extreme that they name: In G's order the kernel is symmetric, and the diagonal blocks met by the 2 steps are positive definite and well conditioned.
All inputs are finite; a program needn't handle non-finite values.
Results may differ from a plain program's by a relative error of at most 0.0001.
Values sent between devices are 32-bit elements; how exact they have to be, the bound alone decides.
No kernel may reach another device: no remote copies, remote signals or barrier semaphores. Data moves between devices by JAX's collectives and lax.ppermute only.
A program may use at most 64 MiB of HBM per device.

v0:
```python
import jax
import jax.numpy as jnp
from jax import lax
from jax.sharding import PartitionSpec as P

NB = 256
PANELS = 2


FULL_PRECISION = lax.Precision.HIGHEST


def from_root(value, axis, root):
    mine = lax.axis_index(axis) == root
    return lax.psum(jnp.where(mine, value, jnp.zeros_like(value)), axis)


def factor_block(square):
    diag_factor = jnp.linalg.cholesky(square)
    identity = jnp.eye(square.shape[0], dtype=square.dtype)
    inverse = jax.scipy.linalg.solve_triangular(diag_factor, identity, lower=True)
    return (diag_factor, inverse)


def place_blocks(values, block_ids, step, diag_factor):
    count = block_ids.shape[0]
    width = diag_factor.shape[0]
    shaped = values.reshape(count, width, width)
    labels = block_ids[:, None, None]
    kept = jnp.where(
        labels > step, shaped, jnp.where(labels == step, diag_factor[None], jnp.zeros_like(shaped))
    )
    return kept.reshape(count * width, width)


def turn_panel(panel_rows, col_blocks, row_count):
    target = col_blocks[0]
    offset = target // row_count * NB
    piece = lax.dynamic_slice_in_dim(panel_rows, offset, NB, 0)
    pieces = from_root(piece, "row", target % row_count)
    return pieces


def local(kernel):
    rows_dev, cols_dev = kernel.shape
    row_count = lax.axis_size("row")
    col_count = lax.axis_size("col")
    row_blocks = jnp.arange(rows_dev // NB, dtype=jnp.int32) * row_count + lax.axis_index("row")
    col_blocks = jnp.arange(cols_dev // NB, dtype=jnp.int32) * col_count + lax.axis_index("col")
    row_of = jnp.repeat(row_blocks, NB)
    col_of = jnp.repeat(col_blocks, NB)
    current = kernel
    for step in range(PANELS):
        diag_factor, inverse = factor_block(current[:NB, :NB])
        inverse = from_root(inverse, "row", step)
        panel_rows = lax.dot_general(
            current, inverse, (((1,), (1,)), ((), ())), precision=FULL_PRECISION
        )
        panel_rows = place_blocks(panel_rows, row_blocks, step, diag_factor)
        rows_panel = from_root(panel_rows, "col", step)
        cols_panel = turn_panel(rows_panel, col_blocks, row_count)
        product = lax.dot_general(
            rows_panel, cols_panel, (((1,), (1,)), ((), ())), precision=FULL_PRECISION
        )
        trailing = jnp.where(row_of[:, None] > step, current - product, jnp.zeros_like(current))
        refilled = jnp.concatenate([rows_panel, current[:, NB:]], axis=1)
        current = jnp.where(
            col_of[None, :] < step, current, jnp.where(col_of[None, :] == step, refilled, trailing)
        )
    return current


def solution(mesh):
    placed = (P("row", "col"),)
    return jax.shard_map(
        local, mesh=mesh, in_specs=placed, out_specs=P("row", "col"), check_vma=False
    )
```

profile of v0, /device:TPU:1, one launch (start us, length us, event | category | flops | bytes accessed | tf_op | source)
XLA Modules:
  0.0 1033.9 jit_solution(9264166148345210578)
XLA Ops:
  6.6 1.2 copy.8
  8.0 11.7 %cholesky.130 = f32[128,128]{1,0:T(8,128)S(1)} custom-call(f32[128,128]{1,0:T(8,128)S(1)} %cholesky.194), custom_call_target="Cholesky" | custom-call | tf_op jit(solution)/shard_map/jit(cholesky)/cholesky | solution.py:19
  19.8 9.8 custom-call.13
  30.1 11.7 %cholesky.147 = f32[128,128]{1,0:T(8,128)S(1)} custom-call(f32[128,128]{1,0:T(8,128)S(1)} %convolution_subtract_fusion.5), custom_call_target="Cholesky" | custom-call | tf_op jit(solution)/shard_map/jit(cholesky)/cholesky | solution.py:19
  41.9 0.7 compare_reduce_fusion.2
  44.0 4.3 while.4
  44.8 1.3 bitcast_dynamic-update-slice_fusion.4
  46.9 1.3 bitcast_dynamic-update-slice_fusion.4
  48.2 19.7 %custom-call.14 = f32[2,128,128]{1,2,0:T(8,128)S(1)} custom-call(f32[2,128,128]{2,1,0:T(8,128)S(1)} %get-tuple-element.21), custom_call_target="InvertDiagBlocksLowerTriangular" | custom-call | tf_op jit(solution)/shard_map/jit(_solve_triangular)/triangular_solve | solution.py:21
  69.0 0.7 maximum_select_fusion
  70.4 118.5 %all-reduce.8.cloned.1.call-done = f32[256,256]{0,1:T(8,128)} async-done(((f32[256,256]{0,1:T(8,128)}), f32[256,256]{0,1:T(8,128)}) %all-reduce.8.cloned.1.call-update) | async-done | bytes 262160 | tf_op jit(solution)/shard_map/psum | solution.py:15
  188.9 2.8 fusion.2
  191.8 208.9 %all-reduce.10.cloned.1.call-done = f32[512,256]{0,1:T(8,128)} async-done(((f32[512,256]{0,1:T(8,128)}), f32[512,256]{0,1:T(8,128)}) %all-reduce.10.cloned.1.call-update) | async-done | bytes 524304 | tf_op jit(solution)/shard_map/psum | solution.py:15
  400.7 1.7 dynamic-slice_select_fusion.1
  402.6 114.8 %all-reduce.12.cloned.1.call-done = f32[256,256]{0,1:T(8,128)} async-done(((f32[256,256]{0,1:T(8,128)}), f32[256,256]{0,1:T(8,128)}) %all-reduce.12.cloned.1.call-update) | async-done | bytes 262160 | tf_op jit(solution)/shard_map/psum | solution.py:15
  517.3 1.6 fusion.8
  519.2 11.7 %cholesky.164 = f32[128,128]{1,0:T(8,128)S(1)} custom-call(f32[128,128]{1,0:T(8,128)S(1)} %cholesky.197), custom_call_target="Cholesky" | custom-call | tf_op jit(solution)/shard_map/jit(cholesky)/cholesky | solution.py:19
  531.0 9.8 custom-call.15
  541.3 11.7 %cholesky.181 = f32[128,128]{1,0:T(8,128)S(1)} custom-call(f32[128,128]{1,0:T(8,128)S(1)} %convolution_subtract_fusion.4), custom_call_target="Cholesky" | custom-call | tf_op jit(solution)/shard_map/jit(cholesky)/cholesky | solution.py:19
  553.0 0.7 compare_reduce_fusion
  555.8 4.3 while.5
  556.6 1.4 bitcast_dynamic-update-slice_fusion.5
  558.7 1.4 bitcast_dynamic-update-slice_fusion.5
  560.1 19.7 %custom-call.16 = f32[2,128,128]{1,2,0:T(8,128)S(1)} custom-call(f32[2,128,128]{2,1,0:T(8,128)S(1)} %get-tuple-element.22), custom_call_target="InvertDiagBlocksLowerTriangular" | custom-call | tf_op jit(solution)/shard_map/jit(_solve_triangular)/triangular_solve | solution.py:21
  580.9 0.7 maximum_select_fusion.1
  582.3 113.9 %all-reduce.14.cloned.1.call-done = f32[256,256]{0,1:T(8,128)} async-done(((f32[256,256]{0,1:T(8,128)}), f32[256,256]{0,1:T(8,128)}) %all-reduce.14.cloned.1.call-update) | async-done | bytes 262160 | tf_op jit(solution)/shard_map/psum | solution.py:15
  696.2 2.4 fusion
  698.7 209.0 %all-reduce.16.cloned.1.call-done = f32[512,256]{0,1:T(8,128)} async-done(((f32[512,256]{0,1:T(8,128)}), f32[512,256]{0,1:T(8,128)}) %all-reduce.16.cloned.1.call-update) | async-done | bytes 524304 | tf_op jit(solution)/shard_map/psum | solution.py:15
  907.7 1.7 dynamic-slice_select_fusion
  909.5 115.0 %all-reduce.18.cloned.1.call-done = f32[256,256]{0,1:T(8,128)} async-done(((f32[256,256]{0,1:T(8,128)}), f32[256,256]{0,1:T(8,128)}) %all-reduce.18.cloned.1.call-update) | async-done | bytes 262160 | tf_op jit(solution)/shard_map/psum | solution.py:15
  1024.4 1.6 fusion.5
  1026.1 1.0 copy.14
  (76 shorter events, 8.4 us)
Async XLA Ops:
  6.5 182.3 %all-reduce.8.cloned.1.call-start = ((), (), s32[]{:S(2)}) async-start(), calls=%async_computation | async-start | bytes 524288 | tf_op jit(solution)/shard_map/psum | solution.py:15
  69.7 331.0 %all-reduce.10.cloned.1.call-start = ((), (), s32[]{:S(2)}) async-start(), calls=%async_computation.1 | async-start | bytes 1048576 | tf_op jit(solution)/shard_map/psum | solution.py:15
  70.1 118.8 %copy-start = (f32[512,256]{1,0:T(8,128)S(1)}, f32[512,256]{1,0:T(8,128)}, u32[]{:S(2)}) copy-start(f32[512,256]{1,0:T(8,128)} %param.4) | copy-start | bytes 1572868
  191.7 325.6 %all-reduce.12.cloned.1.call-start = ((), (), s32[]{:S(2)}) async-start(), calls=%async_computation.2 | async-start | bytes 524288 | tf_op jit(solution)/shard_map/psum | solution.py:15
  400.7 116.6 %copy-start.1 = (f32[512,256]{0,1:T(8,128)S(1)}, f32[512,256]{0,1:T(8,128)}, u32[]{:S(2)}) copy-start(f32[512,256]{0,1:T(8,128)} %all-reduce.10.cloned.1.call-done) | copy-start | bytes 1572868
  402.5 293.7 %all-reduce.14.cloned.1.call-start = ((), (), s32[]{:S(2)}) async-start(), calls=%async_computation.3 | async-start | bytes 524288 | tf_op jit(solution)/shard_map/psum | solution.py:15
  581.6 326.1 %all-reduce.16.cloned.1.call-start = ((), (), s32[]{:S(2)}) async-start(), calls=%async_computation.4 | async-start | bytes 1048576 | tf_op jit(solution)/shard_map/psum | solution.py:15
  698.6 325.8 %all-reduce.18.cloned.1.call-start = ((), (), s32[]{:S(2)}) async-start(), calls=%async_computation.5 | async-start | bytes 524288 | tf_op jit(solution)/shard_map/psum | solution.py:15
  907.7 116.8 %copy-start.2 = (f32[512,256]{0,1:T(8,128)S(1)}, f32[512,256]{0,1:T(8,128)}, u32[]{:S(2)}) copy-start(f32[512,256]{0,1:T(8,128)} %all-reduce.16.cloned.1.call-done) | copy-start | bytes 1572868
Sparse Core Ops, SparseCore 0:
  69.9 118.9 all-reduce.7
  191.8 208.8 all-reduce.9
  403.9 113.3 all-reduce.11
  581.8 114.3 all-reduce.13
  698.8 208.8 all-reduce.15
  911.0 113.3 all-reduce.17
where the time goes:
time: 1030 us
  waiting for transfers between devices  880 us (85%)
  other arithmetic  113 us (11%)
  between operations  16.5 us (2%)
  local copies, waits for them, and re-layouts  12 us (1%)
  matrix products  11.4 us (1%)
    psum x6, waiting for transfers between devices, from_root(): return lax.psum(jnp.where(mine, value, jnp.zeros_like(value)), axis)  880 us
    another operation x13, other arithmetic, factor_block(): diag_factor = jnp.linalg.cholesky(square)  68.7 us
    another operation x5, other arithmetic, factor_block(): jax.scipy.linalg.solve_triangular(diag_factor, identity, lower=True)  39.4 us
  transfers between devices with their start and end apart: 6, of which 6 were waited for; matrix products, arithmetic and copies ran while one was open for 0% of the time, Pallas kernels for 0%

commit v1 on v0

v1 whole, which is shorter than its diff:
```python
import jax
import jax.numpy as jnp
from jax import lax
from jax.experimental import pallas as pl
from jax.experimental.pallas import tpu as pltpu
from jax.sharding import PartitionSpec as P

NB = 256
BASE = 32
LANES = 128
SUBS = 8
HIGHEST = lax.Precision.HIGHEST
VMEM_LIMIT = 24 * 1024 * 1024

CHIPS_Z = 16
PANEL_TREE = (
    ((0, 7),),
    ((0, 4), (7, 11)),
    ((0, 2), (4, 6), (7, 9), (11, 13)),
    ((0, 15), (2, 1), (4, 3), (6, 5), (7, 8), (9, 10), (11, 12), (13, 14)),
)
PIECE_TREE = (
    (((0, 8),), ((0, 4),), ((0, 12),)),
    (
        tuple((s, s + 2) for s in (0, 4, 8, 12)),
        tuple((s, (s + 15) % 16) for s in (0, 4, 8, 12)),
        tuple((s, s + 1) for s in (0, 4, 8, 12)),
    ),
)


def product(a, b, a_dim, b_dim):
    return lax.dot_general(
        a,
        b,
        (((a_dim,), (b_dim,)), ((), ())),
        precision=HIGHEST,
        preferred_element_type=jnp.float32,
    )


def small_inverse(rows, off):
    groups = BASE // SUBS
    lane = lax.broadcasted_iota(jnp.int32, (SUBS, LANES), 1)
    sub = lax.broadcasted_iota(jnp.int32, (SUBS, LANES), 0)
    cols = [[None] * groups for _ in range(BASE)]
    for c in range(BASE):
        for q in range(c // SUBS, groups):
            piece = rows[SUBS * q : SUBS * q + SUBS, off + c : off + c + 1]
            cols[c][q] = jnp.broadcast_to(piece, (SUBS, LANES))
    inv = [jnp.where(lane == sub + (off + SUBS * q), 1.0, 0.0) for q in range(groups)]
    scale = []
    for k in range(BASE):
        qk, rk = divmod(k, SUBS)
        root = lax.rsqrt(jnp.broadcast_to(cols[k][qk][rk : rk + 1], (SUBS, LANES)))
        recip = root * root
        for c in range(k + 1, BASE):
            qc, rc = divmod(c, SUBS)
            factor = jnp.broadcast_to(cols[k][qc][rc : rc + 1], (SUBS, LANES)) * recip
            for q in range(qc, groups):
                cols[c][q] = cols[c][q] - cols[k][q] * factor
        row = jnp.broadcast_to(inv[qk][rk : rk + 1], (SUBS, LANES)) * recip
        for q in range(qk, groups):
            update = cols[k][q] * row
            if q == qk:
                update = jnp.where(sub > rk, update, 0.0)
            inv[q] = inv[q] - update
        scale.append(root)
    out = []
    for q in range(groups):
        factor = scale[SUBS * q]
        for r in range(1, SUBS):
            factor = jnp.where(sub == r, scale[SUBS * q + r], factor)
        out.append(inv[q] * factor)
    return jnp.concatenate(out, axis=0)


def inverse_factor(square, out_ref, work):
    rows = lax.broadcasted_iota(jnp.int32, (NB, NB), 0)
    cols = lax.broadcasted_iota(jnp.int32, (NB, NB), 1)
    work[:, :NB] = square
    work[:, NB:] = jnp.where(rows == cols, 1.0, 0.0)
    for low in range(0, NB, BASE):
        tile = low // LANES * LANES
        off = low - tile
        high = low + BASE
        small = small_inverse(work[low:high, tile : tile + LANES], off)
        strip = product(small[:, off : off + BASE], work[low:high, :], 1, 0)
        out_ref[low:high, :] = strip[:, NB:]
        if high < NB:
            work[high:, :] = work[high:, :] - product(strip[:, high:NB], strip, 0, 0)


def first_kernel(square_ref, inv_ref, work):
    inverse_factor(square_ref[...], inv_ref, work)


def second_kernel(inv0_ref, upper_ref, square_ref, turned_ref, inv_ref, work):
    turned = product(inv0_ref[...], upper_ref[...], 1, 0)
    turned_ref[...] = turned
    inverse_factor(square_ref[...] - product(turned, turned, 0, 0), inv_ref, work)


def final_kernel(mine_ref, own_ref, other_ref, cols_ref, inv0_ref, turned_ref, inv1_ref, out_ref):
    row = lax.axis_index("row")
    col = lax.axis_index("col")
    core0 = lax.rem(col, 2) == 0
    rows_in = lax.broadcasted_iota(jnp.int32, (NB, NB), 0)
    cols_in = lax.broadcasted_iota(jnp.int32, (NB, NB), 1)
    inv0 = inv0_ref[...]
    turned = turned_ref[...]
    inv1 = inv1_ref[...]
    right0 = product(inv0, cols_ref[0], 1, 0)
    right1 = product(inv1, cols_ref[1] - product(turned, right0, 0, 0), 1, 0)
    for block in range(2):
        place = pl.ds(block * NB, NB)
        label = row + 16 * block
        own = own_ref[place, :]
        other = other_ref[place, :]
        panel0 = jnp.where(core0, own, other)
        panel1 = jnp.where(core0, other, own)
        left0 = product(panel0, inv0, 1, 1)
        left1 = product(panel1 - product(left0, turned, 1, 0), inv1, 1, 1)

        @pl.when(col >= 2)
        def _():
            trailing = mine_ref[place, :] - product(left0, right0, 1, 0) - product(left1, right1, 1, 0)
            out_ref[place, :] = jnp.where(label >= 2, trailing, 0.0)

        @pl.when(col < 2)
        def _():
            panel = jnp.where(col == 0, left0, left1)
            keep = (label > col) | ((label == col) & (rows_in >= cols_in))
            out_ref[place, :] = jnp.where(keep, panel, 0.0)


def call(body, outs, scratch):
    return pl.pallas_call(
        body,
        out_shape=outs,
        scratch_shapes=scratch,
        compiler_params=pltpu.CompilerParams(vmem_limit_bytes=VMEM_LIMIT),
    )


def both_cores(pairs, mirror):
    out = []
    for s, t in pairs:
        out.append((2 * s, 2 * t))
        if mirror:
            s, t = (CHIPS_Z - s) % CHIPS_Z, (CHIPS_Z - t) % CHIPS_Z
        out.append((2 * s + 1, 2 * t + 1))
    return out


def swap_cores(value):
    return lax.ppermute(value, "col", [(c, c ^ 1) for c in range(2 * CHIPS_Z)])


def local(kernel):
    square = jax.ShapeDtypeStruct((NB, NB), jnp.float32)
    work = [pltpu.VMEM((NB, 2 * NB), jnp.float32)]
    col = lax.axis_index("col")
    bottom = col < 2
    core0 = col % 2 == 0

    panel = jnp.where(bottom, kernel, 0.0)
    scattered = lax.all_to_all(kernel[:NB].reshape(16, 16, NB), "row", 0, 0)
    pieces = scattered[:2]
    swapped = swap_cores(pieces)
    lead = jnp.stack(
        [
            jnp.where(core0, pieces[0], swapped[0]),
            jnp.where(core0, swapped[0], pieces[0]),
            jnp.where(core0, swapped[1], pieces[1]),
        ]
    )
    lead = jnp.where(bottom, lead, 0.0)
    for stage in PIECE_TREE:
        lead = lead + sum(lax.ppermute(lead, "col", both_cores(p, False)) for p in stage)
    mine = jnp.concatenate([pieces, lead])
    gathered = lax.all_to_all(jnp.broadcast_to(mine[None], (16,) + mine.shape), "row", 0, 0)
    gathered = gathered.transpose(1, 0, 2, 3).reshape(5, NB, NB)

    for pairs in PANEL_TREE:
        panel = panel + lax.ppermute(panel, "col", both_cores(pairs, True))
    other = swap_cores(panel)

    inv0 = call(first_kernel, square, work)(gathered[2])
    turned, inv1 = call(second_kernel, (square, square), work)(inv0, gathered[3], gathered[4])
    return call(final_kernel, jax.ShapeDtypeStruct(kernel.shape, jnp.float32), [])(
        kernel, panel, other, gathered[:2], inv0, turned, inv1
    )


def solution(mesh):
    return jax.shard_map(
        local, mesh=mesh, in_specs=(P("row", "col"),), out_specs=P("row", "col"), check_vma=False
    )
```

time: 1030 us -> 105 us (0.10)
  waiting for transfers between devices: 880 us -> 16.6 us
  other arithmetic: 113 us -> 0.37 us
  starting transfers between devices: 0.21 us -> 57.6 us
  Pallas kernels: 0 us -> 26 us
  between operations: 16.5 us -> 0.28 us
  matrix products: 11.4 us -> 0 us
    psum x6 -> x0, waiting for transfers between devices: 880 us -> none  [from_root(): return lax.psum(jnp.where(mine, value, jnp.zeros_like(value)), axis)]
    another operation x18 -> x0, other arithmetic: 108 us -> none  [the longest x13 68.7 us: factor_block(): diag_factor = jnp.linalg.cholesky(square)]
    ppermute x0 -> x12, starting transfers between devices: none -> 46.3 us  [the longest x4 23.8 us: local(): panel = panel + lax.ppermute(panel, 'col', both_cores(pairs, True))]
    pallas_call x0 -> x3, Pallas kernels: none -> 26 us  [the longest x1 11.2 us: local(): call(second_kernel, (square, square), work)(inv0, gathered[3], gathered[4])]
    ppermute x0 -> x12, waiting for transfers between devices: none -> 11.5 us  [the longest x4 7.18 us: local(): panel = panel + lax.ppermute(panel, 'col', both_cores(pairs, True))]
    all_to_all x0 -> x2, starting transfers between devices: none -> 11.3 us  [the longest x1 7.58 us: local(): scattered = lax.all_to_all(kernel[:NB].reshape(16, 16, NB), 'row', 0, 0)]
  transfers between devices with their start and end apart: 6 -> 14, of which waited for: 6 -> 5; matrix products, arithmetic and copies ran while one was open for 0% -> 2% of each run, Pallas kernels for 0% -> 20%
where the time goes in v1:
time: 105 us; the launch traced here: 104 us
  starting transfers between devices  57.6 us (55%)
  Pallas kernels  26 us (25%)
  waiting for transfers between devices  16.6 us (16%)
  local copies, waits for them, and re-layouts  3.13 us (3%)
    ppermute x4, starting transfers between devices, local(): panel = panel + lax.ppermute(panel, 'col', both_cores(pairs, True))  23.8 us
    ppermute x6, starting transfers between devices, local(): lax.ppermute(lead, 'col', both_cores(p, False))  16.1 us
    pallas_call x1, Pallas kernels, local(): call(second_kernel, (square, square), work)(inv0, gathered[3], gathered[4])  11.2 us
    pallas_call x1, Pallas kernels, local(): inv0 = call(first_kernel, square, work)(gathered[2])  9.98 us
    all_to_all x1, starting transfers between devices, local(): scattered = lax.all_to_all(kernel[:NB].reshape(16, 16, NB), 'row', 0, 0)  7.58 us
    ppermute x4, waiting for transfers between devices, local(): panel = panel + lax.ppermute(panel, 'col', both_cores(pairs, True))  7.18 us
    ppermute x2, starting transfers between devices, swap_cores(): return lax.ppermute(value, 'col', [(c, c ^ 1) for c in range(2 * CHIPS_Z)])  6.44 us
    all_to_all x1, waiting for transfers between devices, local(): lax.all_to_all(jnp.broadcast_to(mine[None], (16,) + mine.shape), 'row', 0...  5.07 us
  transfers between devices with their start and end apart: 14, of which 5 were waited for; matrix products, arithmetic and copies ran while one was open for 2% of the time, Pallas kernels for 20%

profile of v1, /device:TPU:1, one launch (start us, length us, event | category | flops | bytes accessed | tf_op | source)
XLA Modules:
  0.0 103.9 jit_solution(7569964972859616740)
XLA Ops:
  0.0 1.7 %slice.40 = f32[256,256]{1,0:T(8,128)} slice(f32[512,256]{1,0:T(8,128)} %mine_ref.1), slice={[0:256], [0:256]} | slice | bytes 524288 | tf_op jit(solution)/shard_map/slice | solution.py:168
  1.7 7.6 %all-to-all-start = ((f32[16,16,256]{2,1,0:T(8,128)}), f32[16,16,256]{2,1,0:T(8,128)S(1)}, u32[]{:S(2)}, u32[]{:S(2)}) async-start(f32[16,16,256]{2,1,0:T(8,128)} %bitcast), calls=%async_computation | async-start | bytes 524288 | tf_op jit(solution)/shard_map/all_to_all | solution.py:168
  9.4 15.0 %collective-permute-start = (f32[512,256]{1,0:T(8,128)S(1)}, f32[512,256]{1,0:T(8,128)S(1)}, u32[]{:S(2)}, u32[]{:S(2)}) collective-permute-start(f32[512,256]{1,0:T(8,128)S(1)} %broadcast_select_fusion), channel_id=1, source_target_pairs={{0,14},{1,19},{32,46},{33,51},{64,78},{65,83},{96,110},{97,115},{1... | collective-permute-start | bytes 1572872 | tf_op jit(solution)/shard_map/ppermute | solution.py:186
  24.4 0.0 all-to-all-done
  24.5 1.9 %collective-permute-start.5 = (f32[2,16,256]{2,1,0:T(8,128)S(1)}, f32[2,16,256]{2,1,0:T(8,128)S(1)}, u32[]{:S(2)}, u32[]{:S(2)}) collective-permute-start(f32[2,16,256]{2,1,0:T(8,128)S(1)} %slice.51), channel_id=1, source_target_pairs={{0,1},{1,0},{2,3},{3,2},{4,5},{5,4},{6,7},{7,6},{8,9},{9,8},{10,11... | collective-permute-start | bytes 98312 | tf_op jit(solution)/shard_map/ppermute | solution.py:157
  26.4 1.2 %collective-permute-done.5 = f32[2,16,256]{2,1,0:T(8,128)S(1)} collective-permute-done((f32[2,16,256]{2,1,0:T(8,128)S(1)}, f32[2,16,256]{2,1,0:T(8,128)S(1)}, u32[]{:S(2)}, u32[]{:S(2)}) %collective-permute-start.5) | collective-permute-done | bytes 32800 | tf_op jit(solution)/shard_map/ppermute | solution.py:157
  27.6 9.6 %collective-permute-start.6 = (f32[3,16,256]{2,1,0:T(8,128)S(1)}, f32[3,16,256]{2,1,0:T(8,128)S(1)}, u32[]{:S(2)}, u32[]{:S(2)}) collective-permute-start(f32[3,16,256]{2,1,0:T(8,128)S(1)} %maximum_select_fusion), channel_id=1, source_target_pairs={{0,16},{1,17},{32,48},{33,49},{64,80},{65,81},{96,112},{97,113},{1... | collective-permute-start | bytes 147464 | tf_op jit(solution)/shard_map/ppermute | solution.py:180
  37.2 1.3 %collective-permute-start.7 = (f32[3,16,256]{2,1,0:T(8,128)S(1)}, f32[3,16,256]{2,1,0:T(8,128)S(1)}, u32[]{:S(2)}, u32[]{:S(2)}) collective-permute-start(f32[3,16,256]{2,1,0:T(8,128)S(1)} %maximum_select_fusion), channel_id=1, source_target_pairs={{0,8},{1,9},{32,40},{33,41},{64,72},{65,73},{96,104},{97,105},{128... | collective-permute-start | bytes 147464 | tf_op jit(solution)/shard_map/ppermute | solution.py:180
  38.5 1.3 %collective-permute-start.8 = (f32[3,16,256]{2,1,0:T(8,128)S(1)}, f32[3,16,256]{2,1,0:T(8,128)S(1)}, u32[]{:S(2)}, u32[]{:S(2)}) collective-permute-start(f32[3,16,256]{2,1,0:T(8,128)S(1)} %maximum_select_fusion), channel_id=1, source_target_pairs={{0,24},{1,25},{32,56},{33,57},{64,88},{65,89},{96,120},{97,121},{1... | collective-permute-start | bytes 147464 | tf_op jit(solution)/shard_map/ppermute | solution.py:180
  39.8 0.0 collective-permute-done
  39.8 0.1 fusion.1
  39.9 1.3 %collective-permute-start.1 = (f32[512,256]{1,0:T(8,128)S(1)}, f32[512,256]{1,0:T(8,128)S(1)}, u32[]{:S(2)}, u32[]{:S(2)}) collective-permute-start(f32[512,256]{1,0:T(8,128)S(1)} %fusion.1), channel_id=1, source_target_pairs={{0,8},{1,25},{14,22},{19,11},{32,40},{33,57},{46,54},{51,43},{64,7... | collective-permute-start | bytes 1572872 | tf_op jit(solution)/shard_map/ppermute | solution.py:186
  41.2 0.0 collective-permute-done.8
  41.3 1.3 %collective-permute-start.10 = (f32[3,16,256]{2,1,0:T(8,128)S(1)}, f32[3,16,256]{2,1,0:T(8,128)S(1)}, u32[]{:S(2)}, u32[]{:S(2)}) collective-permute-start(f32[3,16,256]{2,1,0:T(8,128)S(1)} %add_add_fusion.1), channel_id=1, source_target_pairs={{0,30},{1,31},{8,6},{9,7},{16,14},{17,15},{24,22},{25,23},{32,62},... | collective-permute-start | bytes 147464 | tf_op jit(solution)/shard_map/ppermute | solution.py:180
  42.6 1.3 %collective-permute-start.11 = (f32[3,16,256]{2,1,0:T(8,128)S(1)}, f32[3,16,256]{2,1,0:T(8,128)S(1)}, u32[]{:S(2)}, u32[]{:S(2)}) collective-permute-start(f32[3,16,256]{2,1,0:T(8,128)S(1)} %add_add_fusion.1), channel_id=1, source_target_pairs={{0,2},{1,3},{8,10},{9,11},{16,18},{17,19},{24,26},{25,27},{32,34},... | collective-permute-start | bytes 147464 | tf_op jit(solution)/shard_map/ppermute | solution.py:180
  43.9 1.3 %collective-permute-start.9 = (f32[3,16,256]{2,1,0:T(8,128)S(1)}, f32[3,16,256]{2,1,0:T(8,128)S(1)}, u32[]{:S(2)}, u32[]{:S(2)}) collective-permute-start(f32[3,16,256]{2,1,0:T(8,128)S(1)} %add_add_fusion.1), channel_id=1, source_target_pairs={{0,4},{1,5},{8,12},{9,13},{16,20},{17,21},{24,28},{25,29},{32,36},... | collective-permute-start | bytes 147464 | tf_op jit(solution)/shard_map/ppermute | solution.py:180
  45.2 3.2 %collective-permute-done.10 = f32[3,16,256]{2,1,0:T(8,128)S(1)} collective-permute-done((f32[3,16,256]{2,1,0:T(8,128)S(1)}, f32[3,16,256]{2,1,0:T(8,128)S(1)}, u32[]{:S(2)}, u32[]{:S(2)}) %collective-permute-start.10) | collective-permute-done | bytes 49184 | tf_op jit(solution)/shard_map/ppermute | solution.py:180
  48.4 0.1 add.35
  48.5 6.1 %collective-permute-start.2 = (f32[512,256]{1,0:T(8,128)S(1)}, f32[512,256]{1,0:T(8,128)S(1)}, u32[]{:S(2)}, u32[]{:S(2)}) collective-permute-start(f32[512,256]{1,0:T(8,128)S(1)} %add.35), channel_id=1, source_target_pairs={{0,4},{1,29},{8,12},{25,21},{14,18},{19,15},{22,26},{11,7},{32,36}... | collective-permute-start | bytes 1572872 | tf_op jit(solution)/shard_map/ppermute | solution.py:186
  54.6 1.2 %broadcast_in_dim.16 = f32[16,5,16,256]{3,2,1,0:T(8,128)} broadcast(f32[5,16,256]{2,1,0:T(8,128)S(1)} %pad_maximum_fusion), dimensions={1,2,3} | broadcast | bytes 1392640 | tf_op jit(solution)/shard_map/broadcast_in_dim | solution.py:182
  55.8 3.7 %all-to-all-start.1 = ((f32[16,5,16,256]{3,2,1,0:T(8,128)}), f32[16,5,16,256]{3,2,1,0:T(8,128)S(1)}, u32[]{:S(2)}, u32[]{:S(2)}) async-start(f32[16,5,16,256]{3,2,1,0:T(8,128)} %broadcast_in_dim.16), calls=%async_computation.1 | async-start | bytes 2621440 | tf_op jit(solution)/shard_map/all_to_all | solution.py:182
  59.5 1.1 %collective-permute-done.2 = f32[512,256]{1,0:T(8,128)S(1)} collective-permute-done((f32[512,256]{1,0:T(8,128)S(1)}, f32[512,256]{1,0:T(8,128)S(1)}, u32[]{:S(2)}, u32[]{:S(2)}) %collective-permute-start.2) | collective-permute-done | bytes 524320 | tf_op jit(solution)/shard_map/ppermute | solution.py:186
  60.6 0.1 add.36
  60.7 1.3 %collective-permute-start.3 = (f32[512,256]{1,0:T(8,128)S(1)}, f32[512,256]{1,0:T(8,128)S(1)}, u32[]{:S(2)}, u32[]{:S(2)}) collective-permute-start(f32[512,256]{1,0:T(8,128)S(1)} %add.36), channel_id=1, source_target_pairs={{0,30},{1,3},{4,2},{29,31},{8,6},{25,27},{12,10},{21,23},{14,16},{... | collective-permute-start | bytes 1572872 | tf_op jit(solution)/shard_map/ppermute | solution.py:186
  62.0 6.1 %collective-permute-done.3 = f32[512,256]{1,0:T(8,128)S(1)} collective-permute-done((f32[512,256]{1,0:T(8,128)S(1)}, f32[512,256]{1,0:T(8,128)S(1)}, u32[]{:S(2)}, u32[]{:S(2)}) %collective-permute-start.3) | collective-permute-done | bytes 524320 | tf_op jit(solution)/shard_map/ppermute | solution.py:186
  68.1 0.1 add.37.own_ref
  68.2 4.5 %collective-permute-start.4 = (f32[512,256]{1,0:T(8,128)S(1)}, f32[512,256]{1,0:T(8,128)S(1)}, u32[]{:S(2)}, u32[]{:S(2)}) collective-permute-start(f32[512,256]{1,0:T(8,128)S(1)} %add.37.own_ref), channel_id=1, source_target_pairs={{0,1},{1,0},{2,3},{3,2},{4,5},{5,4},{6,7},{7,6},{8,9},{9,8},{10,11... | collective-permute-start | bytes 1572872 | tf_op jit(solution)/shard_map/ppermute | solution.py:157
  72.7 5.1 %all-to-all-done.1 = f32[16,5,16,256]{3,2,1,0:T(8,128)S(1)} async-done(((f32[16,5,16,256]{3,2,1,0:T(8,128)}), f32[16,5,16,256]{3,2,1,0:T(8,128)S(1)}, u32[]{:S(2)}, u32[]{:S(2)}) %all-to-all-start.1) | async-done | bytes 1310752 | tf_op jit(solution)/shard_map/all_to_all | solution.py:182
  77.8 0.1 fusion
  77.9 10.0 %shard_map.17.inv0_ref = f32[256,256]{1,0:T(8,128)S(1)} custom-call(f32[256,256]{1,0:T(8,128)S(1)} %bitcast.9), custom_call_target="tpu_custom_call" | custom-call | tf_op jit(solution)/shard_map/pallas_call | solution.py:189
  87.9 11.2 %shard_map.18 = (f32[256,256]{1,0:T(8,128)S(1)}, f32[256,256]{1,0:T(8,128)S(1)}) custom-call(f32[256,256]{1,0:T(8,128)S(1)} %shard_map.17.inv0_ref, f32[256,256]{1,0:T(8,128)S(1)} %bitcast.8, f32[256,256]{1,0:T(8,128)S(1)} %bitcast.7), custom_call_target="tpu_custom_call" | custom-call | tf_op jit(solution)/shard_map/pallas_call | solution.py:190
  99.2 4.7 %shard_map.19 = f32[512,256]{1,0:T(8,128)} custom-call(f32[512,256]{1,0:T(8,128)S(1)} %copy-done, f32[512,256]{1,0:T(8,128)S(1)} %add.37.own_ref, f32[512,256]{1,0:T(8,128)S(1)} %collective-permute-done.4.other_ref, f32[2,256,256]{2,1,0:T(8,128)S(1)} %bitcast.6, f32[256,256]{1,0:T(8,128)S(1)} %shard_map.17.inv0_ref, ...), custom_call_target="tpu_custom_call" | custom-call | tf_op jit(solution)/shard_map/pallas_call | solution.py:191
  (17 shorter events, 0.2 us)
Async XLA Ops:
  0.0 9.3 %copy-start = (f32[512,256]{1,0:T(8,128)S(1)}, f32[512,256]{1,0:T(8,128)}, u32[]{:S(2)}) copy-start(f32[512,256]{1,0:T(8,128)} %mine_ref.1) | copy-start | bytes 1572868
  1.7 22.7 %all-to-all-start = ((f32[16,16,256]{2,1,0:T(8,128)}), f32[16,16,256]{2,1,0:T(8,128)S(1)}, u32[]{:S(2)}, u32[]{:S(2)}) async-start(f32[16,16,256]{2,1,0:T(8,128)} %bitcast), calls=%async_computation | async-start | bytes 524288 | tf_op jit(solution)/shard_map/all_to_all | solution.py:168
  9.4 30.4 %collective-permute-start = (f32[512,256]{1,0:T(8,128)S(1)}, f32[512,256]{1,0:T(8,128)S(1)}, u32[]{:S(2)}, u32[]{:S(2)}) collective-permute-start(f32[512,256]{1,0:T(8,128)S(1)} %broadcast_select_fusion), channel_id=1, source_target_pairs={{0,14},{1,19},{32,46},{33,51},{64,78},{65,83},{96,110},{97,115},{1... | collective-permute-start | bytes 1572872 | tf_op jit(solution)/shard_map/ppermute | solution.py:186
  24.5 3.1 %collective-permute-start.5 = (f32[2,16,256]{2,1,0:T(8,128)S(1)}, f32[2,16,256]{2,1,0:T(8,128)S(1)}, u32[]{:S(2)}, u32[]{:S(2)}) collective-permute-start(f32[2,16,256]{2,1,0:T(8,128)S(1)} %slice.51), channel_id=1, source_target_pairs={{0,1},{1,0},{2,3},{3,2},{4,5},{5,4},{6,7},{7,6},{8,9},{9,8},{10,11... | collective-permute-start | bytes 98312 | tf_op jit(solution)/shard_map/ppermute | solution.py:157
  27.6 13.6 %collective-permute-start.6 = (f32[3,16,256]{2,1,0:T(8,128)S(1)}, f32[3,16,256]{2,1,0:T(8,128)S(1)}, u32[]{:S(2)}, u32[]{:S(2)}) collective-permute-start(f32[3,16,256]{2,1,0:T(8,128)S(1)} %maximum_select_fusion), channel_id=1, source_target_pairs={{0,16},{1,17},{32,48},{33,49},{64,80},{65,81},{96,112},{97,113},{1... | collective-permute-start | bytes 147464 | tf_op jit(solution)/shard_map/ppermute | solution.py:180
  37.2 4.0 %collective-permute-start.7 = (f32[3,16,256]{2,1,0:T(8,128)S(1)}, f32[3,16,256]{2,1,0:T(8,128)S(1)}, u32[]{:S(2)}, u32[]{:S(2)}) collective-permute-start(f32[3,16,256]{2,1,0:T(8,128)S(1)} %maximum_select_fusion), channel_id=1, source_target_pairs={{0,8},{1,9},{32,40},{33,41},{64,72},{65,73},{96,104},{97,105},{128... | collective-permute-start | bytes 147464 | tf_op jit(solution)/shard_map/ppermute | solution.py:180
  38.5 2.7 %collective-permute-start.8 = (f32[3,16,256]{2,1,0:T(8,128)S(1)}, f32[3,16,256]{2,1,0:T(8,128)S(1)}, u32[]{:S(2)}, u32[]{:S(2)}) collective-permute-start(f32[3,16,256]{2,1,0:T(8,128)S(1)} %maximum_select_fusion), channel_id=1, source_target_pairs={{0,24},{1,25},{32,56},{33,57},{64,88},{65,89},{96,120},{97,121},{1... | collective-permute-start | bytes 147464 | tf_op jit(solution)/shard_map/ppermute | solution.py:180
  39.9 8.5 %collective-permute-start.1 = (f32[512,256]{1,0:T(8,128)S(1)}, f32[512,256]{1,0:T(8,128)S(1)}, u32[]{:S(2)}, u32[]{:S(2)}) collective-permute-start(f32[512,256]{1,0:T(8,128)S(1)} %fusion.1), channel_id=1, source_target_pairs={{0,8},{1,25},{14,22},{19,11},{32,40},{33,57},{46,54},{51,43},{64,7... | collective-permute-start | bytes 1572872 | tf_op jit(solution)/shard_map/ppermute | solution.py:186
  41.3 7.1 %collective-permute-start.10 = (f32[3,16,256]{2,1,0:T(8,128)S(1)}, f32[3,16,256]{2,1,0:T(8,128)S(1)}, u32[]{:S(2)}, u32[]{:S(2)}) collective-permute-start(f32[3,16,256]{2,1,0:T(8,128)S(1)} %add_add_fusion.1), channel_id=1, source_target_pairs={{0,30},{1,31},{8,6},{9,7},{16,14},{17,15},{24,22},{25,23},{32,62},... | collective-permute-start | bytes 147464 | tf_op jit(solution)/shard_map/ppermute | solution.py:180
  42.6 5.8 %collective-permute-start.11 = (f32[3,16,256]{2,1,0:T(8,128)S(1)}, f32[3,16,256]{2,1,0:T(8,128)S(1)}, u32[]{:S(2)}, u32[]{:S(2)}) collective-permute-start(f32[3,16,256]{2,1,0:T(8,128)S(1)} %add_add_fusion.1), channel_id=1, source_target_pairs={{0,2},{1,3},{8,10},{9,11},{16,18},{17,19},{24,26},{25,27},{32,34},... | collective-permute-start | bytes 147464 | tf_op jit(solution)/shard_map/ppermute | solution.py:180
  43.9 4.5 %collective-permute-start.9 = (f32[3,16,256]{2,1,0:T(8,128)S(1)}, f32[3,16,256]{2,1,0:T(8,128)S(1)}, u32[]{:S(2)}, u32[]{:S(2)}) collective-permute-start(f32[3,16,256]{2,1,0:T(8,128)S(1)} %add_add_fusion.1), channel_id=1, source_target_pairs={{0,4},{1,5},{8,12},{9,13},{16,20},{17,21},{24,28},{25,29},{32,36},... | collective-permute-start | bytes 147464 | tf_op jit(solution)/shard_map/ppermute | solution.py:180
  48.5 12.2 %collective-permute-start.2 = (f32[512,256]{1,0:T(8,128)S(1)}, f32[512,256]{1,0:T(8,128)S(1)}, u32[]{:S(2)}, u32[]{:S(2)}) collective-permute-start(f32[512,256]{1,0:T(8,128)S(1)} %add.35), channel_id=1, source_target_pairs={{0,4},{1,29},{8,12},{25,21},{14,18},{19,15},{22,26},{11,7},{32,36}... | collective-permute-start | bytes 1572872 | tf_op jit(solution)/shard_map/ppermute | solution.py:186
  55.8 22.0 %all-to-all-start.1 = ((f32[16,5,16,256]{3,2,1,0:T(8,128)}), f32[16,5,16,256]{3,2,1,0:T(8,128)S(1)}, u32[]{:S(2)}, u32[]{:S(2)}) async-start(f32[16,5,16,256]{3,2,1,0:T(8,128)} %broadcast_in_dim.16), calls=%async_computation.1 | async-start | bytes 2621440 | tf_op jit(solution)/shard_map/all_to_all | solution.py:182
  60.7 7.4 %collective-permute-start.3 = (f32[512,256]{1,0:T(8,128)S(1)}, f32[512,256]{1,0:T(8,128)S(1)}, u32[]{:S(2)}, u32[]{:S(2)}) collective-permute-start(f32[512,256]{1,0:T(8,128)S(1)} %add.36), channel_id=1, source_target_pairs={{0,30},{1,3},{4,2},{29,31},{8,6},{25,27},{12,10},{21,23},{14,16},{... | collective-permute-start | bytes 1572872 | tf_op jit(solution)/shard_map/ppermute | solution.py:186
  68.2 31.0 %collective-permute-start.4 = (f32[512,256]{1,0:T(8,128)S(1)}, f32[512,256]{1,0:T(8,128)S(1)}, u32[]{:S(2)}, u32[]{:S(2)}) collective-permute-start(f32[512,256]{1,0:T(8,128)S(1)} %add.37.own_ref), channel_id=1, source_target_pairs={{0,1},{1,0},{2,3},{3,2},{4,5},{5,4},{6,7},{7,6},{8,9},{9,8},{10,11... | collective-permute-start | bytes 1572872 | tf_op jit(solution)/shard_map/ppermute | solution.py:157

commit v2 on v1

v2 whole, which is shorter than its diff:
```python
import jax
import jax.numpy as jnp
from jax import lax
from jax.experimental import pallas as pl
from jax.experimental.pallas import tpu as pltpu
from jax.sharding import PartitionSpec as P

NB = 256
BASE = 32
LANES = 128
SUBS = 8
HIGHEST = lax.Precision.HIGHEST
VMEM_LIMIT = 10 * 1024 * 1024

CHIPS_Z = 16
PANEL_TREE = (
    ((0, 7),),
    ((0, 4), (7, 11)),
    ((0, 2), (4, 6), (7, 9), (11, 13)),
    ((0, 15), (2, 1), (4, 3), (6, 5), (7, 8), (9, 10), (11, 12), (13, 14)),
)
PIECE_TREE = (
    (((0, 12),), ((0, 4),), ((0, 8),)),
    (
        tuple((s, s + 1) for s in (0, 4, 8, 12)),
        tuple((s, (s + 15) % 16) for s in (0, 4, 8, 12)),
        tuple((s, s + 2) for s in (0, 4, 8, 12)),
    ),
)


def product(a, b, a_dim, b_dim):
    return lax.dot_general(
        a,
        b,
        (((a_dim,), (b_dim,)), ((), ())),
        precision=HIGHEST,
        preferred_element_type=jnp.float32,
    )


def small_inverse(rows, off):
    groups = BASE // SUBS
    lane = lax.broadcasted_iota(jnp.int32, (SUBS, LANES), 1)
    sub = lax.broadcasted_iota(jnp.int32, (SUBS, LANES), 0)
    cols = [[None] * groups for _ in range(BASE)]
    for c in range(BASE):
        for q in range(c // SUBS, groups):
            piece = rows[SUBS * q : SUBS * q + SUBS, off + c : off + c + 1]
            cols[c][q] = jnp.broadcast_to(piece, (SUBS, LANES))
    inv = [jnp.where(lane == sub + (off + SUBS * q), 1.0, 0.0) for q in range(groups)]
    scale = []
    for k in range(BASE):
        qk, rk = divmod(k, SUBS)
        root = lax.rsqrt(jnp.broadcast_to(cols[k][qk][rk : rk + 1], (SUBS, LANES)))
        recip = root * root
        for c in range(k + 1, BASE):
            qc, rc = divmod(c, SUBS)
            factor = jnp.broadcast_to(cols[k][qc][rc : rc + 1], (SUBS, LANES)) * recip
            for q in range(qc, groups):
                cols[c][q] = cols[c][q] - cols[k][q] * factor
        row = jnp.broadcast_to(inv[qk][rk : rk + 1], (SUBS, LANES)) * recip
        for q in range(qk, groups):
            update = cols[k][q] * row
            if q == qk:
                update = jnp.where(sub > rk, update, 0.0)
            inv[q] = inv[q] - update
        scale.append(root)
    out = []
    for q in range(groups):
        factor = scale[SUBS * q]
        for r in range(1, SUBS):
            factor = jnp.where(sub == r, scale[SUBS * q + r], factor)
        out.append(inv[q] * factor)
    return jnp.concatenate(out, axis=0)


def inverse_factor(square, out_ref, work):
    rows = lax.broadcasted_iota(jnp.int32, (NB, NB), 0)
    cols = lax.broadcasted_iota(jnp.int32, (NB, NB), 1)
    work[:, :NB] = square
    work[:, NB:] = jnp.where(rows == cols, 1.0, 0.0)
    for low in range(0, NB, BASE):
        tile = low // LANES * LANES
        off = low - tile
        high = low + BASE
        small = small_inverse(work[low:high, tile : tile + LANES], off)
        strip = product(small[:, off : off + BASE], work[low:high, :], 1, 0)
        out_ref[low:high, :] = strip[:, NB:]
        if high < NB:
            work[high:, :] = work[high:, :] - product(strip[:, high:NB], strip, 0, 0)


def first_kernel(lead_ref, inv_ref, work):
    inverse_factor(lead_ref[:, 0].reshape(NB, NB), inv_ref, work)


def second_kernel(inv0_ref, lead_ref, turned_ref, inv_ref, work):
    turned = product(inv0_ref[...], lead_ref[:, 1].reshape(NB, NB), 1, 0)
    turned_ref[...] = turned
    square = lead_ref[:, 2].reshape(NB, NB) - product(turned, turned, 0, 0)
    inverse_factor(square, inv_ref, work)


def lead_kernel(first_ref, swapped_ref, lead_ref):
    col = lax.axis_index("col")
    bottom = col < 2
    core0 = lax.rem(col, 2) == 0
    first = jnp.where(bottom, first_ref[...], 0.0)
    swapped = jnp.where(bottom, swapped_ref[...], 0.0)
    lead_ref[0] = jnp.where(core0, first[0], swapped[0])
    lead_ref[1] = jnp.where(core0, swapped[0], first[0])
    lead_ref[2] = jnp.where(core0, swapped[1], first[1])


def mask_kernel(value_ref, out_ref):
    out_ref[...] = jnp.where(lax.axis_index("col") < 2, value_ref[...], 0.0)


def sum_kernel(*refs):
    total = refs[0][...]
    for ref in refs[1:-1]:
        total = total + ref[...]
    refs[-1][...] = total


def spread_kernel(early_ref, late_ref, base_ref, a_ref, b_ref, c_ref, out_ref):
    total = base_ref[...] + a_ref[...] + b_ref[...] + c_ref[...]
    pieces = early_ref[...] + late_ref[...]
    for target in range(out_ref.shape[0]):
        out_ref[target, :3] = total
        out_ref[target, 3:] = pieces


def factors_kernel(cols_ref, inv0_ref, turned_ref, inv1_ref, x0_ref, x1_ref):
    col = lax.axis_index("col")
    inv0 = inv0_ref[...]
    turned = turned_ref[...]
    inv1 = inv1_ref[...]

    @pl.when(col >= 2)
    def _():
        right0 = product(inv0, cols_ref[:, 3].reshape(NB, NB), 1, 0)
        below = cols_ref[:, 4].reshape(NB, NB) - product(turned, right0, 0, 0)
        right1 = product(inv1, below, 1, 0)
        x1 = product(inv1, right1, 0, 0)
        x1_ref[...] = x1
        x0_ref[...] = product(inv0, right0 - product(turned, x1, 1, 0), 0, 0)

    @pl.when(col == 0)
    def _():
        x0_ref[...] = -inv0.T
        x1_ref[...] = jnp.zeros_like(inv0)

    @pl.when(col == 1)
    def _():
        x0_ref[...] = product(inv0, product(turned, inv1, 1, 1), 0, 0)
        x1_ref[...] = -inv1.T


def final_kernel(mine_ref, own_ref, other0_ref, other_ref, x0_ref, x1_ref, out_ref):
    row = lax.axis_index("row")
    col = lax.axis_index("col")
    core0 = lax.rem(col, 2) == 0
    rows_in = lax.broadcasted_iota(jnp.int32, (NB, NB), 0)
    cols_in = lax.broadcasted_iota(jnp.int32, (NB, NB), 1)
    x_own = jnp.where(core0, x0_ref[...], x1_ref[...])
    x_other = jnp.where(core0, x1_ref[...], x0_ref[...])
    for block in range(2):
        place = pl.ds(block * NB, NB)
        label = row + 16 * block
        other = other0_ref[place, :] + other_ref[place, :]
        taken = product(own_ref[place, :], x_own, 1, 0) + product(other, x_other, 1, 0)
        value = jnp.where(col >= 2, mine_ref[place, :], 0.0) - taken
        last = jnp.minimum(col, 2)
        keep = (label > last) | ((label == last) & ((col >= 2) | (rows_in >= cols_in)))
        out_ref[place, :] = jnp.where(keep, value, 0.0)


def call(body, out, *operands, order=(), work=False, flops=0):
    kept = len(operands)
    blocks = [pltpu.VMEM] * kept + [pl.ANY] * len(order)

    def whole(*refs):
        body(*refs[:kept], *refs[kept + len(order) :])

    outs = jax.tree.map(lambda shape: jax.ShapeDtypeStruct(shape, jnp.float32), out, is_leaf=lambda v: type(v[0]) is int)
    return pl.pallas_call(
        whole,
        out_shape=outs,
        in_specs=[pl.BlockSpec(memory_space=space) for space in blocks],
        scratch_shapes=[pltpu.VMEM((NB, 2 * NB), jnp.float32)] if work else [],
        compiler_params=pltpu.CompilerParams(vmem_limit_bytes=VMEM_LIMIT),
        cost_estimate=pl.CostEstimate(flops=flops, bytes_accessed=0, transcendentals=0) if flops else None,
        name=body.__name__,
    )(*operands, *order)


def both_cores(pairs, mirror):
    out = []
    for s, t in pairs:
        out.append((2 * s, 2 * t))
        if mirror:
            s, t = (CHIPS_Z - s) % CHIPS_Z, (CHIPS_Z - t) % CHIPS_Z
        out.append((2 * s + 1, 2 * t + 1))
    return out


def swap_cores(value, chips):
    return lax.ppermute(value, "col", [(2 * z + c, 2 * z + 1 - c) for z in chips for c in (0, 1)])


def scatter_rows(top):
    return lax.all_to_all(top.reshape(16, 16, NB), "row", 0, 0)[:2]


def no_rows(top):
    return jnp.zeros((2, 16, NB), top.dtype)


def along_z(value, pairs, mirror=False):
    return lax.ppermute(value, "col", both_cores(pairs, mirror))


def local(kernel):
    square = (NB, NB)
    top = kernel[:NB]
    ten_us = 10_000_000_000

    height = lax.axis_index("col") // 2
    bottom = height == 0
    first = lax.cond(bottom, scatter_rows, no_rows, top)
    swapped = swap_cores(first, [0])
    lead = call(lead_kernel, (3, 16, NB), first, swapped)
    other0 = swap_cores(call(mask_kernel, kernel.shape, kernel, order=(lead,)), [0])
    sent = [along_z(lead, p) for p in PIECE_TREE[0]]
    waits = (height == 7) | (height == 9)
    early = lax.cond(bottom | waits, lambda t, l: l[:2], lambda t, l: scatter_rows(t), top, lead)
    lead = call(sum_kernel, (3, 16, NB), lead, *sent, order=(early,))

    panel = call(mask_kernel, kernel.shape, kernel, order=(lead,))
    panel = call(sum_kernel, kernel.shape, panel, along_z(panel, PANEL_TREE[0], True))
    late = lax.cond(waits, lambda t, l: scatter_rows(t), lambda t, l: no_rows(t), top, lead)
    sent = [along_z(lead, p) for p in PIECE_TREE[1]]
    spread = call(spread_kernel, (16, 5, 16, NB), early, late, lead, *sent, order=(panel,))
    lead = lax.all_to_all(spread, "row", 0, 0)

    panel = call(sum_kernel, kernel.shape, panel, along_z(panel, PANEL_TREE[1], True), order=(spread,))
    inv0 = call(first_kernel, square, lead, order=(panel,), work=True, flops=ten_us)
    panel = call(sum_kernel, kernel.shape, panel, along_z(panel, PANEL_TREE[2], True), order=(inv0,))
    turned, inv1 = call(
        second_kernel, (square, square), inv0, lead, order=(panel,), work=True, flops=ten_us
    )
    panel = call(sum_kernel, kernel.shape, panel, along_z(panel, PANEL_TREE[3], True), order=(inv1,))
    other = swap_cores(panel, range(1, CHIPS_Z))
    x0, x1 = call(factors_kernel, (square, square), lead, inv0, turned, inv1, order=(panel,))
    return call(final_kernel, kernel.shape, kernel, panel, other0, other, x0, x1)


def solution(mesh):
    return jax.shard_map(
        local, mesh=mesh, in_specs=(P("row", "col"),), out_specs=P("row", "col"), check_vma=False
    )
```

time: 105 us -> 93.3 us (0.89)
  the two profiles are of different devices: /device:TPU:1 before, /device:TPU:193 now
where the time goes in v2:
time: 93.3 us; the launch traced here: 92.8 us
  waiting for transfers between devices  30.9 us (33%)
  Pallas kernels  28.9 us (31%)
  starting transfers between devices  17.5 us (19%)
  blocking collectives  14.1 us (15%)
  local copies, waits for them, and re-layouts  1.05 us (1%)
    pallas_call x13, Pallas kernels, call(): pl.pallas_call(whole, out_shape=outs, in_specs=[pl.BlockSpec(memory_space...  28.9 us
    all_to_all x1, waiting for transfers between devices, local(): lead = lax.all_to_all(spread, 'row', 0, 0)  17.7 us
    all_to_all x1, blocking collectives, scatter_rows(): return lax.all_to_all(top.reshape(16, 16, NB), 'row', 0, 0)[:2]  14.1 us
    ppermute x10, waiting for transfers between devices, along_z(): return lax.ppermute(value, 'col', both_cores(pairs, mirror))  13.1 us
    ppermute x10, starting transfers between devices, along_z(): return lax.ppermute(value, 'col', both_cores(pairs, mirror))  8.17 us
    ppermute x3, starting transfers between devices, swap_cores(): lax.ppermute(value, 'col', [(2 * z + c, 2 * z + 1 - c) for z in chips for...  5.68 us
    all_to_all x1, starting transfers between devices, local(): lead = lax.all_to_all(spread, 'row', 0, 0)  3.7 us
  transfers between devices with their start and end apart: 14, of which 2 were waited for; matrix products, arithmetic and copies ran while one was open for 0% of the time, Pallas kernels for 27%

profile of v2, /device:TPU:193, one launch (start us, length us, event | category | flops | bytes accessed | tf_op | source)
XLA Modules:
  0.0 92.8 jit_solution(14561617866459658948)
XLA Ops:
  0.0 1.0 %slice.24 = f32[256,256]{1,0:T(8,128)S(1)} slice(f32[512,256]{1,0:T(8,128)} %refs_0_.5), slice={[0:256], [0:256]} | slice | bytes 524288 | tf_op jit(solution)/shard_map/slice | solution.py:227
  1.1 0.7 collective-permute-start
  1.8 0.0 collective-permute-done.refs_1_
  1.8 0.7 collective-permute-start.1
  2.5 0.7 collective-permute-start.2
  3.1 0.7 collective-permute-start.3
  3.8 14.1 %conditional.4 = (f32[2,16,256]{2,1,0:T(8,128)S(1)}) conditional(s32[]{:T(128)} %convert_element_type.10, f32[256,256]{1,0:T(8,128)S(1)} %slice.24, f32[3,16,256]{2,1,0:T(8,128)S(1)} %lead_kernel.1.refs_0_.refs_1_), branch_computations={%region_2.3_spmd, %region_3.4_spmd} | conditional | bytes 589832 | solution.py:238
  3.8 14.1 %all_to_all.18 = f32[16,16,256]{2,1,0:T(8,128)S(1)} all-to-all(f32[16,16,256]{2,1,0:T(8,128)S(1)} %bitcast.4), channel_id=1, replica_groups=mesh['row'=16,'col'=32] {'row'}, dimensions={0} | all-to-all | bytes 524288 | tf_op jit(solution)/shard_map/cond/branch_0_fun/all_to_all | solution.py:214
  17.9 0.0 collective-permute-done.2.refs_2_
  18.0 0.1 mask_kernel.2.refs_0_
  18.1 0.7 collective-permute-start.4
  18.8 0.7 collective-permute-start.6
  19.4 0.7 collective-permute-start.7
  20.1 1.3 %collective-permute-start.8 = (f32[3,16,256]{2,1,0:T(8,128)S(1)}, f32[3,16,256]{2,1,0:T(8,128)S(1)}, u32[]{:S(2)}, u32[]{:S(2)}) collective-permute-start(f32[3,16,256]{2,1,0:T(8,128)S(1)} %sum_kernel.5.refs_1_.refs_2_), channel_id=1, source_target_pairs={{0,4},{1,5},{8,12},{9,13},{16,20},{17,21},{24,28},{25,29},{32,36},... | collective-permute-start | bytes 147464 | tf_op jit(solution)/shard_map/ppermute | solution.py:222
  21.5 0.1 sum_kernel.6.refs_6_.refs_0_
  21.5 13.1 %collective-permute-done.8.refs_5_ = f32[3,16,256]{2,1,0:T(8,128)S(1)} collective-permute-done((f32[3,16,256]{2,1,0:T(8,128)S(1)}, f32[3,16,256]{2,1,0:T(8,128)S(1)}, u32[]{:S(2)}, u32[]{:S(2)}) %collective-permute-start.8) | collective-permute-done | bytes 49184 | tf_op jit(solution)/shard_map/ppermute | solution.py:222
  34.7 1.2 %spread_kernel.1.refs_2_ = f32[16,5,16,256]{3,2,1,0:T(8,128)} custom-call(f32[2,16,256]{2,1,0:T(8,128)S(1)} %get-tuple-element.27.refs_4_.refs_0_, f32[2,16,256]{2,1,0:T(8,128)S(1)} %get-tuple-element.28.refs_1_, f32[3,16,256]{2,1,0:T(8,128)S(1)} %sum_kernel.5.refs_1_.refs_2_, f32[3,16,256]{2,1,0:T(8,128)S(1)} %collective-permute-done.6.refs_3_, ...), custom_call_target="tpu_custom_call" | custom-call | tf_op jit(solution)/shard_map/spread_kernel/pallas_call | solution.py:188
  35.9 3.7 %all-to-all-start.3 = ((f32[16,5,16,256]{3,2,1,0:T(8,128)}), f32[16,5,16,256]{3,2,1,0:T(8,128)S(1)}, u32[]{:S(2)}, u32[]{:S(2)}) async-start(f32[16,5,16,256]{3,2,1,0:T(8,128)} %spread_kernel.1.refs_2_), calls=%async_computation.3 | async-start | bytes 2621440 | tf_op jit(solution)/shard_map/all_to_all | solution.py:246
  39.6 0.7 collective-permute-start.5
  40.3 0.1 mask_kernel.3
  40.4 1.5 %collective-permute-start.11 = (f32[512,256]{1,0:T(8,128)S(1)}, f32[512,256]{1,0:T(8,128)}, u32[]{:S(2)}, u32[]{:S(2)}) collective-permute-start(f32[512,256]{1,0:T(8,128)S(1)} %mask_kernel.3), channel_id=1, source_target_pairs={{0,1},{1,0},{32,33},{33,32},{64,65},{65,64},{96,97},{97,96},{128,1... | collective-permute-start | bytes 1572872 | tf_op jit(solution)/shard_map/ppermute | solution.py:210
  41.8 0.1 sum_kernel.7.refs_1_.refs_0_
  41.9 0.7 collective-permute-start.9
  42.6 17.7 %all-to-all-done.3.refs_0_.refs_1_ = f32[16,5,16,256]{3,2,1,0:T(8,128)S(1)} async-done(((f32[16,5,16,256]{3,2,1,0:T(8,128)}), f32[16,5,16,256]{3,2,1,0:T(8,128)S(1)}, u32[]{:S(2)}, u32[]{:S(2)}) %all-to-all-start.3) | async-done | bytes 1310752 | tf_op jit(solution)/shard_map/all_to_all | solution.py:246
  60.3 10.0 %first_kernel.1.refs_2_.refs_0_.refs_1_ = f32[256,256]{1,0:T(8,128)S(1)} custom-call(f32[16,5,16,256]{3,2,1,0:T(8,128)S(1)} %all-to-all-done.3.refs_0_.refs_1_, f32[512,256]{1,0:T(8,128)S(1)} %sum_kernel.7.refs_1_.refs_0_), custom_call_target="tpu_custom_call" | custom-call | flops 10000000000 | tf_op jit(solution)/shard_map/first_kernel/pallas_call | solution.py:188
  70.3 0.1 sum_kernel.8.refs_2_.refs_0_
  70.4 1.5 %collective-permute-start.10 = (f32[512,256]{1,0:T(8,128)S(1)}, f32[512,256]{1,0:T(8,128)S(1)}, u32[]{:S(2)}, u32[]{:S(2)}) collective-permute-start(f32[512,256]{1,0:T(8,128)S(1)} %sum_kernel.8.refs_2_.refs_0_), channel_id=1, source_target_pairs={{0,30},{1,3},{4,2},{29,31},{8,6},{25,27},{12,10},{21,23},{14,16},{... | collective-permute-start | bytes 1572872 | tf_op jit(solution)/shard_map/ppermute | solution.py:222
  71.9 11.1 %second_kernel.1 = (f32[256,256]{1,0:T(8,128)S(1)}, f32[256,256]{1,0:T(8,128)S(1)}) custom-call(f32[256,256]{1,0:T(8,128)S(1)} %first_kernel.1.refs_2_.refs_0_.refs_1_, f32[16,5,16,256]{3,2,1,0:T(8,128)S(1)} %all-to-all-done.3.refs_0_.refs_1_, f32[512,256]{1,0:T(8,128)S(1)} %sum_kernel.8.refs_2_.refs_0_), custom_call_target="tpu_custom_call" | custom-call | flops 10000000000 | tf_op jit(solution)/shard_map/second_kernel/pallas_call | solution.py:188
  83.0 0.1 sum_kernel.9.refs_4_.refs_1_
  83.0 3.6 %collective-permute-start.12 = (f32[512,256]{1,0:T(8,128)S(1)}, f32[512,256]{1,0:T(8,128)S(1)}, u32[]{:S(2)}, u32[]{:S(2)}) collective-permute-start(f32[512,256]{1,0:T(8,128)S(1)} %sum_kernel.9.refs_4_.refs_1_), channel_id=1, source_target_pairs={{2,3},{3,2},{4,5},{5,4},{6,7},{7,6},{8,9},{9,8},{10,11},{11,10},{1... | collective-permute-start | bytes 1572872 | tf_op jit(solution)/shard_map/ppermute | solution.py:210
  86.6 3.2 %factors_kernel.1 = (f32[256,256]{1,0:T(8,128)S(1)}, f32[256,256]{1,0:T(8,128)S(1)}) custom-call(f32[16,5,16,256]{3,2,1,0:T(8,128)S(1)} %all-to-all-done.3.refs_0_.refs_1_, f32[256,256]{1,0:T(8,128)S(1)} %first_kernel.1.refs_2_.refs_0_.refs_1_, f32[256,256]{1,0:T(8,128)S(1)} %get-tuple-element.23.refs_2_, f32[256,256]{1,0:T(8,128)S(1)} %get-tuple-element.22.refs_2_.refs_3_, ...), custom_call_target="tpu_custom_call" | custom-call | tf_op jit(solution)/shard_map/factors_kernel/pallas_call | solution.py:188
  89.9 3.0 %final_kernel.1 = f32[512,256]{1,0:T(8,128)} custom-call(f32[512,256]{1,0:T(8,128)S(1)} %copy-done, f32[512,256]{1,0:T(8,128)S(1)} %sum_kernel.9.refs_4_.refs_1_, f32[512,256]{1,0:T(8,128)} %collective-permute-done.11.refs_2_, f32[512,256]{1,0:T(8,128)S(1)} %collective-permute-done.12.refs_3_, f32[256,256]{1,0:T(8,128)S(1)} %get-tuple-element.24.refs_4_, ...), custom_call_target="tpu_custom_call" | custom-call | tf_op jit(solution)/shard_map/final_kernel/pallas_call | solution.py:188
  (19 shorter events, 0.1 us)
Async XLA Ops:
  0.0 18.0 %copy-start = (f32[512,256]{1,0:T(8,128)S(1)}, f32[512,256]{1,0:T(8,128)}, u32[]{:S(2)}) copy-start(f32[512,256]{1,0:T(8,128)} %refs_0_.5) | copy-start | bytes 1572868
  1.1 0.7 collective-permute-start
  1.8 16.1 %collective-permute-start.1 = (f32[3,16,256]{2,1,0:T(8,128)S(1)}, f32[3,16,256]{2,1,0:T(8,128)S(1)}, u32[]{:S(2)}, u32[]{:S(2)}) collective-permute-start(f32[3,16,256]{2,1,0:T(8,128)S(1)} %lead_kernel.1.refs_0_.refs_1_), channel_id=1, source_target_pairs={{0,24},{1,25},{32,56},{33,57},{64,88},{65,89},{96,120},{97,121},{1... | collective-permute-start | bytes 147464 | tf_op jit(solution)/shard_map/ppermute | solution.py:222
  2.5 15.5 %collective-permute-start.2 = (f32[3,16,256]{2,1,0:T(8,128)S(1)}, f32[3,16,256]{2,1,0:T(8,128)S(1)}, u32[]{:S(2)}, u32[]{:S(2)}) collective-permute-start(f32[3,16,256]{2,1,0:T(8,128)S(1)} %lead_kernel.1.refs_0_.refs_1_), channel_id=1, source_target_pairs={{0,8},{1,9},{32,40},{33,41},{64,72},{65,73},{96,104},{97,105},{128... | collective-permute-start | bytes 147464 | tf_op jit(solution)/shard_map/ppermute | solution.py:222
  3.1 14.8 %collective-permute-start.3 = (f32[3,16,256]{2,1,0:T(8,128)S(1)}, f32[3,16,256]{2,1,0:T(8,128)S(1)}, u32[]{:S(2)}, u32[]{:S(2)}) collective-permute-start(f32[3,16,256]{2,1,0:T(8,128)S(1)} %lead_kernel.1.refs_0_.refs_1_), channel_id=1, source_target_pairs={{0,16},{1,17},{32,48},{33,49},{64,80},{65,81},{96,112},{97,113},{1... | collective-permute-start | bytes 147464 | tf_op jit(solution)/shard_map/ppermute | solution.py:222
  18.1 3.4 %collective-permute-start.4 = (f32[512,256]{1,0:T(8,128)S(1)}, f32[512,256]{1,0:T(8,128)S(1)}, u32[]{:S(2)}, u32[]{:S(2)}) collective-permute-start(f32[512,256]{1,0:T(8,128)S(1)} %mask_kernel.2.refs_0_), channel_id=1, source_target_pairs={{0,14},{1,19},{32,46},{33,51},{64,78},{65,83},{96,110},{97,115},{1... | collective-permute-start | bytes 1572872 | tf_op jit(solution)/shard_map/ppermute | solution.py:222
  18.8 2.8 %collective-permute-start.6 = (f32[3,16,256]{2,1,0:T(8,128)S(1)}, f32[3,16,256]{2,1,0:T(8,128)S(1)}, u32[]{:S(2)}, u32[]{:S(2)}) collective-permute-start(f32[3,16,256]{2,1,0:T(8,128)S(1)} %sum_kernel.5.refs_1_.refs_2_), channel_id=1, source_target_pairs={{0,2},{1,3},{8,10},{9,11},{16,18},{17,19},{24,26},{25,27},{32,34},... | collective-permute-start | bytes 147464 | tf_op jit(solution)/shard_map/ppermute | solution.py:222
  19.4 2.1 %collective-permute-start.7 = (f32[3,16,256]{2,1,0:T(8,128)S(1)}, f32[3,16,256]{2,1,0:T(8,128)S(1)}, u32[]{:S(2)}, u32[]{:S(2)}) collective-permute-start(f32[3,16,256]{2,1,0:T(8,128)S(1)} %sum_kernel.5.refs_1_.refs_2_), channel_id=1, source_target_pairs={{0,30},{1,31},{8,6},{9,7},{16,14},{17,15},{24,22},{25,23},{32,62},... | collective-permute-start | bytes 147464 | tf_op jit(solution)/shard_map/ppermute | solution.py:222
  20.1 14.6 %collective-permute-start.8 = (f32[3,16,256]{2,1,0:T(8,128)S(1)}, f32[3,16,256]{2,1,0:T(8,128)S(1)}, u32[]{:S(2)}, u32[]{:S(2)}) collective-permute-start(f32[3,16,256]{2,1,0:T(8,128)S(1)} %sum_kernel.5.refs_1_.refs_2_), channel_id=1, source_target_pairs={{0,4},{1,5},{8,12},{9,13},{16,20},{17,21},{24,28},{25,29},{32,36},... | collective-permute-start | bytes 147464 | tf_op jit(solution)/shard_map/ppermute | solution.py:222
  35.9 24.4 %all-to-all-start.3 = ((f32[16,5,16,256]{3,2,1,0:T(8,128)}), f32[16,5,16,256]{3,2,1,0:T(8,128)S(1)}, u32[]{:S(2)}, u32[]{:S(2)}) async-start(f32[16,5,16,256]{3,2,1,0:T(8,128)} %spread_kernel.1.refs_2_), calls=%async_computation.3 | async-start | bytes 2621440 | tf_op jit(solution)/shard_map/all_to_all | solution.py:246
  39.6 2.2 %collective-permute-start.5 = (f32[512,256]{1,0:T(8,128)S(1)}, f32[512,256]{1,0:T(8,128)S(1)}, u32[]{:S(2)}, u32[]{:S(2)}) collective-permute-start(f32[512,256]{1,0:T(8,128)S(1)} %sum_kernel.6.refs_6_.refs_0_), channel_id=1, source_target_pairs={{0,8},{1,25},{14,22},{19,11},{32,40},{33,57},{46,54},{51,43},{64,7... | collective-permute-start | bytes 1572872 | tf_op jit(solution)/shard_map/ppermute | solution.py:222
  40.4 49.5 %collective-permute-start.11 = (f32[512,256]{1,0:T(8,128)S(1)}, f32[512,256]{1,0:T(8,128)}, u32[]{:S(2)}, u32[]{:S(2)}) collective-permute-start(f32[512,256]{1,0:T(8,128)S(1)} %mask_kernel.3), channel_id=1, source_target_pairs={{0,1},{1,0},{32,33},{33,32},{64,65},{65,64},{96,97},{97,96},{128,1... | collective-permute-start | bytes 1572872 | tf_op jit(solution)/shard_map/ppermute | solution.py:210
  41.9 28.4 %collective-permute-start.9 = (f32[512,256]{1,0:T(8,128)S(1)}, f32[512,256]{1,0:T(8,128)S(1)}, u32[]{:S(2)}, u32[]{:S(2)}) collective-permute-start(f32[512,256]{1,0:T(8,128)S(1)} %sum_kernel.7.refs_1_.refs_0_), channel_id=1, source_target_pairs={{0,4},{1,29},{8,12},{25,21},{14,18},{19,15},{22,26},{11,7},{32,36}... | collective-permute-start | bytes 1572872 | tf_op jit(solution)/shard_map/ppermute | solution.py:222
  70.4 12.5 %collective-permute-start.10 = (f32[512,256]{1,0:T(8,128)S(1)}, f32[512,256]{1,0:T(8,128)S(1)}, u32[]{:S(2)}, u32[]{:S(2)}) collective-permute-start(f32[512,256]{1,0:T(8,128)S(1)} %sum_kernel.8.refs_2_.refs_0_), channel_id=1, source_target_pairs={{0,30},{1,3},{4,2},{29,31},{8,6},{25,27},{12,10},{21,23},{14,16},{... | collective-permute-start | bytes 1572872 | tf_op jit(solution)/shard_map/ppermute | solution.py:222
  83.0 6.8 %collective-permute-start.12 = (f32[512,256]{1,0:T(8,128)S(1)}, f32[512,256]{1,0:T(8,128)S(1)}, u32[]{:S(2)}, u32[]{:S(2)}) collective-permute-start(f32[512,256]{1,0:T(8,128)S(1)} %sum_kernel.9.refs_4_.refs_1_), channel_id=1, source_target_pairs={{2,3},{3,2},{4,5},{5,4},{6,7},{7,6},{8,9},{9,8},{10,11},{11,10},{1... | collective-permute-start | bytes 1572872 | tf_op jit(solution)/shard_map/ppermute | solution.py:210

commit v3 on v2

--- a/solution.py
+++ b/solution.py
@@ -39,6 +39,22 @@
     )
 
 
+def split(a):
+    high = a.astype(jnp.bfloat16)
+    return high, (a - high.astype(jnp.float32)).astype(jnp.bfloat16)
+
+
+def product3(a, b, a_dim, b_dim):
+    dims = (((a_dim,), (b_dim,)), ((), ()))
+    a_high, a_low = split(a)
+    b_high, b_low = split(b)
+
+    def dot(x, y):
+        return lax.dot_general(x, y, dims, preferred_element_type=jnp.float32)
+
+    return dot(a_high, b_high) + (dot(a_high, b_low) + dot(a_low, b_high))
+
+
 def small_inverse(rows, off):
     groups = BASE // SUBS
     lane = lax.broadcasted_iota(jnp.int32, (SUBS, LANES), 1)
@@ -54,11 +70,12 @@
         qk, rk = divmod(k, SUBS)
         root = lax.rsqrt(jnp.broadcast_to(cols[k][qk][rk : rk + 1], (SUBS, LANES)))
         recip = root * root
+        scaled = [None if part is None else part * recip for part in cols[k]]
         for c in range(k + 1, BASE):
             qc, rc = divmod(c, SUBS)
-            factor = jnp.broadcast_to(cols[k][qc][rc : rc + 1], (SUBS, LANES)) * recip
+            factor = jnp.broadcast_to(cols[k][qc][rc : rc + 1], (SUBS, LANES))
             for q in range(qc, groups):
-                cols[c][q] = cols[c][q] - cols[k][q] * factor
+                cols[c][q] = cols[c][q] - scaled[q] * factor
         row = jnp.broadcast_to(inv[qk][rk : rk + 1], (SUBS, LANES)) * recip
         for q in range(qk, groups):
             update = cols[k][q] * row
@@ -76,19 +93,30 @@
 
 
 def inverse_factor(square, out_ref, work):
-    rows = lax.broadcasted_iota(jnp.int32, (NB, NB), 0)
-    cols = lax.broadcasted_iota(jnp.int32, (NB, NB), 1)
-    work[:, :NB] = square
-    work[:, NB:] = jnp.where(rows == cols, 1.0, 0.0)
+    work[...] = square
     for low in range(0, NB, BASE):
         tile = low // LANES * LANES
         off = low - tile
         high = low + BASE
         small = small_inverse(work[low:high, tile : tile + LANES], off)
-        strip = product(small[:, off : off + BASE], work[low:high, :], 1, 0)
-        out_ref[low:high, :] = strip[:, NB:]
-        if high < NB:
-            work[high:, :] = work[high:, :] - product(strip[:, high:NB], strip, 0, 0)
+        block = small[:, off : off + BASE]
+        strip = product(block, work[low:high, :], 1, 0)
+        lane = lax.broadcasted_iota(jnp.int32, (BASE, LANES), 1)
+        own = jnp.where((lane >= off) & (lane < off + BASE), small, strip[:, tile : tile + LANES])
+        strip = jnp.concatenate(
+            [own if t == tile else strip[:, t : t + LANES] for t in range(0, NB, LANES)], axis=1
+        )
+        out_ref[low:high, :] = strip
+        for first, last in ((high, high + BASE), (high + BASE, NB)):
+            if first < last <= NB:
+                left = product(work[first:last, low:high], block, 1, 1)
+                old = work[first:last, :]
+                lanes = lax.broadcasted_iota(jnp.int32, old.shape, 1)
+                old = jnp.where((lanes >= low) & (lanes < high), 0.0, old)
+                work[first:last, :] = old - product(left, strip, 1, 0)
+    rows = lax.broadcasted_iota(jnp.int32, (NB, NB), 0)
+    cols = lax.broadcasted_iota(jnp.int32, (NB, NB), 1)
+    out_ref[...] = jnp.where(rows >= cols, out_ref[...], 0.0)
 
 
 def first_kernel(lead_ref, inv_ref, work):
@@ -140,12 +168,11 @@
 
     @pl.when(col >= 2)
     def _():
-        right0 = product(inv0, cols_ref[:, 3].reshape(NB, NB), 1, 0)
-        below = cols_ref[:, 4].reshape(NB, NB) - product(turned, right0, 0, 0)
-        right1 = product(inv1, below, 1, 0)
-        x1 = product(inv1, right1, 0, 0)
+        right0 = product3(inv0, cols_ref[:, 3].reshape(NB, NB), 1, 0)
+        below = cols_ref[:, 4].reshape(NB, NB) - product3(turned, right0, 0, 0)
+        x1 = product3(inv1, product3(inv1, below, 1, 0), 0, 0)
         x1_ref[...] = x1
-        x0_ref[...] = product(inv0, right0 - product(turned, x1, 1, 0), 0, 0)
+        x0_ref[...] = product3(inv0, right0 - product3(turned, x1, 1, 0), 0, 0)
 
     @pl.when(col == 0)
     def _():
@@ -162,19 +189,24 @@
     row = lax.axis_index("row")
     col = lax.axis_index("col")
     core0 = lax.rem(col, 2) == 0
-    rows_in = lax.broadcasted_iota(jnp.int32, (NB, NB), 0)
-    cols_in = lax.broadcasted_iota(jnp.int32, (NB, NB), 1)
     x_own = jnp.where(core0, x0_ref[...], x1_ref[...])
     x_other = jnp.where(core0, x1_ref[...], x0_ref[...])
-    for block in range(2):
-        place = pl.ds(block * NB, NB)
-        label = row + 16 * block
-        other = other0_ref[place, :] + other_ref[place, :]
-        taken = product(own_ref[place, :], x_own, 1, 0) + product(other, x_other, 1, 0)
-        value = jnp.where(col >= 2, mine_ref[place, :], 0.0) - taken
-        last = jnp.minimum(col, 2)
-        keep = (label > last) | ((label == last) & ((col >= 2) | (rows_in >= cols_in)))
-        out_ref[place, :] = jnp.where(keep, value, 0.0)
+
+    @pl.when(col >= 2)
+    def _():
+        for block in range(2):
+            place = pl.ds(block * NB, NB)
+            taken = product3(own_ref[place, :], x_own, 1, 0) + product3(other_ref[place, :], x_other, 1, 0)
+            out_ref[place, :] = jnp.where(row + 16 * block >= 2, mine_ref[place, :] - taken, 0.0)
+
+    @pl.when(col < 2)
+    def _():
+        lower = lax.broadcasted_iota(jnp.int32, (NB, NB), 0) >= lax.broadcasted_iota(jnp.int32, (NB, NB), 1)
+        for block in range(2):
+            place = pl.ds(block * NB, NB)
+            label = row + 16 * block
+            taken = product(own_ref[place, :], x_own, 1, 0) + product(other0_ref[place, :], x_other, 1, 0)
+            out_ref[place, :] = jnp.where((label > col) | ((label == col) & lower), -taken, 0.0)
 
 
 def call(body, out, *operands, order=(), work=False, flops=0):
@@ -189,7 +221,7 @@
         whole,
         out_shape=outs,
         in_specs=[pl.BlockSpec(memory_space=space) for space in blocks],
-        scratch_shapes=[pltpu.VMEM((NB, 2 * NB), jnp.float32)] if work else [],
+        scratch_shapes=[pltpu.VMEM((NB, NB), jnp.float32)] if work else [],
         compiler_params=pltpu.CompilerParams(vmem_limit_bytes=VMEM_LIMIT),
         cost_estimate=pl.CostEstimate(flops=flops, bytes_accessed=0, transcendentals=0) if flops else None,
         name=body.__name__,

time: 93.3 us -> 88.4 us (0.947)
  the two profiles are of different devices: /device:TPU:193 before, /device:TPU:97 now
where the time goes in v3:
time: 88.4 us; the launch traced here: 87.9 us
  starting transfers between devices  24.9 us (28%)
  waiting for transfers between devices  23.9 us (27%)
  Pallas kernels  23.6 us (27%)
  blocking collectives  14.1 us (16%)
  local copies, waits for them, and re-layouts  1.05 us (1%)
    pallas_call x13, Pallas kernels, call(): pl.pallas_call(whole, out_shape=outs, in_specs=[pl.BlockSpec(memory_space...  23.6 us
    all_to_all x1, blocking collectives, scatter_rows(): return lax.all_to_all(top.reshape(16, 16, NB), 'row', 0, 0)[:2]  14.1 us
    all_to_all x1, waiting for transfers between devices, local(): lead = lax.all_to_all(spread, 'row', 0, 0)  14 us
    ppermute x3, starting transfers between devices, swap_cores(): lax.ppermute(value, 'col', [(2 * z + c, 2 * z + 1 - c) for z in chips for...  11.6 us
    ppermute x10, waiting for transfers between devices, along_z(): return lax.ppermute(value, 'col', both_cores(pairs, mirror))  9.9 us
    ppermute x10, starting transfers between devices, along_z(): return lax.ppermute(value, 'col', both_cores(pairs, mirror))  9.59 us
    all_to_all x1, starting transfers between devices, local(): lead = lax.all_to_all(spread, 'row', 0, 0)  3.7 us
  transfers between devices with their start and end apart: 14, of which 2 were waited for; matrix products, arithmetic and copies ran while one was open for 0% of the time, Pallas kernels for 23%

profile of v3, /device:TPU:97, one launch (start us, length us, event | category | flops | bytes accessed | tf_op | source)
XLA Modules:
  0.0 87.9 jit_solution(7822369843545313586)
XLA Ops:
  0.0 1.0 %slice.24 = f32[256,256]{1,0:T(8,128)S(1)} slice(f32[512,256]{1,0:T(8,128)} %refs_0_.5), slice={[0:256], [0:256]} | slice | bytes 524288 | tf_op jit(solution)/shard_map/slice | solution.py:259
  1.1 0.7 collective-permute-start
  1.8 0.7 collective-permute-start.1
  2.5 0.7 collective-permute-start.2
  3.1 0.7 collective-permute-start.3
  3.8 14.1 %conditional.4 = (f32[2,16,256]{2,1,0:T(8,128)S(1)}) conditional(s32[]{:T(128)} %convert_element_type.10, f32[256,256]{1,0:T(8,128)S(1)} %slice.24, f32[3,16,256]{2,1,0:T(8,128)S(1)} %lead_kernel.1.refs_0_.refs_1_), branch_computations={%region_2.3_spmd, %region_3.4_spmd} | conditional | bytes 589832 | solution.py:270
  3.8 14.1 %all_to_all.18 = f32[16,16,256]{2,1,0:T(8,128)S(1)} all-to-all(f32[16,16,256]{2,1,0:T(8,128)S(1)} %bitcast.4), channel_id=1, replica_groups=mesh['row'=16,'col'=32] {'row'}, dimensions={0} | all-to-all | bytes 524288 | tf_op jit(solution)/shard_map/cond/branch_0_fun/all_to_all | solution.py:246
  18.0 0.1 mask_kernel.2.refs_0_
  18.1 0.7 collective-permute-start.4
  18.8 0.7 collective-permute-start.6
  19.4 1.3 %collective-permute-start.7 = (f32[3,16,256]{2,1,0:T(8,128)S(1)}, f32[3,16,256]{2,1,0:T(8,128)S(1)}, u32[]{:S(2)}, u32[]{:S(2)}) collective-permute-start(f32[3,16,256]{2,1,0:T(8,128)S(1)} %sum_kernel.5.refs_1_.refs_2_), channel_id=1, source_target_pairs={{0,30},{1,31},{8,6},{9,7},{16,14},{17,15},{24,22},{25,23},{32,62},... | collective-permute-start | bytes 147464 | tf_op jit(solution)/shard_map/ppermute | solution.py:254
  20.7 0.7 collective-permute-start.8
  21.5 0.1 sum_kernel.6.refs_6_.refs_0_
  21.5 9.9 %collective-permute-done.7.refs_4_ = f32[3,16,256]{2,1,0:T(8,128)S(1)} collective-permute-done((f32[3,16,256]{2,1,0:T(8,128)S(1)}, f32[3,16,256]{2,1,0:T(8,128)S(1)}, u32[]{:S(2)}, u32[]{:S(2)}) %collective-permute-start.7) | collective-permute-done | bytes 49184 | tf_op jit(solution)/shard_map/ppermute | solution.py:254
  31.4 1.2 %spread_kernel.1.refs_2_ = f32[16,5,16,256]{3,2,1,0:T(8,128)} custom-call(f32[2,16,256]{2,1,0:T(8,128)S(1)} %get-tuple-element.27.refs_4_.refs_0_, f32[2,16,256]{2,1,0:T(8,128)S(1)} %get-tuple-element.28.refs_1_, f32[3,16,256]{2,1,0:T(8,128)S(1)} %sum_kernel.5.refs_1_.refs_2_, f32[3,16,256]{2,1,0:T(8,128)S(1)} %collective-permute-done.6.refs_3_, ...), custom_call_target="tpu_custom_call" | custom-call | tf_op jit(solution)/shard_map/spread_kernel/pallas_call | solution.py:220
  32.6 3.7 %all-to-all-start.3 = ((f32[16,5,16,256]{3,2,1,0:T(8,128)}), f32[16,5,16,256]{3,2,1,0:T(8,128)S(1)}, u32[]{:S(2)}, u32[]{:S(2)}) async-start(f32[16,5,16,256]{3,2,1,0:T(8,128)} %spread_kernel.1.refs_2_), calls=%async_computation.3 | async-start | bytes 2621440 | tf_op jit(solution)/shard_map/all_to_all | solution.py:278
  36.3 0.7 collective-permute-start.5
  37.0 0.1 mask_kernel.3
  37.1 1.5 %collective-permute-start.11 = (f32[512,256]{1,0:T(8,128)S(1)}, f32[512,256]{1,0:T(8,128)}, u32[]{:S(2)}, u32[]{:S(2)}) collective-permute-start(f32[512,256]{1,0:T(8,128)S(1)} %mask_kernel.3), channel_id=1, source_target_pairs={{0,1},{1,0},{32,33},{33,32},{64,65},{65,64},{96,97},{97,96},{128,1... | collective-permute-start | bytes 1572872 | tf_op jit(solution)/shard_map/ppermute | solution.py:242
  38.6 0.1 sum_kernel.7.refs_1_.refs_0_
  38.6 1.3 %collective-permute-start.9 = (f32[512,256]{1,0:T(8,128)S(1)}, f32[512,256]{1,0:T(8,128)S(1)}, u32[]{:S(2)}, u32[]{:S(2)}) collective-permute-start(f32[512,256]{1,0:T(8,128)S(1)} %sum_kernel.7.refs_1_.refs_0_), channel_id=1, source_target_pairs={{0,4},{1,29},{8,12},{25,21},{14,18},{19,15},{22,26},{11,7},{32,36}... | collective-permute-start | bytes 1572872 | tf_op jit(solution)/shard_map/ppermute | solution.py:254
  39.9 14.0 %all-to-all-done.3.refs_0_.refs_1_ = f32[16,5,16,256]{3,2,1,0:T(8,128)S(1)} async-done(((f32[16,5,16,256]{3,2,1,0:T(8,128)}), f32[16,5,16,256]{3,2,1,0:T(8,128)S(1)}, u32[]{:S(2)}, u32[]{:S(2)}) %all-to-all-start.3) | async-done | bytes 1310752 | tf_op jit(solution)/shard_map/all_to_all | solution.py:278
  53.9 8.2 %first_kernel.1.refs_2_.refs_0_.refs_1_ = f32[256,256]{1,0:T(8,128)S(1)} custom-call(f32[16,5,16,256]{3,2,1,0:T(8,128)S(1)} %all-to-all-done.3.refs_0_.refs_1_, f32[512,256]{1,0:T(8,128)S(1)} %sum_kernel.7.refs_1_.refs_0_), custom_call_target="tpu_custom_call" | custom-call | flops 10000000000 | tf_op jit(solution)/shard_map/first_kernel/pallas_call | solution.py:220
  62.2 0.0 collective-permute-done.9.refs_1_
  62.2 0.1 sum_kernel.8.refs_2_.refs_0_
  62.2 2.3 %collective-permute-start.10 = (f32[512,256]{1,0:T(8,128)S(1)}, f32[512,256]{1,0:T(8,128)S(1)}, u32[]{:S(2)}, u32[]{:S(2)}) collective-permute-start(f32[512,256]{1,0:T(8,128)S(1)} %sum_kernel.8.refs_2_.refs_0_), channel_id=1, source_target_pairs={{0,30},{1,3},{4,2},{29,31},{8,6},{25,27},{12,10},{21,23},{14,16},{... | collective-permute-start | bytes 1572872 | tf_op jit(solution)/shard_map/ppermute | solution.py:254
  64.6 9.3 %second_kernel.1 = (f32[256,256]{1,0:T(8,128)S(1)}, f32[256,256]{1,0:T(8,128)S(1)}) custom-call(f32[256,256]{1,0:T(8,128)S(1)} %first_kernel.1.refs_2_.refs_0_.refs_1_, f32[16,5,16,256]{3,2,1,0:T(8,128)S(1)} %all-to-all-done.3.refs_0_.refs_1_, f32[512,256]{1,0:T(8,128)S(1)} %sum_kernel.8.refs_2_.refs_0_), custom_call_target="tpu_custom_call" | custom-call | flops 10000000000 | tf_op jit(solution)/shard_map/second_kernel/pallas_call | solution.py:220
  73.8 0.0 collective-permute-done.10.refs_1_
  73.8 0.1 sum_kernel.9.refs_4_.refs_1_
  73.9 9.5 %collective-permute-start.12 = (f32[512,256]{1,0:T(8,128)S(1)}, f32[512,256]{1,0:T(8,128)S(1)}, u32[]{:S(2)}, u32[]{:S(2)}) collective-permute-start(f32[512,256]{1,0:T(8,128)S(1)} %sum_kernel.9.refs_4_.refs_1_), channel_id=1, source_target_pairs={{2,3},{3,2},{4,5},{5,4},{6,7},{7,6},{8,9},{9,8},{10,11},{11,10},{1... | collective-permute-start | bytes 1572872 | tf_op jit(solution)/shard_map/ppermute | solution.py:242
  83.4 2.0 %factors_kernel.1 = (f32[256,256]{1,0:T(8,128)S(1)}, f32[256,256]{1,0:T(8,128)S(1)}) custom-call(f32[16,5,16,256]{3,2,1,0:T(8,128)S(1)} %all-to-all-done.3.refs_0_.refs_1_, f32[256,256]{1,0:T(8,128)S(1)} %first_kernel.1.refs_2_.refs_0_.refs_1_, f32[256,256]{1,0:T(8,128)S(1)} %get-tuple-element.23.refs_2_, f32[256,256]{1,0:T(8,128)S(1)} %get-tuple-element.22.refs_2_.refs_3_, ...), custom_call_target="tpu_custom_call" | custom-call | tf_op jit(solution)/shard_map/factors_kernel/pallas_call | solution.py:220
  85.4 2.5 %final_kernel.1 = f32[512,256]{1,0:T(8,128)} custom-call(f32[512,256]{1,0:T(8,128)S(1)} %copy-done, f32[512,256]{1,0:T(8,128)S(1)} %sum_kernel.9.refs_4_.refs_1_, f32[512,256]{1,0:T(8,128)} %collective-permute-done.11.refs_2_, f32[512,256]{1,0:T(8,128)S(1)} %collective-permute-done.12.refs_3_, f32[256,256]{1,0:T(8,128)S(1)} %get-tuple-element.24.refs_4_, ...), custom_call_target="tpu_custom_call" | custom-call | tf_op jit(solution)/shard_map/final_kernel/pallas_call | solution.py:220
  (19 shorter events, 0.1 us)
Async XLA Ops:
  0.0 18.0 %copy-start = (f32[512,256]{1,0:T(8,128)S(1)}, f32[512,256]{1,0:T(8,128)}, u32[]{:S(2)}) copy-start(f32[512,256]{1,0:T(8,128)} %refs_0_.5) | copy-start | bytes 1572868
  1.1 0.7 collective-permute-start
  1.8 16.1 %collective-permute-start.1 = (f32[3,16,256]{2,1,0:T(8,128)S(1)}, f32[3,16,256]{2,1,0:T(8,128)S(1)}, u32[]{:S(2)}, u32[]{:S(2)}) collective-permute-start(f32[3,16,256]{2,1,0:T(8,128)S(1)} %lead_kernel.1.refs_0_.refs_1_), channel_id=1, source_target_pairs={{0,24},{1,25},{32,56},{33,57},{64,88},{65,89},{96,120},{97,121},{1... | collective-permute-start | bytes 147464 | tf_op jit(solution)/shard_map/ppermute | solution.py:254
  2.5 15.5 %collective-permute-start.2 = (f32[3,16,256]{2,1,0:T(8,128)S(1)}, f32[3,16,256]{2,1,0:T(8,128)S(1)}, u32[]{:S(2)}, u32[]{:S(2)}) collective-permute-start(f32[3,16,256]{2,1,0:T(8,128)S(1)} %lead_kernel.1.refs_0_.refs_1_), channel_id=1, source_target_pairs={{0,8},{1,9},{32,40},{33,41},{64,72},{65,73},{96,104},{97,105},{128... | collective-permute-start | bytes 147464 | tf_op jit(solution)/shard_map/ppermute | solution.py:254
  3.1 14.8 %collective-permute-start.3 = (f32[3,16,256]{2,1,0:T(8,128)S(1)}, f32[3,16,256]{2,1,0:T(8,128)S(1)}, u32[]{:S(2)}, u32[]{:S(2)}) collective-permute-start(f32[3,16,256]{2,1,0:T(8,128)S(1)} %lead_kernel.1.refs_0_.refs_1_), channel_id=1, source_target_pairs={{0,16},{1,17},{32,48},{33,49},{64,80},{65,81},{96,112},{97,113},{1... | collective-permute-start | bytes 147464 | tf_op jit(solution)/shard_map/ppermute | solution.py:254
  18.1 3.4 %collective-permute-start.4 = (f32[512,256]{1,0:T(8,128)S(1)}, f32[512,256]{1,0:T(8,128)S(1)}, u32[]{:S(2)}, u32[]{:S(2)}) collective-permute-start(f32[512,256]{1,0:T(8,128)S(1)} %mask_kernel.2.refs_0_), channel_id=1, source_target_pairs={{0,14},{1,19},{32,46},{33,51},{64,78},{65,83},{96,110},{97,115},{1... | collective-permute-start | bytes 1572872 | tf_op jit(solution)/shard_map/ppermute | solution.py:254
  18.8 2.8 %collective-permute-start.6 = (f32[3,16,256]{2,1,0:T(8,128)S(1)}, f32[3,16,256]{2,1,0:T(8,128)S(1)}, u32[]{:S(2)}, u32[]{:S(2)}) collective-permute-start(f32[3,16,256]{2,1,0:T(8,128)S(1)} %sum_kernel.5.refs_1_.refs_2_), channel_id=1, source_target_pairs={{0,2},{1,3},{8,10},{9,11},{16,18},{17,19},{24,26},{25,27},{32,34},... | collective-permute-start | bytes 147464 | tf_op jit(solution)/shard_map/ppermute | solution.py:254
  19.4 12.0 %collective-permute-start.7 = (f32[3,16,256]{2,1,0:T(8,128)S(1)}, f32[3,16,256]{2,1,0:T(8,128)S(1)}, u32[]{:S(2)}, u32[]{:S(2)}) collective-permute-start(f32[3,16,256]{2,1,0:T(8,128)S(1)} %sum_kernel.5.refs_1_.refs_2_), channel_id=1, source_target_pairs={{0,30},{1,31},{8,6},{9,7},{16,14},{17,15},{24,22},{25,23},{32,62},... | collective-permute-start | bytes 147464 | tf_op jit(solution)/shard_map/ppermute | solution.py:254
  20.7 10.7 %collective-permute-start.8 = (f32[3,16,256]{2,1,0:T(8,128)S(1)}, f32[3,16,256]{2,1,0:T(8,128)S(1)}, u32[]{:S(2)}, u32[]{:S(2)}) collective-permute-start(f32[3,16,256]{2,1,0:T(8,128)S(1)} %sum_kernel.5.refs_1_.refs_2_), channel_id=1, source_target_pairs={{0,4},{1,5},{8,12},{9,13},{16,20},{17,21},{24,28},{25,29},{32,36},... | collective-permute-start | bytes 147464 | tf_op jit(solution)/shard_map/ppermute | solution.py:254
  32.6 21.3 %all-to-all-start.3 = ((f32[16,5,16,256]{3,2,1,0:T(8,128)}), f32[16,5,16,256]{3,2,1,0:T(8,128)S(1)}, u32[]{:S(2)}, u32[]{:S(2)}) async-start(f32[16,5,16,256]{3,2,1,0:T(8,128)} %spread_kernel.1.refs_2_), calls=%async_computation.3 | async-start | bytes 2621440 | tf_op jit(solution)/shard_map/all_to_all | solution.py:278
  36.3 2.2 %collective-permute-start.5 = (f32[512,256]{1,0:T(8,128)S(1)}, f32[512,256]{1,0:T(8,128)S(1)}, u32[]{:S(2)}, u32[]{:S(2)}) collective-permute-start(f32[512,256]{1,0:T(8,128)S(1)} %sum_kernel.6.refs_6_.refs_0_), channel_id=1, source_target_pairs={{0,8},{1,25},{14,22},{19,11},{32,40},{33,57},{46,54},{51,43},{64,7... | collective-permute-start | bytes 1572872 | tf_op jit(solution)/shard_map/ppermute | solution.py:254
  37.1 48.3 %collective-permute-start.11 = (f32[512,256]{1,0:T(8,128)S(1)}, f32[512,256]{1,0:T(8,128)}, u32[]{:S(2)}, u32[]{:S(2)}) collective-permute-start(f32[512,256]{1,0:T(8,128)S(1)} %mask_kernel.3), channel_id=1, source_target_pairs={{0,1},{1,0},{32,33},{33,32},{64,65},{65,64},{96,97},{97,96},{128,1... | collective-permute-start | bytes 1572872 | tf_op jit(solution)/shard_map/ppermute | solution.py:242
  38.6 23.5 %collective-permute-start.9 = (f32[512,256]{1,0:T(8,128)S(1)}, f32[512,256]{1,0:T(8,128)S(1)}, u32[]{:S(2)}, u32[]{:S(2)}) collective-permute-start(f32[512,256]{1,0:T(8,128)S(1)} %sum_kernel.7.refs_1_.refs_0_), channel_id=1, source_target_pairs={{0,4},{1,29},{8,12},{25,21},{14,18},{19,15},{22,26},{11,7},{32,36}... | collective-permute-start | bytes 1572872 | tf_op jit(solution)/shard_map/ppermute | solution.py:254
  62.2 11.6 %collective-permute-start.10 = (f32[512,256]{1,0:T(8,128)S(1)}, f32[512,256]{1,0:T(8,128)S(1)}, u32[]{:S(2)}, u32[]{:S(2)}) collective-permute-start(f32[512,256]{1,0:T(8,128)S(1)} %sum_kernel.8.refs_2_.refs_0_), channel_id=1, source_target_pairs={{0,30},{1,3},{4,2},{29,31},{8,6},{25,27},{12,10},{21,23},{14,16},{... | collective-permute-start | bytes 1572872 | tf_op jit(solution)/shard_map/ppermute | solution.py:254
  73.9 11.5 %collective-permute-start.12 = (f32[512,256]{1,0:T(8,128)S(1)}, f32[512,256]{1,0:T(8,128)S(1)}, u32[]{:S(2)}, u32[]{:S(2)}) collective-permute-start(f32[512,256]{1,0:T(8,128)S(1)} %sum_kernel.9.refs_4_.refs_1_), channel_id=1, source_target_pairs={{2,3},{3,2},{4,5},{5,4},{6,7},{7,6},{8,9},{9,8},{10,11},{11,10},{1... | collective-permute-start | bytes 1572872 | tf_op jit(solution)/shard_map/ppermute | solution.py:242

commit v4 on v3

--- a/solution.py
+++ b/solution.py
@@ -10,7 +10,7 @@
 LANES = 128
 SUBS = 8
 HIGHEST = lax.Precision.HIGHEST
-VMEM_LIMIT = 10 * 1024 * 1024
+VMEM_LIMIT = 6 * 1024 * 1024
 
 CHIPS_Z = 16
 PANEL_TREE = (
@@ -123,26 +123,29 @@
     inverse_factor(lead_ref[:, 0].reshape(NB, NB), inv_ref, work)
 
 
-def second_kernel(inv0_ref, lead_ref, turned_ref, inv_ref, work):
-    turned = product(inv0_ref[...], lead_ref[:, 1].reshape(NB, NB), 1, 0)
+def second_kernel(inv0_ref, lead_ref, swapped_ref, turned_ref, inv_ref, work):
+    core0 = lax.rem(lax.axis_index("col"), 2) == 0
+    mine = lead_ref[:, 1].reshape(NB, NB)
+    swapped = swapped_ref[...].reshape(NB, NB)
+    turned = product(inv0_ref[...], jnp.where(core0, mine, swapped), 1, 1)
     turned_ref[...] = turned
-    square = lead_ref[:, 2].reshape(NB, NB) - product(turned, turned, 0, 0)
-    inverse_factor(square, inv_ref, work)
-
-
-def lead_kernel(first_ref, swapped_ref, lead_ref):
-    col = lax.axis_index("col")
-    bottom = col < 2
-    core0 = lax.rem(col, 2) == 0
-    first = jnp.where(bottom, first_ref[...], 0.0)
-    swapped = jnp.where(bottom, swapped_ref[...], 0.0)
-    lead_ref[0] = jnp.where(core0, first[0], swapped[0])
-    lead_ref[1] = jnp.where(core0, swapped[0], first[0])
-    lead_ref[2] = jnp.where(core0, swapped[1], first[1])
-
-
-def mask_kernel(value_ref, out_ref):
-    out_ref[...] = jnp.where(lax.axis_index("col") < 2, value_ref[...], 0.0)
+    square = jnp.where(core0, swapped, mine)
+    inverse_factor(square - product(turned, turned, 0, 0), inv_ref, work)
+
+
+def lead_kernel(first_ref, passed_ref, lead_ref):
+    core0 = lax.rem(lax.axis_index("col"), 2) == 0
+    lead_ref[0] = jnp.where(core0, first_ref[0], passed_ref[...])
+    lead_ref[1] = first_ref[1]
+
+
+def pick_kernel(lead_ref, out_ref):
+    out_ref[...] = lead_ref[:, 1]
+
+
+def panel_kernel(value_ref, panel_ref, mine_ref):
+    panel_ref[...] = jnp.where(lax.axis_index("col") < 2, value_ref[...], 0.0)
+    mine_ref[...] = value_ref[...]
 
 
 def sum_kernel(*refs):
@@ -156,8 +159,8 @@
     total = base_ref[...] + a_ref[...] + b_ref[...] + c_ref[...]
     pieces = early_ref[...] + late_ref[...]
     for target in range(out_ref.shape[0]):
-        out_ref[target, :3] = total
-        out_ref[target, 3:] = pieces
+        out_ref[target, :2] = total
+        out_ref[target, 2:] = pieces
 
 
 def factors_kernel(cols_ref, inv0_ref, turned_ref, inv1_ref, x0_ref, x1_ref):
@@ -168,8 +171,8 @@
 
     @pl.when(col >= 2)
     def _():
-        right0 = product3(inv0, cols_ref[:, 3].reshape(NB, NB), 1, 0)
-        below = cols_ref[:, 4].reshape(NB, NB) - product3(turned, right0, 0, 0)
+        right0 = product3(inv0, cols_ref[:, 2].reshape(NB, NB), 1, 0)
+        below = cols_ref[:, 3].reshape(NB, NB) - product3(turned, right0, 0, 0)
         x1 = product3(inv1, product3(inv1, below, 1, 0), 0, 0)
         x1_ref[...] = x1
         x0_ref[...] = product3(inv0, right0 - product3(turned, x1, 1, 0), 0, 0)
@@ -185,7 +188,7 @@
         x1_ref[...] = -inv1.T
 
 
-def final_kernel(mine_ref, own_ref, other0_ref, other_ref, x0_ref, x1_ref, out_ref):
+def final_kernel(mine_ref, own_ref, other_ref, x0_ref, x1_ref, other0_ref, out_ref, held, sem):
     row = lax.axis_index("row")
     col = lax.axis_index("col")
     core0 = lax.rem(col, 2) == 0
@@ -196,36 +199,43 @@
     def _():
         for block in range(2):
             place = pl.ds(block * NB, NB)
-            taken = product3(own_ref[place, :], x_own, 1, 0) + product3(other_ref[place, :], x_other, 1, 0)
+            taken = product(own_ref[place, :], x_own, 1, 0) + product(other_ref[place, :], x_other, 1, 0)
             out_ref[place, :] = jnp.where(row + 16 * block >= 2, mine_ref[place, :] - taken, 0.0)
 
     @pl.when(col < 2)
     def _():
+        copy = pltpu.make_async_copy(other0_ref, held, sem)
+        copy.start()
+        copy.wait()
         lower = lax.broadcasted_iota(jnp.int32, (NB, NB), 0) >= lax.broadcasted_iota(jnp.int32, (NB, NB), 1)
         for block in range(2):
             place = pl.ds(block * NB, NB)
             label = row + 16 * block
-            taken = product(own_ref[place, :], x_own, 1, 0) + product(other0_ref[place, :], x_other, 1, 0)
+            taken = product(own_ref[place, :], x_own, 1, 0) + product(held[place, :], x_other, 1, 0)
             out_ref[place, :] = jnp.where((label > col) | ((label == col) & lower), -taken, 0.0)
 
 
-def call(body, out, *operands, order=(), work=False, flops=0):
+def call(body, out, *operands, far=(), order=(), work=False, flops=0):
     kept = len(operands)
-    blocks = [pltpu.VMEM] * kept + [pl.ANY] * len(order)
+    read = kept + len(far)
+    blocks = [pltpu.VMEM] * kept + [pl.ANY] * (len(far) + len(order))
+    scratch = [pltpu.VMEM((NB, NB), jnp.float32)] if work else []
+    for array in far:
+        scratch += [pltpu.VMEM(array.shape, array.dtype), pltpu.SemaphoreType.DMA]
 
     def whole(*refs):
-        body(*refs[:kept], *refs[kept + len(order) :])
+        body(*refs[:read], *refs[read + len(order) :])
 
     outs = jax.tree.map(lambda shape: jax.ShapeDtypeStruct(shape, jnp.float32), out, is_leaf=lambda v: type(v[0]) is int)
     return pl.pallas_call(
         whole,
         out_shape=outs,
         in_specs=[pl.BlockSpec(memory_space=space) for space in blocks],
-        scratch_shapes=[pltpu.VMEM((NB, NB), jnp.float32)] if work else [],
+        scratch_shapes=scratch,
         compiler_params=pltpu.CompilerParams(vmem_limit_bytes=VMEM_LIMIT),
         cost_estimate=pl.CostEstimate(flops=flops, bytes_accessed=0, transcendentals=0) if flops else None,
         name=body.__name__,
-    )(*operands, *order)
+    )(*operands, *far, *order)
 
 
 def both_cores(pairs, mirror):
@@ -262,31 +272,30 @@
     height = lax.axis_index("col") // 2
     bottom = height == 0
     first = lax.cond(bottom, scatter_rows, no_rows, top)
-    swapped = swap_cores(first, [0])
-    lead = call(lead_kernel, (3, 16, NB), first, swapped)
-    other0 = swap_cores(call(mask_kernel, kernel.shape, kernel, order=(lead,)), [0])
+    lead = call(lead_kernel, (2, 16, NB), first, lax.ppermute(first[0], "col", [(0, 1)]))
     sent = [along_z(lead, p) for p in PIECE_TREE[0]]
     waits = (height == 7) | (height == 9)
-    early = lax.cond(bottom | waits, lambda t, l: l[:2], lambda t, l: scatter_rows(t), top, lead)
-    lead = call(sum_kernel, (3, 16, NB), lead, *sent, order=(early,))
-
-    panel = call(mask_kernel, kernel.shape, kernel, order=(lead,))
+    early = lax.cond(bottom | waits, lambda t, l: l, lambda t, l: scatter_rows(t), top, lead)
+    lead = call(sum_kernel, (2, 16, NB), lead, *sent, order=(early,))
+
+    panel, mine = call(panel_kernel, (kernel.shape, kernel.shape), kernel, order=(lead,))
+    other0 = swap_cores(mine, [0])
     panel = call(sum_kernel, kernel.shape, panel, along_z(panel, PANEL_TREE[0], True))
     late = lax.cond(waits, lambda t, l: scatter_rows(t), lambda t, l: no_rows(t), top, lead)
     sent = [along_z(lead, p) for p in PIECE_TREE[1]]
-    spread = call(spread_kernel, (16, 5, 16, NB), early, late, lead, *sent, order=(panel,))
+    spread = call(spread_kernel, (16, 4, 16, NB), early, late, lead, *sent, order=(panel,))
     lead = lax.all_to_all(spread, "row", 0, 0)
-
     panel = call(sum_kernel, kernel.shape, panel, along_z(panel, PANEL_TREE[1], True), order=(spread,))
-    inv0 = call(first_kernel, square, lead, order=(panel,), work=True, flops=ten_us)
+    swapped = swap_cores(call(pick_kernel, (16, 16, NB), lead, order=(panel,)), range(CHIPS_Z))
+    inv0 = call(first_kernel, square, lead, order=(panel, other0), work=True, flops=ten_us)
     panel = call(sum_kernel, kernel.shape, panel, along_z(panel, PANEL_TREE[2], True), order=(inv0,))
     turned, inv1 = call(
-        second_kernel, (square, square), inv0, lead, order=(panel,), work=True, flops=ten_us
+        second_kernel, (square, square), inv0, lead, swapped, order=(panel,), work=True, flops=ten_us
     )
     panel = call(sum_kernel, kernel.shape, panel, along_z(panel, PANEL_TREE[3], True), order=(inv1,))
     other = swap_cores(panel, range(1, CHIPS_Z))
     x0, x1 = call(factors_kernel, (square, square), lead, inv0, turned, inv1, order=(panel,))
-    return call(final_kernel, kernel.shape, kernel, panel, other0, other, x0, x1)
+    return call(final_kernel, kernel.shape, mine, panel, other, x0, x1, far=(other0,))
 
 
 def solution(mesh):

time: 88.4 us -> 86.6 us (0.980)
  the two profiles are of different devices: /device:TPU:97 before, /device:TPU:1 now
where the time goes in v4:
time: 86.6 us; the launch traced here: 86 us
  starting transfers between devices  38.5 us (44%)
  Pallas kernels  23.1 us (27%)
  blocking collectives  14.9 us (17%)
  waiting for transfers between devices  7.95 us (9%)
  local copies, waits for them, and re-layouts  0.98 us (1%)
    pallas_call x13, Pallas kernels, call(): pl.pallas_call(whole, out_shape=outs, in_specs=[pl.BlockSpec(memory_space...  23.1 us
    ppermute x10, starting transfers between devices, along_z(): return lax.ppermute(value, 'col', both_cores(pairs, mirror))  22.9 us
    all_to_all x1, blocking collectives, scatter_rows(): return lax.all_to_all(top.reshape(16, 16, NB), 'row', 0, 0)[:2]  14.9 us
    ppermute x3, starting transfers between devices, swap_cores(): lax.ppermute(value, 'col', [(2 * z + c, 2 * z + 1 - c) for z in chips for...  10.6 us
    ppermute x10, waiting for transfers between devices, along_z(): return lax.ppermute(value, 'col', both_cores(pairs, mirror))  4 us
    ppermute x1, waiting for transfers between devices, local(): lax.ppermute(first[0], 'col', [(0, 1)])  3.89 us
    all_to_all x1, starting transfers between devices, local(): lead = lax.all_to_all(spread, 'row', 0, 0)  3.65 us
  transfers between devices with their start and end apart: 15, of which 5 were waited for; matrix products, arithmetic and copies ran while one was open for 0% of the time, Pallas kernels for 22%

profile of v4, /device:TPU:1, one launch (start us, length us, event | category | flops | bytes accessed | tf_op | source)
XLA Modules:
  0.0 86.0 jit_solution(2732808357348460159)
XLA Ops:
  0.0 1.0 %slice.24 = f32[256,256]{1,0:T(8,128)S(1)} slice(f32[512,256]{1,0:T(8,128)} %refs_0_.1), slice={[0:256], [0:256]} | slice | bytes 524288 | tf_op jit(solution)/shard_map/slice | solution.py:269
  1.0 15.0 %conditional.3 = (f32[2,16,256]{2,1,0:T(8,128)S(1)}) conditional(s32[]{:T(128)} %convert_element_type.9, () %tuple.23, f32[256,256]{1,0:T(8,128)S(1)} %slice.24), branch_computations={%region_0.1_spmd, %region_1.2_spmd} | conditional | bytes 589832 | solution.py:274
  1.0 14.9 %all_to_all.17 = f32[16,16,256]{2,1,0:T(8,128)S(1)} all-to-all(f32[16,16,256]{2,1,0:T(8,128)S(1)} %bitcast.5), channel_id=1, replica_groups=mesh['row'=16,'col'=32] {'row'}, dimensions={0} | all-to-all | bytes 524288 | tf_op jit(solution)/shard_map/cond/branch_1_fun/all_to_all | solution.py:256
  15.9 1.4 %collective-permute-start = (f32[16,256]{1,0:T(8,128)S(1)}, f32[16,256]{1,0:T(8,128)S(1)}, u32[]{:S(2)}, u32[]{:S(2)}) collective-permute-start(f32[16,256]{1,0:T(8,128)S(1)} %slice_bitcast_fusion), channel_id=1, source_target_pairs={{0,1},{32,33},{64,65},{96,97},{128,129},{160,161},{192,193},{224,2... | collective-permute-start | bytes 49160 | tf_op jit(solution)/shard_map/ppermute | solution.py:275
  17.4 3.9 %collective-permute-done.refs_1_ = f32[16,256]{1,0:T(8,128)S(1)} collective-permute-done((f32[16,256]{1,0:T(8,128)S(1)}, f32[16,256]{1,0:T(8,128)S(1)}, u32[]{:S(2)}, u32[]{:S(2)}) %collective-permute-start) | collective-permute-done | bytes 16416 | tf_op jit(solution)/shard_map/ppermute | solution.py:275
  21.3 1.3 %collective-permute-start.3 = (f32[2,16,256]{2,1,0:T(8,128)S(1)}, f32[2,16,256]{2,1,0:T(8,128)S(1)}, u32[]{:S(2)}, u32[]{:S(2)}) collective-permute-start(f32[2,16,256]{2,1,0:T(8,128)S(1)} %lead_kernel.1.refs_0_), channel_id=1, source_target_pairs={{0,16},{1,17},{32,48},{33,49},{64,80},{65,81},{96,112},{97,113},{1... | collective-permute-start | bytes 98312 | tf_op jit(solution)/shard_map/ppermute | solution.py:264
  22.6 1.3 %collective-permute-start.2 = (f32[2,16,256]{2,1,0:T(8,128)S(1)}, f32[2,16,256]{2,1,0:T(8,128)S(1)}, u32[]{:S(2)}, u32[]{:S(2)}) collective-permute-start(f32[2,16,256]{2,1,0:T(8,128)S(1)} %lead_kernel.1.refs_0_), channel_id=1, source_target_pairs={{0,8},{1,9},{32,40},{33,41},{64,72},{65,73},{96,104},{97,105},{128... | collective-permute-start | bytes 98312 | tf_op jit(solution)/shard_map/ppermute | solution.py:264
  23.9 1.3 %collective-permute-start.1 = (f32[2,16,256]{2,1,0:T(8,128)S(1)}, f32[2,16,256]{2,1,0:T(8,128)S(1)}, u32[]{:S(2)}, u32[]{:S(2)}) collective-permute-start(f32[2,16,256]{2,1,0:T(8,128)S(1)} %lead_kernel.1.refs_0_), channel_id=1, source_target_pairs={{0,24},{1,25},{32,56},{33,57},{64,88},{65,89},{96,120},{97,121},{1... | collective-permute-start | bytes 98312 | tf_op jit(solution)/shard_map/ppermute | solution.py:264
  25.2 0.9 %collective-permute-done.1.refs_1_ = f32[2,16,256]{2,1,0:T(8,128)S(1)} collective-permute-done((f32[2,16,256]{2,1,0:T(8,128)S(1)}, f32[2,16,256]{2,1,0:T(8,128)S(1)}, u32[]{:S(2)}, u32[]{:S(2)}) %collective-permute-start.1) | collective-permute-done | bytes 32800 | tf_op jit(solution)/shard_map/ppermute | solution.py:264
  26.2 0.1 panel_kernel.1
  26.3 1.3 %collective-permute-start.4 = (f32[512,256]{1,0:T(8,128)S(1)}, f32[512,256]{1,0:T(8,128)S(1)}, u32[]{:S(2)}, u32[]{:S(2)}) collective-permute-start(f32[512,256]{1,0:T(8,128)S(1)} %get-tuple-element.25.refs_0_), channel_id=1, source_target_pairs={{0,14},{1,19},{32,46},{33,51},{64,78},{65,83},{96,110},{97,115},{1... | collective-permute-start | bytes 1572872 | tf_op jit(solution)/shard_map/ppermute | solution.py:264
  27.6 1.3 %collective-permute-start.8 = (f32[2,16,256]{2,1,0:T(8,128)S(1)}, f32[2,16,256]{2,1,0:T(8,128)S(1)}, u32[]{:S(2)}, u32[]{:S(2)}) collective-permute-start(f32[2,16,256]{2,1,0:T(8,128)S(1)} %sum_kernel.5.refs_1_.refs_2_), channel_id=1, source_target_pairs={{0,4},{1,5},{8,12},{9,13},{16,20},{17,21},{24,28},{25,29},{32,36},... | collective-permute-start | bytes 98312 | tf_op jit(solution)/shard_map/ppermute | solution.py:264
  28.9 2.6 %collective-permute-start.7 = (f32[2,16,256]{2,1,0:T(8,128)S(1)}, f32[2,16,256]{2,1,0:T(8,128)S(1)}, u32[]{:S(2)}, u32[]{:S(2)}) collective-permute-start(f32[2,16,256]{2,1,0:T(8,128)S(1)} %sum_kernel.5.refs_1_.refs_2_), channel_id=1, source_target_pairs={{0,30},{1,31},{8,6},{9,7},{16,14},{17,15},{24,22},{25,23},{32,62},... | collective-permute-start | bytes 98312 | tf_op jit(solution)/shard_map/ppermute | solution.py:264
  31.5 1.3 %collective-permute-start.6 = (f32[2,16,256]{2,1,0:T(8,128)S(1)}, f32[2,16,256]{2,1,0:T(8,128)S(1)}, u32[]{:S(2)}, u32[]{:S(2)}) collective-permute-start(f32[2,16,256]{2,1,0:T(8,128)S(1)} %sum_kernel.5.refs_1_.refs_2_), channel_id=1, source_target_pairs={{0,2},{1,3},{8,10},{9,11},{16,18},{17,19},{24,26},{25,27},{32,34},... | collective-permute-start | bytes 98312 | tf_op jit(solution)/shard_map/ppermute | solution.py:264
  32.8 0.9 %collective-permute-done.4.refs_1_ = f32[512,256]{1,0:T(8,128)S(1)} collective-permute-done((f32[512,256]{1,0:T(8,128)S(1)}, f32[512,256]{1,0:T(8,128)S(1)}, u32[]{:S(2)}, u32[]{:S(2)}) %collective-permute-start.4) | collective-permute-done | bytes 524320 | tf_op jit(solution)/shard_map/ppermute | solution.py:264
  33.7 0.1 sum_kernel.6.refs_6_.refs_0_
  33.7 0.3 collective-permute-done.7.refs_4_
  34.0 1.1 %spread_kernel.1.refs_2_ = f32[16,4,16,256]{3,2,1,0:T(8,128)} custom-call(f32[2,16,256]{2,1,0:T(8,128)S(1)} %get-tuple-element.31.refs_4_.refs_0_, f32[2,16,256]{2,1,0:T(8,128)S(1)} %get-tuple-element.32.refs_1_, f32[2,16,256]{2,1,0:T(8,128)S(1)} %sum_kernel.5.refs_1_.refs_2_, f32[2,16,256]{2,1,0:T(8,128)S(1)} %collective-permute-done.6.refs_3_, ...), custom_call_target="tpu_custom_call" | custom-call | tf_op jit(solution)/shard_map/spread_kernel/pallas_call | solution.py:230
  35.1 3.7 %all-to-all-start.3 = ((f32[16,4,16,256]{3,2,1,0:T(8,128)}), f32[16,4,16,256]{3,2,1,0:T(8,128)S(1)}, u32[]{:S(2)}, u32[]{:S(2)}) async-start(f32[16,4,16,256]{3,2,1,0:T(8,128)} %spread_kernel.1.refs_2_), calls=%async_computation.3 | async-start | bytes 2097152 | tf_op jit(solution)/shard_map/all_to_all | solution.py:287
  38.8 7.1 %collective-permute-start.5 = (f32[512,256]{1,0:T(8,128)S(1)}, f32[512,256]{1,0:T(8,128)S(1)}, u32[]{:S(2)}, u32[]{:S(2)}) collective-permute-start(f32[512,256]{1,0:T(8,128)S(1)} %sum_kernel.6.refs_6_.refs_0_), channel_id=1, source_target_pairs={{0,8},{1,25},{14,22},{19,11},{32,40},{33,57},{46,54},{51,43},{64,7... | collective-permute-start | bytes 1572872 | tf_op jit(solution)/shard_map/ppermute | solution.py:264
  45.9 4.2 %collective-permute-start.10 = (f32[512,256]{1,0:T(8,128)S(1)}, f32[512,256]{1,0:T(8,128)}, u32[]{:S(2)}, u32[]{:S(2)}) collective-permute-start(f32[512,256]{1,0:T(8,128)S(1)} %get-tuple-element.24.refs_0_), channel_id=1, source_target_pairs={{0,1},{1,0},{32,33},{33,32},{64,65},{65,64},{96,97},{97,96},{128,1... | collective-permute-start | bytes 1572872 | tf_op jit(solution)/shard_map/ppermute | solution.py:252
  50.1 1.9 %collective-permute-done.5.refs_1_ = f32[512,256]{1,0:T(8,128)S(1)} collective-permute-done((f32[512,256]{1,0:T(8,128)S(1)}, f32[512,256]{1,0:T(8,128)S(1)}, u32[]{:S(2)}, u32[]{:S(2)}) %collective-permute-start.5) | collective-permute-done | bytes 524320 | tf_op jit(solution)/shard_map/ppermute | solution.py:264
  52.1 1.3 %collective-permute-start.9 = (f32[512,256]{1,0:T(8,128)S(1)}, f32[512,256]{1,0:T(8,128)S(1)}, u32[]{:S(2)}, u32[]{:S(2)}) collective-permute-start(f32[512,256]{1,0:T(8,128)S(1)} %sum_kernel.7.refs_1_.refs_0_), channel_id=1, source_target_pairs={{0,4},{1,29},{8,12},{25,21},{14,18},{19,15},{22,26},{11,7},{32,36}... | collective-permute-start | bytes 1572872 | tf_op jit(solution)/shard_map/ppermute | solution.py:264
  53.5 5.7 %collective-permute-start.12 = (f32[16,16,256]{2,1,0:T(8,128)S(1)}, f32[16,16,256]{2,1,0:T(8,128)S(1)}, u32[]{:S(2)}, u32[]{:S(2)}) collective-permute-start(f32[16,16,256]{2,1,0:T(8,128)S(1)} %pick_kernel.1), channel_id=1, source_target_pairs={{0,1},{1,0},{2,3},{3,2},{4,5},{5,4},{6,7},{7,6},{8,9},{9,8},{10,11... | collective-permute-start | bytes 786440 | tf_op jit(solution)/shard_map/ppermute | solution.py:252
  59.2 8.2 %first_kernel.1.refs_2_.refs_0_.refs_1_ = f32[256,256]{1,0:T(8,128)S(1)} custom-call(f32[16,4,16,256]{3,2,1,0:T(8,128)S(1)} %all-to-all-done.3.refs_0_.refs_1_, f32[512,256]{1,0:T(8,128)S(1)} %sum_kernel.7.refs_1_.refs_0_, f32[512,256]{1,0:T(8,128)} %collective-permute-done.10.refs_2_.refs_5_), custom_call_target="tpu_custom_call" | custom-call | flops 10000000000 | tf_op jit(solution)/shard_map/first_kernel/pallas_call | solution.py:230
  67.4 0.1 sum_kernel.8.refs_3_.refs_0_
  67.5 4.1 %collective-permute-start.11 = (f32[512,256]{1,0:T(8,128)S(1)}, f32[512,256]{1,0:T(8,128)S(1)}, u32[]{:S(2)}, u32[]{:S(2)}) collective-permute-start(f32[512,256]{1,0:T(8,128)S(1)} %sum_kernel.8.refs_3_.refs_0_), channel_id=1, source_target_pairs={{0,30},{1,3},{4,2},{29,31},{8,6},{25,27},{12,10},{21,23},{14,16},{... | collective-permute-start | bytes 1572872 | tf_op jit(solution)/shard_map/ppermute | solution.py:264
  71.6 9.3 %second_kernel.1 = (f32[256,256]{1,0:T(8,128)S(1)}, f32[256,256]{1,0:T(8,128)S(1)}) custom-call(f32[256,256]{1,0:T(8,128)S(1)} %first_kernel.1.refs_2_.refs_0_.refs_1_, f32[16,4,16,256]{3,2,1,0:T(8,128)S(1)} %all-to-all-done.3.refs_0_.refs_1_, f32[16,16,256]{2,1,0:T(8,128)S(1)} %collective-permute-done.12.refs_2_, f32[512,256]{1,0:T(8,128)S(1)} %sum_kernel.8.refs_3_.refs_0_), custom_call_target="tpu_custom_call" | custom-call | flops 10000000000 | tf_op jit(solution)/shard_map/second_kernel/pallas_call | solution.py:230
  80.9 0.1 sum_kernel.9.refs_4_.refs_1_
  81.0 0.7 collective-permute-start.13
  81.7 1.2 %factors_kernel.1 = (f32[256,256]{1,0:T(8,128)S(1)}, f32[256,256]{1,0:T(8,128)S(1)}) custom-call(f32[16,4,16,256]{3,2,1,0:T(8,128)S(1)} %all-to-all-done.3.refs_0_.refs_1_, f32[256,256]{1,0:T(8,128)S(1)} %first_kernel.1.refs_2_.refs_0_.refs_1_, f32[256,256]{1,0:T(8,128)S(1)} %get-tuple-element.27.refs_2_, f32[256,256]{1,0:T(8,128)S(1)} %get-tuple-element.26.refs_2_.refs_3_, ...), custom_call_target="tpu_custom_call" | custom-call | tf_op jit(solution)/shard_map/factors_kernel/pallas_call | solution.py:230
  82.9 3.0 %final_kernel.1 = f32[512,256]{1,0:T(8,128)} custom-call(f32[512,256]{1,0:T(8,128)S(1)} %get-tuple-element.24.refs_0_, f32[512,256]{1,0:T(8,128)S(1)} %sum_kernel.9.refs_4_.refs_1_, f32[512,256]{1,0:T(8,128)S(1)} %collective-permute-done.13.refs_2_, f32[256,256]{1,0:T(8,128)S(1)} %get-tuple-element.28.refs_3_, f32[256,256]{1,0:T(8,128)S(1)} %get-tuple-element.29.refs_4_, ...), custom_call_target="tpu_custom_call" | custom-call | tf_op jit(solution)/shard_map/final_kernel/pallas_call | solution.py:230
  (22 shorter events, 0.2 us)
Async XLA Ops:
  15.9 10.2 %copy-start = (f32[512,256]{1,0:T(8,128)S(1)}, f32[512,256]{1,0:T(8,128)}, u32[]{:S(2)}) copy-start(f32[512,256]{1,0:T(8,128)} %refs_0_.1) | copy-start | bytes 1572868
  15.9 5.3 %collective-permute-start = (f32[16,256]{1,0:T(8,128)S(1)}, f32[16,256]{1,0:T(8,128)S(1)}, u32[]{:S(2)}, u32[]{:S(2)}) collective-permute-start(f32[16,256]{1,0:T(8,128)S(1)} %slice_bitcast_fusion), channel_id=1, source_target_pairs={{0,1},{32,33},{64,65},{96,97},{128,129},{160,161},{192,193},{224,2... | collective-permute-start | bytes 49160 | tf_op jit(solution)/shard_map/ppermute | solution.py:275
  21.3 3.9 %collective-permute-start.3 = (f32[2,16,256]{2,1,0:T(8,128)S(1)}, f32[2,16,256]{2,1,0:T(8,128)S(1)}, u32[]{:S(2)}, u32[]{:S(2)}) collective-permute-start(f32[2,16,256]{2,1,0:T(8,128)S(1)} %lead_kernel.1.refs_0_), channel_id=1, source_target_pairs={{0,16},{1,17},{32,48},{33,49},{64,80},{65,81},{96,112},{97,113},{1... | collective-permute-start | bytes 98312 | tf_op jit(solution)/shard_map/ppermute | solution.py:264
  22.6 2.7 %collective-permute-start.2 = (f32[2,16,256]{2,1,0:T(8,128)S(1)}, f32[2,16,256]{2,1,0:T(8,128)S(1)}, u32[]{:S(2)}, u32[]{:S(2)}) collective-permute-start(f32[2,16,256]{2,1,0:T(8,128)S(1)} %lead_kernel.1.refs_0_), channel_id=1, source_target_pairs={{0,8},{1,9},{32,40},{33,41},{64,72},{65,73},{96,104},{97,105},{128... | collective-permute-start | bytes 98312 | tf_op jit(solution)/shard_map/ppermute | solution.py:264
  23.9 2.3 %collective-permute-start.1 = (f32[2,16,256]{2,1,0:T(8,128)S(1)}, f32[2,16,256]{2,1,0:T(8,128)S(1)}, u32[]{:S(2)}, u32[]{:S(2)}) collective-permute-start(f32[2,16,256]{2,1,0:T(8,128)S(1)} %lead_kernel.1.refs_0_), channel_id=1, source_target_pairs={{0,24},{1,25},{32,56},{33,57},{64,88},{65,89},{96,120},{97,121},{1... | collective-permute-start | bytes 98312 | tf_op jit(solution)/shard_map/ppermute | solution.py:264
  26.3 7.4 %collective-permute-start.4 = (f32[512,256]{1,0:T(8,128)S(1)}, f32[512,256]{1,0:T(8,128)S(1)}, u32[]{:S(2)}, u32[]{:S(2)}) collective-permute-start(f32[512,256]{1,0:T(8,128)S(1)} %get-tuple-element.25.refs_0_), channel_id=1, source_target_pairs={{0,14},{1,19},{32,46},{33,51},{64,78},{65,83},{96,110},{97,115},{1... | collective-permute-start | bytes 1572872 | tf_op jit(solution)/shard_map/ppermute | solution.py:264
  27.6 6.1 %collective-permute-start.8 = (f32[2,16,256]{2,1,0:T(8,128)S(1)}, f32[2,16,256]{2,1,0:T(8,128)S(1)}, u32[]{:S(2)}, u32[]{:S(2)}) collective-permute-start(f32[2,16,256]{2,1,0:T(8,128)S(1)} %sum_kernel.5.refs_1_.refs_2_), channel_id=1, source_target_pairs={{0,4},{1,5},{8,12},{9,13},{16,20},{17,21},{24,28},{25,29},{32,36},... | collective-permute-start | bytes 98312 | tf_op jit(solution)/shard_map/ppermute | solution.py:264
  28.9 5.1 %collective-permute-start.7 = (f32[2,16,256]{2,1,0:T(8,128)S(1)}, f32[2,16,256]{2,1,0:T(8,128)S(1)}, u32[]{:S(2)}, u32[]{:S(2)}) collective-permute-start(f32[2,16,256]{2,1,0:T(8,128)S(1)} %sum_kernel.5.refs_1_.refs_2_), channel_id=1, source_target_pairs={{0,30},{1,31},{8,6},{9,7},{16,14},{17,15},{24,22},{25,23},{32,62},... | collective-permute-start | bytes 98312 | tf_op jit(solution)/shard_map/ppermute | solution.py:264
  31.5 2.6 %collective-permute-start.6 = (f32[2,16,256]{2,1,0:T(8,128)S(1)}, f32[2,16,256]{2,1,0:T(8,128)S(1)}, u32[]{:S(2)}, u32[]{:S(2)}) collective-permute-start(f32[2,16,256]{2,1,0:T(8,128)S(1)} %sum_kernel.5.refs_1_.refs_2_), channel_id=1, source_target_pairs={{0,2},{1,3},{8,10},{9,11},{16,18},{17,19},{24,26},{25,27},{32,34},... | collective-permute-start | bytes 98312 | tf_op jit(solution)/shard_map/ppermute | solution.py:264
  35.1 18.3 %all-to-all-start.3 = ((f32[16,4,16,256]{3,2,1,0:T(8,128)}), f32[16,4,16,256]{3,2,1,0:T(8,128)S(1)}, u32[]{:S(2)}, u32[]{:S(2)}) async-start(f32[16,4,16,256]{3,2,1,0:T(8,128)} %spread_kernel.1.refs_2_), calls=%async_computation.3 | async-start | bytes 2097152 | tf_op jit(solution)/shard_map/all_to_all | solution.py:287
  38.8 13.2 %collective-permute-start.5 = (f32[512,256]{1,0:T(8,128)S(1)}, f32[512,256]{1,0:T(8,128)S(1)}, u32[]{:S(2)}, u32[]{:S(2)}) collective-permute-start(f32[512,256]{1,0:T(8,128)S(1)} %sum_kernel.6.refs_6_.refs_0_), channel_id=1, source_target_pairs={{0,8},{1,25},{14,22},{19,11},{32,40},{33,57},{46,54},{51,43},{64,7... | collective-permute-start | bytes 1572872 | tf_op jit(solution)/shard_map/ppermute | solution.py:264
  45.9 13.3 %collective-permute-start.10 = (f32[512,256]{1,0:T(8,128)S(1)}, f32[512,256]{1,0:T(8,128)}, u32[]{:S(2)}, u32[]{:S(2)}) collective-permute-start(f32[512,256]{1,0:T(8,128)S(1)} %get-tuple-element.24.refs_0_), channel_id=1, source_target_pairs={{0,1},{1,0},{32,33},{33,32},{64,65},{65,64},{96,97},{97,96},{128,1... | collective-permute-start | bytes 1572872 | tf_op jit(solution)/shard_map/ppermute | solution.py:252
  52.1 15.4 %collective-permute-start.9 = (f32[512,256]{1,0:T(8,128)S(1)}, f32[512,256]{1,0:T(8,128)S(1)}, u32[]{:S(2)}, u32[]{:S(2)}) collective-permute-start(f32[512,256]{1,0:T(8,128)S(1)} %sum_kernel.7.refs_1_.refs_0_), channel_id=1, source_target_pairs={{0,4},{1,29},{8,12},{25,21},{14,18},{19,15},{22,26},{11,7},{32,36}... | collective-permute-start | bytes 1572872 | tf_op jit(solution)/shard_map/ppermute | solution.py:264
  53.5 18.1 %collective-permute-start.12 = (f32[16,16,256]{2,1,0:T(8,128)S(1)}, f32[16,16,256]{2,1,0:T(8,128)S(1)}, u32[]{:S(2)}, u32[]{:S(2)}) collective-permute-start(f32[16,16,256]{2,1,0:T(8,128)S(1)} %pick_kernel.1), channel_id=1, source_target_pairs={{0,1},{1,0},{2,3},{3,2},{4,5},{5,4},{6,7},{7,6},{8,9},{9,8},{10,11... | collective-permute-start | bytes 786440 | tf_op jit(solution)/shard_map/ppermute | solution.py:252
  67.5 13.4 %collective-permute-start.11 = (f32[512,256]{1,0:T(8,128)S(1)}, f32[512,256]{1,0:T(8,128)S(1)}, u32[]{:S(2)}, u32[]{:S(2)}) collective-permute-start(f32[512,256]{1,0:T(8,128)S(1)} %sum_kernel.8.refs_3_.refs_0_), channel_id=1, source_target_pairs={{0,30},{1,3},{4,2},{29,31},{8,6},{25,27},{12,10},{21,23},{14,16},{... | collective-permute-start | bytes 1572872 | tf_op jit(solution)/shard_map/ppermute | solution.py:264
  81.0 1.9 %collective-permute-start.13 = (f32[512,256]{1,0:T(8,128)S(1)}, f32[512,256]{1,0:T(8,128)S(1)}, u32[]{:S(2)}, u32[]{:S(2)}) collective-permute-start(f32[512,256]{1,0:T(8,128)S(1)} %sum_kernel.9.refs_4_.refs_1_), channel_id=1, source_target_pairs={{2,3},{3,2},{4,5},{5,4},{6,7},{7,6},{8,9},{9,8},{10,11},{11,10},{1... | collective-permute-start | bytes 1572872 | tf_op jit(solution)/shard_map/ppermute | solution.py:252

commit v5 on v4

--- a/solution.py
+++ b/solution.py
@@ -100,7 +100,7 @@
         high = low + BASE
         small = small_inverse(work[low:high, tile : tile + LANES], off)
         block = small[:, off : off + BASE]
-        strip = product(block, work[low:high, :], 1, 0)
+        strip = product3(block, work[low:high, :], 1, 0)
         lane = lax.broadcasted_iota(jnp.int32, (BASE, LANES), 1)
         own = jnp.where((lane >= off) & (lane < off + BASE), small, strip[:, tile : tile + LANES])
         strip = jnp.concatenate(
@@ -109,11 +109,11 @@
         out_ref[low:high, :] = strip
         for first, last in ((high, high + BASE), (high + BASE, NB)):
             if first < last <= NB:
-                left = product(work[first:last, low:high], block, 1, 1)
+                left = product3(work[first:last, low:high], block, 1, 1)
                 old = work[first:last, :]
                 lanes = lax.broadcasted_iota(jnp.int32, old.shape, 1)
                 old = jnp.where((lanes >= low) & (lanes < high), 0.0, old)
-                work[first:last, :] = old - product(left, strip, 1, 0)
+                work[first:last, :] = old - product3(left, strip, 1, 0)
     rows = lax.broadcasted_iota(jnp.int32, (NB, NB), 0)
     cols = lax.broadcasted_iota(jnp.int32, (NB, NB), 1)
     out_ref[...] = jnp.where(rows >= cols, out_ref[...], 0.0)
@@ -123,14 +123,18 @@
     inverse_factor(lead_ref[:, 0].reshape(NB, NB), inv_ref, work)
 
 
-def second_kernel(inv0_ref, lead_ref, swapped_ref, turned_ref, inv_ref, work):
+def second_kernel(inv0_ref, lead_ref, swapped_ref, turned_ref, right_ref, below_ref, inv_ref, work):
     core0 = lax.rem(lax.axis_index("col"), 2) == 0
     mine = lead_ref[:, 1].reshape(NB, NB)
     swapped = swapped_ref[...].reshape(NB, NB)
-    turned = product(inv0_ref[...], jnp.where(core0, mine, swapped), 1, 1)
+    inv0 = inv0_ref[...]
+    turned = product3(inv0, jnp.where(core0, mine, swapped), 1, 1)
     turned_ref[...] = turned
-    square = jnp.where(core0, swapped, mine)
-    inverse_factor(square - product(turned, turned, 0, 0), inv_ref, work)
+    square = jnp.where(core0, swapped, mine) - product3(turned, turned, 0, 0)
+    right = product3(inv0, lead_ref[:, 2].reshape(NB, NB), 1, 0)
+    right_ref[...] = right
+    below_ref[...] = lead_ref[:, 3].reshape(NB, NB) - product3(turned, right, 0, 0)
+    inverse_factor(square, inv_ref, work)
 
 
 def lead_kernel(first_ref, passed_ref, lead_ref):
@@ -163,7 +167,7 @@
         out_ref[target, 2:] = pieces
 
 
-def factors_kernel(cols_ref, inv0_ref, turned_ref, inv1_ref, x0_ref, x1_ref):
+def factors_kernel(right_ref, below_ref, inv0_ref, turned_ref, inv1_ref, x0_ref, x1_ref):
     col = lax.axis_index("col")
     inv0 = inv0_ref[...]
     turned = turned_ref[...]
@@ -171,11 +175,9 @@
 
     @pl.when(col >= 2)
     def _():
-        right0 = product3(inv0, cols_ref[:, 2].reshape(NB, NB), 1, 0)
-        below = cols_ref[:, 3].reshape(NB, NB) - product3(turned, right0, 0, 0)
-        x1 = product3(inv1, product3(inv1, below, 1, 0), 0, 0)
+        x1 = product3(inv1, product3(inv1, below_ref[...], 1, 0), 0, 0)
         x1_ref[...] = x1
-        x0_ref[...] = product3(inv0, right0 - product3(turned, x1, 1, 0), 0, 0)
+        x0_ref[...] = product3(inv0, right_ref[...] - product3(turned, x1, 1, 0), 0, 0)
 
     @pl.when(col == 0)
     def _():
@@ -289,12 +291,12 @@
     swapped = swap_cores(call(pick_kernel, (16, 16, NB), lead, order=(panel,)), range(CHIPS_Z))
     inv0 = call(first_kernel, square, lead, order=(panel, other0), work=True, flops=ten_us)
     panel = call(sum_kernel, kernel.shape, panel, along_z(panel, PANEL_TREE[2], True), order=(inv0,))
-    turned, inv1 = call(
-        second_kernel, (square, square), inv0, lead, swapped, order=(panel,), work=True, flops=ten_us
+    turned, right, below, inv1 = call(
+        second_kernel, (square,) * 4, inv0, lead, swapped, order=(panel,), work=True, flops=ten_us
     )
     panel = call(sum_kernel, kernel.shape, panel, along_z(panel, PANEL_TREE[3], True), order=(inv1,))
     other = swap_cores(panel, range(1, CHIPS_Z))
-    x0, x1 = call(factors_kernel, (square, square), lead, inv0, turned, inv1, order=(panel,))
+    x0, x1 = call(factors_kernel, (square, square), right, below, inv0, turned, inv1, order=(panel,))
     return call(final_kernel, kernel.shape, mine, panel, other, x0, x1, far=(other0,))
 
 

time: 86.6 us -> 84.8 us (0.979)
  Pallas kernels: 23.1 us -> 21.4 us
    pallas_call x13, Pallas kernels: 23.1 us -> 21.4 us  [call(): pl.pallas_call(whole, out_shape=outs, in_specs=[pl.BlockSpec(memory_space...]
where the time goes in v5:
time: 84.8 us; the launch traced here: 84.3 us
  starting transfers between devices  38.5 us (45%)
  Pallas kernels  21.4 us (25%)
  blocking collectives  14.9 us (18%)
  waiting for transfers between devices  7.99 us (9%)
  local copies, waits for them, and re-layouts  0.98 us (1%)
    ppermute x10, starting transfers between devices, along_z(): return lax.ppermute(value, 'col', both_cores(pairs, mirror))  22.9 us
    pallas_call x13, Pallas kernels, call(): pl.pallas_call(whole, out_shape=outs, in_specs=[pl.BlockSpec(memory_space...  21.4 us
    all_to_all x1, blocking collectives, scatter_rows(): return lax.all_to_all(top.reshape(16, 16, NB), 'row', 0, 0)[:2]  14.9 us
    ppermute x3, starting transfers between devices, swap_cores(): lax.ppermute(value, 'col', [(2 * z + c, 2 * z + 1 - c) for z in chips for...  10.6 us
    ppermute x10, waiting for transfers between devices, along_z(): return lax.ppermute(value, 'col', both_cores(pairs, mirror))  4.04 us
    ppermute x1, waiting for transfers between devices, local(): lax.ppermute(first[0], 'col', [(0, 1)])  3.89 us
    all_to_all x1, starting transfers between devices, local(): lead = lax.all_to_all(spread, 'row', 0, 0)  3.65 us
  transfers between devices with their start and end apart: 15, of which 5 were waited for; matrix products, arithmetic and copies ran while one was open for 0% of the time, Pallas kernels for 22%

profile of v5, /device:TPU:1, one launch (start us, length us, event | category | flops | bytes accessed | tf_op | source)
XLA Modules:
  0.0 84.3 jit_solution(6067326526260369957)
XLA Ops:
  0.0 1.0 %slice.24 = f32[256,256]{1,0:T(8,128)S(1)} slice(f32[512,256]{1,0:T(8,128)} %refs_0_.1), slice={[0:256], [0:256]} | slice | bytes 524288 | tf_op jit(solution)/shard_map/slice | solution.py:271
  1.0 15.0 %conditional.3 = (f32[2,16,256]{2,1,0:T(8,128)S(1)}) conditional(s32[]{:T(128)} %convert_element_type.9, () %tuple.23, f32[256,256]{1,0:T(8,128)S(1)} %slice.24), branch_computations={%region_0.1_spmd, %region_1.2_spmd} | conditional | bytes 589832 | solution.py:276
  1.0 14.9 %all_to_all.17 = f32[16,16,256]{2,1,0:T(8,128)S(1)} all-to-all(f32[16,16,256]{2,1,0:T(8,128)S(1)} %bitcast.5), channel_id=1, replica_groups=mesh['row'=16,'col'=32] {'row'}, dimensions={0} | all-to-all | bytes 524288 | tf_op jit(solution)/shard_map/cond/branch_1_fun/all_to_all | solution.py:258
  15.9 1.4 %collective-permute-start = (f32[16,256]{1,0:T(8,128)S(1)}, f32[16,256]{1,0:T(8,128)S(1)}, u32[]{:S(2)}, u32[]{:S(2)}) collective-permute-start(f32[16,256]{1,0:T(8,128)S(1)} %slice_bitcast_fusion), channel_id=1, source_target_pairs={{0,1},{32,33},{64,65},{96,97},{128,129},{160,161},{192,193},{224,2... | collective-permute-start | bytes 49160 | tf_op jit(solution)/shard_map/ppermute | solution.py:277
  17.4 3.9 %collective-permute-done.refs_1_ = f32[16,256]{1,0:T(8,128)S(1)} collective-permute-done((f32[16,256]{1,0:T(8,128)S(1)}, f32[16,256]{1,0:T(8,128)S(1)}, u32[]{:S(2)}, u32[]{:S(2)}) %collective-permute-start) | collective-permute-done | bytes 16416 | tf_op jit(solution)/shard_map/ppermute | solution.py:277
  21.3 1.3 %collective-permute-start.3 = (f32[2,16,256]{2,1,0:T(8,128)S(1)}, f32[2,16,256]{2,1,0:T(8,128)S(1)}, u32[]{:S(2)}, u32[]{:S(2)}) collective-permute-start(f32[2,16,256]{2,1,0:T(8,128)S(1)} %lead_kernel.1.refs_0_), channel_id=1, source_target_pairs={{0,16},{1,17},{32,48},{33,49},{64,80},{65,81},{96,112},{97,113},{1... | collective-permute-start | bytes 98312 | tf_op jit(solution)/shard_map/ppermute | solution.py:266
  22.6 1.3 %collective-permute-start.2 = (f32[2,16,256]{2,1,0:T(8,128)S(1)}, f32[2,16,256]{2,1,0:T(8,128)S(1)}, u32[]{:S(2)}, u32[]{:S(2)}) collective-permute-start(f32[2,16,256]{2,1,0:T(8,128)S(1)} %lead_kernel.1.refs_0_), channel_id=1, source_target_pairs={{0,8},{1,9},{32,40},{33,41},{64,72},{65,73},{96,104},{97,105},{128... | collective-permute-start | bytes 98312 | tf_op jit(solution)/shard_map/ppermute | solution.py:266
  23.9 1.3 %collective-permute-start.1 = (f32[2,16,256]{2,1,0:T(8,128)S(1)}, f32[2,16,256]{2,1,0:T(8,128)S(1)}, u32[]{:S(2)}, u32[]{:S(2)}) collective-permute-start(f32[2,16,256]{2,1,0:T(8,128)S(1)} %lead_kernel.1.refs_0_), channel_id=1, source_target_pairs={{0,24},{1,25},{32,56},{33,57},{64,88},{65,89},{96,120},{97,121},{1... | collective-permute-start | bytes 98312 | tf_op jit(solution)/shard_map/ppermute | solution.py:266
  25.2 0.9 %collective-permute-done.1.refs_1_ = f32[2,16,256]{2,1,0:T(8,128)S(1)} collective-permute-done((f32[2,16,256]{2,1,0:T(8,128)S(1)}, f32[2,16,256]{2,1,0:T(8,128)S(1)}, u32[]{:S(2)}, u32[]{:S(2)}) %collective-permute-start.1) | collective-permute-done | bytes 32800 | tf_op jit(solution)/shard_map/ppermute | solution.py:266
  26.2 0.1 panel_kernel.1
  26.3 1.3 %collective-permute-start.4 = (f32[512,256]{1,0:T(8,128)S(1)}, f32[512,256]{1,0:T(8,128)S(1)}, u32[]{:S(2)}, u32[]{:S(2)}) collective-permute-start(f32[512,256]{1,0:T(8,128)S(1)} %get-tuple-element.27.refs_0_), channel_id=1, source_target_pairs={{0,14},{1,19},{32,46},{33,51},{64,78},{65,83},{96,110},{97,115},{1... | collective-permute-start | bytes 1572872 | tf_op jit(solution)/shard_map/ppermute | solution.py:266
  27.6 1.3 %collective-permute-start.8 = (f32[2,16,256]{2,1,0:T(8,128)S(1)}, f32[2,16,256]{2,1,0:T(8,128)S(1)}, u32[]{:S(2)}, u32[]{:S(2)}) collective-permute-start(f32[2,16,256]{2,1,0:T(8,128)S(1)} %sum_kernel.5.refs_1_.refs_2_), channel_id=1, source_target_pairs={{0,4},{1,5},{8,12},{9,13},{16,20},{17,21},{24,28},{25,29},{32,36},... | collective-permute-start | bytes 98312 | tf_op jit(solution)/shard_map/ppermute | solution.py:266
  28.9 2.6 %collective-permute-start.7 = (f32[2,16,256]{2,1,0:T(8,128)S(1)}, f32[2,16,256]{2,1,0:T(8,128)S(1)}, u32[]{:S(2)}, u32[]{:S(2)}) collective-permute-start(f32[2,16,256]{2,1,0:T(8,128)S(1)} %sum_kernel.5.refs_1_.refs_2_), channel_id=1, source_target_pairs={{0,30},{1,31},{8,6},{9,7},{16,14},{17,15},{24,22},{25,23},{32,62},... | collective-permute-start | bytes 98312 | tf_op jit(solution)/shard_map/ppermute | solution.py:266
  31.5 1.3 %collective-permute-start.6 = (f32[2,16,256]{2,1,0:T(8,128)S(1)}, f32[2,16,256]{2,1,0:T(8,128)S(1)}, u32[]{:S(2)}, u32[]{:S(2)}) collective-permute-start(f32[2,16,256]{2,1,0:T(8,128)S(1)} %sum_kernel.5.refs_1_.refs_2_), channel_id=1, source_target_pairs={{0,2},{1,3},{8,10},{9,11},{16,18},{17,19},{24,26},{25,27},{32,34},... | collective-permute-start | bytes 98312 | tf_op jit(solution)/shard_map/ppermute | solution.py:266
  32.8 0.9 %collective-permute-done.4.refs_1_ = f32[512,256]{1,0:T(8,128)S(1)} collective-permute-done((f32[512,256]{1,0:T(8,128)S(1)}, f32[512,256]{1,0:T(8,128)S(1)}, u32[]{:S(2)}, u32[]{:S(2)}) %collective-permute-start.4) | collective-permute-done | bytes 524320 | tf_op jit(solution)/shard_map/ppermute | solution.py:266
  33.7 0.1 sum_kernel.6.refs_6_.refs_0_
  33.7 0.3 collective-permute-done.7.refs_4_
  34.0 1.1 %spread_kernel.1.refs_2_ = f32[16,4,16,256]{3,2,1,0:T(8,128)} custom-call(f32[2,16,256]{2,1,0:T(8,128)S(1)} %get-tuple-element.35.refs_4_.refs_0_, f32[2,16,256]{2,1,0:T(8,128)S(1)} %get-tuple-element.36.refs_1_, f32[2,16,256]{2,1,0:T(8,128)S(1)} %sum_kernel.5.refs_1_.refs_2_, f32[2,16,256]{2,1,0:T(8,128)S(1)} %collective-permute-done.6.refs_3_, ...), custom_call_target="tpu_custom_call" | custom-call | tf_op jit(solution)/shard_map/spread_kernel/pallas_call | solution.py:232
  35.1 3.7 %all-to-all-start.3 = ((f32[16,4,16,256]{3,2,1,0:T(8,128)}), f32[16,4,16,256]{3,2,1,0:T(8,128)S(1)}, u32[]{:S(2)}, u32[]{:S(2)}) async-start(f32[16,4,16,256]{3,2,1,0:T(8,128)} %spread_kernel.1.refs_2_), calls=%async_computation.3 | async-start | bytes 2097152 | tf_op jit(solution)/shard_map/all_to_all | solution.py:289
  38.8 7.1 %collective-permute-start.5 = (f32[512,256]{1,0:T(8,128)S(1)}, f32[512,256]{1,0:T(8,128)S(1)}, u32[]{:S(2)}, u32[]{:S(2)}) collective-permute-start(f32[512,256]{1,0:T(8,128)S(1)} %sum_kernel.6.refs_6_.refs_0_), channel_id=1, source_target_pairs={{0,8},{1,25},{14,22},{19,11},{32,40},{33,57},{46,54},{51,43},{64,7... | collective-permute-start | bytes 1572872 | tf_op jit(solution)/shard_map/ppermute | solution.py:266
  45.9 4.2 %collective-permute-start.10 = (f32[512,256]{1,0:T(8,128)S(1)}, f32[512,256]{1,0:T(8,128)S(1)}, u32[]{:S(2)}, u32[]{:S(2)}) collective-permute-start(f32[512,256]{1,0:T(8,128)S(1)} %get-tuple-element.26.refs_0_), channel_id=1, source_target_pairs={{0,1},{1,0},{32,33},{33,32},{64,65},{65,64},{96,97},{97,96},{128,1... | collective-permute-start | bytes 1572872 | tf_op jit(solution)/shard_map/ppermute | solution.py:254
  50.1 1.9 %collective-permute-done.5.refs_1_ = f32[512,256]{1,0:T(8,128)S(1)} collective-permute-done((f32[512,256]{1,0:T(8,128)S(1)}, f32[512,256]{1,0:T(8,128)S(1)}, u32[]{:S(2)}, u32[]{:S(2)}) %collective-permute-start.5) | collective-permute-done | bytes 524320 | tf_op jit(solution)/shard_map/ppermute | solution.py:266
  52.1 1.3 %collective-permute-start.9 = (f32[512,256]{1,0:T(8,128)S(1)}, f32[512,256]{1,0:T(8,128)S(1)}, u32[]{:S(2)}, u32[]{:S(2)}) collective-permute-start(f32[512,256]{1,0:T(8,128)S(1)} %sum_kernel.7.refs_1_.refs_0_), channel_id=1, source_target_pairs={{0,4},{1,29},{8,12},{25,21},{14,18},{19,15},{22,26},{11,7},{32,36}... | collective-permute-start | bytes 1572872 | tf_op jit(solution)/shard_map/ppermute | solution.py:266
  53.5 5.7 %collective-permute-start.12 = (f32[16,16,256]{2,1,0:T(8,128)S(1)}, f32[16,16,256]{2,1,0:T(8,128)S(1)}, u32[]{:S(2)}, u32[]{:S(2)}) collective-permute-start(f32[16,16,256]{2,1,0:T(8,128)S(1)} %pick_kernel.1), channel_id=1, source_target_pairs={{0,1},{1,0},{2,3},{3,2},{4,5},{5,4},{6,7},{7,6},{8,9},{9,8},{10,11... | collective-permute-start | bytes 786440 | tf_op jit(solution)/shard_map/ppermute | solution.py:254
  59.2 8.0 %first_kernel.1.refs_2_.refs_0_ = f32[256,256]{1,0:T(8,128)S(1)} custom-call(f32[16,4,16,256]{3,2,1,0:T(8,128)S(1)} %all-to-all-done.3.refs_0_.refs_1_, f32[512,256]{1,0:T(8,128)S(1)} %sum_kernel.7.refs_1_.refs_0_, f32[512,256]{1,0:T(8,128)S(1)} %collective-permute-done.10.refs_2_.refs_5_), custom_call_target="tpu_custom_call" | custom-call | flops 10000000000 | tf_op jit(solution)/shard_map/first_kernel/pallas_call | solution.py:232
  67.3 0.1 sum_kernel.8.refs_3_.refs_0_
  67.3 4.1 %collective-permute-start.11 = (f32[512,256]{1,0:T(8,128)S(1)}, f32[512,256]{1,0:T(8,128)S(1)}, u32[]{:S(2)}, u32[]{:S(2)}) collective-permute-start(f32[512,256]{1,0:T(8,128)S(1)} %sum_kernel.8.refs_3_.refs_0_), channel_id=1, source_target_pairs={{0,30},{1,3},{4,2},{29,31},{8,6},{25,27},{12,10},{21,23},{14,16},{... | collective-permute-start | bytes 1572872 | tf_op jit(solution)/shard_map/ppermute | solution.py:266
  71.4 8.8 %second_kernel.1 = (f32[256,256]{1,0:T(8,128)S(1)}, f32[256,256]{1,0:T(8,128)S(1)}, f32[256,256]{1,0:T(8,128)S(1)}, f32[256,256]{1,0:T(8,128)S(1)}) custom-call(f32[256,256]{1,0:T(8,128)S(1)} %first_kernel.1.refs_2_.refs_0_, f32[16,4,16,256]{3,2,1,0:T(8,128)S(1)} %all-to-all-done.3.refs_0_.refs_1_, f32[16,16,256]{2,1,0:T(8,128)S(1)} %collective-permute-done.12.refs_2_, ...), custom_call_target="tpu_custom_call" | custom-call | flops 10000000000 | tf_op jit(solution)/shard_map/second_kernel/pallas_call | solution.py:232
  80.3 0.1 sum_kernel.9.refs_5_.refs_1_
  80.3 0.7 collective-permute-start.13
  81.0 1.2 %factors_kernel.1 = (f32[256,256]{1,0:T(8,128)S(1)}, f32[256,256]{1,0:T(8,128)S(1)}) custom-call(f32[256,256]{1,0:T(8,128)S(1)} %get-tuple-element.29.refs_0_, f32[256,256]{1,0:T(8,128)S(1)} %get-tuple-element.30.refs_1_, f32[256,256]{1,0:T(8,128)S(1)} %first_kernel.1.refs_2_.refs_0_, f32[256,256]{1,0:T(8,128)S(1)} %get-tuple-element.31.refs_3_, ...), custom_call_target="tpu_custom_call" | custom-call | tf_op jit(solution)/shard_map/factors_kernel/pallas_call | solution.py:232
  82.2 2.0 %final_kernel.1 = f32[512,256]{1,0:T(8,128)} custom-call(f32[512,256]{1,0:T(8,128)S(1)} %get-tuple-element.26.refs_0_, f32[512,256]{1,0:T(8,128)S(1)} %sum_kernel.9.refs_5_.refs_1_, f32[512,256]{1,0:T(8,128)S(1)} %collective-permute-done.13.refs_2_, f32[256,256]{1,0:T(8,128)S(1)} %get-tuple-element.32.refs_3_, f32[256,256]{1,0:T(8,128)S(1)} %get-tuple-element.33.refs_4_, ...), custom_call_target="tpu_custom_call" | custom-call | tf_op jit(solution)/shard_map/final_kernel/pallas_call | solution.py:232
  (22 shorter events, 0.3 us)
Async XLA Ops:
  15.9 10.2 %copy-start = (f32[512,256]{1,0:T(8,128)S(1)}, f32[512,256]{1,0:T(8,128)}, u32[]{:S(2)}) copy-start(f32[512,256]{1,0:T(8,128)} %refs_0_.1) | copy-start | bytes 1572868
  15.9 5.3 %collective-permute-start = (f32[16,256]{1,0:T(8,128)S(1)}, f32[16,256]{1,0:T(8,128)S(1)}, u32[]{:S(2)}, u32[]{:S(2)}) collective-permute-start(f32[16,256]{1,0:T(8,128)S(1)} %slice_bitcast_fusion), channel_id=1, source_target_pairs={{0,1},{32,33},{64,65},{96,97},{128,129},{160,161},{192,193},{224,2... | collective-permute-start | bytes 49160 | tf_op jit(solution)/shard_map/ppermute | solution.py:277
  21.3 3.9 %collective-permute-start.3 = (f32[2,16,256]{2,1,0:T(8,128)S(1)}, f32[2,16,256]{2,1,0:T(8,128)S(1)}, u32[]{:S(2)}, u32[]{:S(2)}) collective-permute-start(f32[2,16,256]{2,1,0:T(8,128)S(1)} %lead_kernel.1.refs_0_), channel_id=1, source_target_pairs={{0,16},{1,17},{32,48},{33,49},{64,80},{65,81},{96,112},{97,113},{1... | collective-permute-start | bytes 98312 | tf_op jit(solution)/shard_map/ppermute | solution.py:266
  22.6 2.7 %collective-permute-start.2 = (f32[2,16,256]{2,1,0:T(8,128)S(1)}, f32[2,16,256]{2,1,0:T(8,128)S(1)}, u32[]{:S(2)}, u32[]{:S(2)}) collective-permute-start(f32[2,16,256]{2,1,0:T(8,128)S(1)} %lead_kernel.1.refs_0_), channel_id=1, source_target_pairs={{0,8},{1,9},{32,40},{33,41},{64,72},{65,73},{96,104},{97,105},{128... | collective-permute-start | bytes 98312 | tf_op jit(solution)/shard_map/ppermute | solution.py:266
  23.9 2.3 %collective-permute-start.1 = (f32[2,16,256]{2,1,0:T(8,128)S(1)}, f32[2,16,256]{2,1,0:T(8,128)S(1)}, u32[]{:S(2)}, u32[]{:S(2)}) collective-permute-start(f32[2,16,256]{2,1,0:T(8,128)S(1)} %lead_kernel.1.refs_0_), channel_id=1, source_target_pairs={{0,24},{1,25},{32,56},{33,57},{64,88},{65,89},{96,120},{97,121},{1... | collective-permute-start | bytes 98312 | tf_op jit(solution)/shard_map/ppermute | solution.py:266
  26.3 7.4 %collective-permute-start.4 = (f32[512,256]{1,0:T(8,128)S(1)}, f32[512,256]{1,0:T(8,128)S(1)}, u32[]{:S(2)}, u32[]{:S(2)}) collective-permute-start(f32[512,256]{1,0:T(8,128)S(1)} %get-tuple-element.27.refs_0_), channel_id=1, source_target_pairs={{0,14},{1,19},{32,46},{33,51},{64,78},{65,83},{96,110},{97,115},{1... | collective-permute-start | bytes 1572872 | tf_op jit(solution)/shard_map/ppermute | solution.py:266
  27.6 6.1 %collective-permute-start.8 = (f32[2,16,256]{2,1,0:T(8,128)S(1)}, f32[2,16,256]{2,1,0:T(8,128)S(1)}, u32[]{:S(2)}, u32[]{:S(2)}) collective-permute-start(f32[2,16,256]{2,1,0:T(8,128)S(1)} %sum_kernel.5.refs_1_.refs_2_), channel_id=1, source_target_pairs={{0,4},{1,5},{8,12},{9,13},{16,20},{17,21},{24,28},{25,29},{32,36},... | collective-permute-start | bytes 98312 | tf_op jit(solution)/shard_map/ppermute | solution.py:266
  28.9 5.1 %collective-permute-start.7 = (f32[2,16,256]{2,1,0:T(8,128)S(1)}, f32[2,16,256]{2,1,0:T(8,128)S(1)}, u32[]{:S(2)}, u32[]{:S(2)}) collective-permute-start(f32[2,16,256]{2,1,0:T(8,128)S(1)} %sum_kernel.5.refs_1_.refs_2_), channel_id=1, source_target_pairs={{0,30},{1,31},{8,6},{9,7},{16,14},{17,15},{24,22},{25,23},{32,62},... | collective-permute-start | bytes 98312 | tf_op jit(solution)/shard_map/ppermute | solution.py:266
  31.5 2.6 %collective-permute-start.6 = (f32[2,16,256]{2,1,0:T(8,128)S(1)}, f32[2,16,256]{2,1,0:T(8,128)S(1)}, u32[]{:S(2)}, u32[]{:S(2)}) collective-permute-start(f32[2,16,256]{2,1,0:T(8,128)S(1)} %sum_kernel.5.refs_1_.refs_2_), channel_id=1, source_target_pairs={{0,2},{1,3},{8,10},{9,11},{16,18},{17,19},{24,26},{25,27},{32,34},... | collective-permute-start | bytes 98312 | tf_op jit(solution)/shard_map/ppermute | solution.py:266
  35.1 18.3 %all-to-all-start.3 = ((f32[16,4,16,256]{3,2,1,0:T(8,128)}), f32[16,4,16,256]{3,2,1,0:T(8,128)S(1)}, u32[]{:S(2)}, u32[]{:S(2)}) async-start(f32[16,4,16,256]{3,2,1,0:T(8,128)} %spread_kernel.1.refs_2_), calls=%async_computation.3 | async-start | bytes 2097152 | tf_op jit(solution)/shard_map/all_to_all | solution.py:289
  38.8 13.2 %collective-permute-start.5 = (f32[512,256]{1,0:T(8,128)S(1)}, f32[512,256]{1,0:T(8,128)S(1)}, u32[]{:S(2)}, u32[]{:S(2)}) collective-permute-start(f32[512,256]{1,0:T(8,128)S(1)} %sum_kernel.6.refs_6_.refs_0_), channel_id=1, source_target_pairs={{0,8},{1,25},{14,22},{19,11},{32,40},{33,57},{46,54},{51,43},{64,7... | collective-permute-start | bytes 1572872 | tf_op jit(solution)/shard_map/ppermute | solution.py:266
  45.9 13.3 %collective-permute-start.10 = (f32[512,256]{1,0:T(8,128)S(1)}, f32[512,256]{1,0:T(8,128)S(1)}, u32[]{:S(2)}, u32[]{:S(2)}) collective-permute-start(f32[512,256]{1,0:T(8,128)S(1)} %get-tuple-element.26.refs_0_), channel_id=1, source_target_pairs={{0,1},{1,0},{32,33},{33,32},{64,65},{65,64},{96,97},{97,96},{128,1... | collective-permute-start | bytes 1572872 | tf_op jit(solution)/shard_map/ppermute | solution.py:254
  52.1 15.2 %collective-permute-start.9 = (f32[512,256]{1,0:T(8,128)S(1)}, f32[512,256]{1,0:T(8,128)S(1)}, u32[]{:S(2)}, u32[]{:S(2)}) collective-permute-start(f32[512,256]{1,0:T(8,128)S(1)} %sum_kernel.7.refs_1_.refs_0_), channel_id=1, source_target_pairs={{0,4},{1,29},{8,12},{25,21},{14,18},{19,15},{22,26},{11,7},{32,36}... | collective-permute-start | bytes 1572872 | tf_op jit(solution)/shard_map/ppermute | solution.py:266
  53.5 17.9 %collective-permute-start.12 = (f32[16,16,256]{2,1,0:T(8,128)S(1)}, f32[16,16,256]{2,1,0:T(8,128)S(1)}, u32[]{:S(2)}, u32[]{:S(2)}) collective-permute-start(f32[16,16,256]{2,1,0:T(8,128)S(1)} %pick_kernel.1), channel_id=1, source_target_pairs={{0,1},{1,0},{2,3},{3,2},{4,5},{5,4},{6,7},{7,6},{8,9},{9,8},{10,11... | collective-permute-start | bytes 786440 | tf_op jit(solution)/shard_map/ppermute | solution.py:254
  67.3 12.9 %collective-permute-start.11 = (f32[512,256]{1,0:T(8,128)S(1)}, f32[512,256]{1,0:T(8,128)S(1)}, u32[]{:S(2)}, u32[]{:S(2)}) collective-permute-start(f32[512,256]{1,0:T(8,128)S(1)} %sum_kernel.8.refs_3_.refs_0_), channel_id=1, source_target_pairs={{0,30},{1,3},{4,2},{29,31},{8,6},{25,27},{12,10},{21,23},{14,16},{... | collective-permute-start | bytes 1572872 | tf_op jit(solution)/shard_map/ppermute | solution.py:266
  80.3 1.9 %collective-permute-start.13 = (f32[512,256]{1,0:T(8,128)S(1)}, f32[512,256]{1,0:T(8,128)S(1)}, u32[]{:S(2)}, u32[]{:S(2)}) collective-permute-start(f32[512,256]{1,0:T(8,128)S(1)} %sum_kernel.9.refs_5_.refs_1_), channel_id=1, source_target_pairs={{2,3},{3,2},{4,5},{5,4},{6,7},{7,6},{8,9},{9,8},{10,11},{11,10},{1... | collective-permute-start | bytes 1572872 | tf_op jit(solution)/shard_map/ppermute | solution.py:254

commit v6 on v5

--- a/solution.py
+++ b/solution.py
@@ -9,7 +9,6 @@
 BASE = 32
 LANES = 128
 SUBS = 8
-HIGHEST = lax.Precision.HIGHEST
 VMEM_LIMIT = 6 * 1024 * 1024
 
 CHIPS_Z = 16
@@ -27,16 +26,6 @@
         tuple((s, s + 2) for s in (0, 4, 8, 12)),
     ),
 )
-
-
-def product(a, b, a_dim, b_dim):
-    return lax.dot_general(
-        a,
-        b,
-        (((a_dim,), (b_dim,)), ((), ())),
-        precision=HIGHEST,
-        preferred_element_type=jnp.float32,
-    )
 
 
 def split(a):
@@ -186,7 +175,7 @@
 
     @pl.when(col == 1)
     def _():
-        x0_ref[...] = product(inv0, product(turned, inv1, 1, 1), 0, 0)
+        x0_ref[...] = product3(inv0, product3(turned, inv1, 1, 1), 0, 0)
         x1_ref[...] = -inv1.T
 
 
@@ -201,20 +190,21 @@
     def _():
         for block in range(2):
             place = pl.ds(block * NB, NB)
-            taken = product(own_ref[place, :], x_own, 1, 0) + product(other_ref[place, :], x_other, 1, 0)
+            taken = product3(own_ref[place, :], x_own, 1, 0) + product3(other_ref[place, :], x_other, 1, 0)
             out_ref[place, :] = jnp.where(row + 16 * block >= 2, mine_ref[place, :] - taken, 0.0)
 
     @pl.when(col < 2)
     def _():
         copy = pltpu.make_async_copy(other0_ref, held, sem)
         copy.start()
+        first = product3(own_ref[...], x_own, 1, 0)
+        lower = lax.broadcasted_iota(jnp.int32, (NB, NB), 0) >= lax.broadcasted_iota(jnp.int32, (NB, NB), 1)
         copy.wait()
-        lower = lax.broadcasted_iota(jnp.int32, (NB, NB), 0) >= lax.broadcasted_iota(jnp.int32, (NB, NB), 1)
+        taken = first + product3(held[...], x_other, 1, 0)
         for block in range(2):
-            place = pl.ds(block * NB, NB)
+            place = slice(block * NB, block * NB + NB)
             label = row + 16 * block
-            taken = product(own_ref[place, :], x_own, 1, 0) + product(held[place, :], x_other, 1, 0)
-            out_ref[place, :] = jnp.where((label > col) | ((label == col) & lower), -taken, 0.0)
+            out_ref[place, :] = jnp.where((label > col) | ((label == col) & lower), -taken[place, :], 0.0)
 
 
 def call(body, out, *operands, far=(), order=(), work=False, flops=0):

time: 84.8 us -> 84.5 us (level)
  transfers between devices with their start and end apart: 15 -> 15, of which waited for: 5 -> 5; matrix products, arithmetic and copies ran while one was open for 0% -> 0% of each run, Pallas kernels for 22% -> 21%
where the time goes in v6:
time: 84.5 us; the launch traced here: 84 us
  starting transfers between devices  38.5 us (46%)
  Pallas kernels  21.1 us (25%)
  blocking collectives  14.9 us (18%)
  waiting for transfers between devices  7.99 us (9%)
  local copies, waits for them, and re-layouts  0.98 us (1%)
    ppermute x10, starting transfers between devices, along_z(): return lax.ppermute(value, 'col', both_cores(pairs, mirror))  22.9 us
    pallas_call x13, Pallas kernels, call(): pl.pallas_call(whole, out_shape=outs, in_specs=[pl.BlockSpec(memory_space...  21.1 us
    all_to_all x1, blocking collectives, scatter_rows(): return lax.all_to_all(top.reshape(16, 16, NB), 'row', 0, 0)[:2]  14.9 us
    ppermute x3, starting transfers between devices, swap_cores(): lax.ppermute(value, 'col', [(2 * z + c, 2 * z + 1 - c) for z in chips for...  10.6 us
    ppermute x10, waiting for transfers between devices, along_z(): return lax.ppermute(value, 'col', both_cores(pairs, mirror))  4.04 us
    ppermute x1, waiting for transfers between devices, local(): lax.ppermute(first[0], 'col', [(0, 1)])  3.89 us
    all_to_all x1, starting transfers between devices, local(): lead = lax.all_to_all(spread, 'row', 0, 0)  3.65 us
  transfers between devices with their start and end apart: 15, of which 5 were waited for; matrix products, arithmetic and copies ran while one was open for 0% of the time, Pallas kernels for 21%

profile of v6, /device:TPU:1, one launch (start us, length us, event | category | flops | bytes accessed | tf_op | source)
XLA Modules:
  0.0 84.0 jit_solution(5769787186672963105)
XLA Ops:
  0.0 1.0 %slice.24 = f32[256,256]{1,0:T(8,128)S(1)} slice(f32[512,256]{1,0:T(8,128)} %refs_0_.1), slice={[0:256], [0:256]} | slice | bytes 524288 | tf_op jit(solution)/shard_map/slice | solution.py:261
  1.0 15.0 %conditional.3 = (f32[2,16,256]{2,1,0:T(8,128)S(1)}) conditional(s32[]{:T(128)} %convert_element_type.9, () %tuple.23, f32[256,256]{1,0:T(8,128)S(1)} %slice.24), branch_computations={%region_0.1_spmd, %region_1.2_spmd} | conditional | bytes 589832 | solution.py:266
  1.0 14.9 %all_to_all.17 = f32[16,16,256]{2,1,0:T(8,128)S(1)} all-to-all(f32[16,16,256]{2,1,0:T(8,128)S(1)} %bitcast.5), channel_id=1, replica_groups=mesh['row'=16,'col'=32] {'row'}, dimensions={0} | all-to-all | bytes 524288 | tf_op jit(solution)/shard_map/cond/branch_1_fun/all_to_all | solution.py:248
  15.9 1.4 %collective-permute-start = (f32[16,256]{1,0:T(8,128)S(1)}, f32[16,256]{1,0:T(8,128)S(1)}, u32[]{:S(2)}, u32[]{:S(2)}) collective-permute-start(f32[16,256]{1,0:T(8,128)S(1)} %slice_bitcast_fusion), channel_id=1, source_target_pairs={{0,1},{32,33},{64,65},{96,97},{128,129},{160,161},{192,193},{224,2... | collective-permute-start | bytes 49160 | tf_op jit(solution)/shard_map/ppermute | solution.py:267
  17.4 3.9 %collective-permute-done.refs_1_ = f32[16,256]{1,0:T(8,128)S(1)} collective-permute-done((f32[16,256]{1,0:T(8,128)S(1)}, f32[16,256]{1,0:T(8,128)S(1)}, u32[]{:S(2)}, u32[]{:S(2)}) %collective-permute-start) | collective-permute-done | bytes 16416 | tf_op jit(solution)/shard_map/ppermute | solution.py:267
  21.3 1.3 %collective-permute-start.3 = (f32[2,16,256]{2,1,0:T(8,128)S(1)}, f32[2,16,256]{2,1,0:T(8,128)S(1)}, u32[]{:S(2)}, u32[]{:S(2)}) collective-permute-start(f32[2,16,256]{2,1,0:T(8,128)S(1)} %lead_kernel.1.refs_0_), channel_id=1, source_target_pairs={{0,16},{1,17},{32,48},{33,49},{64,80},{65,81},{96,112},{97,113},{1... | collective-permute-start | bytes 98312 | tf_op jit(solution)/shard_map/ppermute | solution.py:256
  22.6 1.3 %collective-permute-start.2 = (f32[2,16,256]{2,1,0:T(8,128)S(1)}, f32[2,16,256]{2,1,0:T(8,128)S(1)}, u32[]{:S(2)}, u32[]{:S(2)}) collective-permute-start(f32[2,16,256]{2,1,0:T(8,128)S(1)} %lead_kernel.1.refs_0_), channel_id=1, source_target_pairs={{0,8},{1,9},{32,40},{33,41},{64,72},{65,73},{96,104},{97,105},{128... | collective-permute-start | bytes 98312 | tf_op jit(solution)/shard_map/ppermute | solution.py:256
  23.9 1.3 %collective-permute-start.1 = (f32[2,16,256]{2,1,0:T(8,128)S(1)}, f32[2,16,256]{2,1,0:T(8,128)S(1)}, u32[]{:S(2)}, u32[]{:S(2)}) collective-permute-start(f32[2,16,256]{2,1,0:T(8,128)S(1)} %lead_kernel.1.refs_0_), channel_id=1, source_target_pairs={{0,24},{1,25},{32,56},{33,57},{64,88},{65,89},{96,120},{97,121},{1... | collective-permute-start | bytes 98312 | tf_op jit(solution)/shard_map/ppermute | solution.py:256
  25.2 0.9 %collective-permute-done.1.refs_1_ = f32[2,16,256]{2,1,0:T(8,128)S(1)} collective-permute-done((f32[2,16,256]{2,1,0:T(8,128)S(1)}, f32[2,16,256]{2,1,0:T(8,128)S(1)}, u32[]{:S(2)}, u32[]{:S(2)}) %collective-permute-start.1) | collective-permute-done | bytes 32800 | tf_op jit(solution)/shard_map/ppermute | solution.py:256
  26.2 0.1 panel_kernel.1
  26.3 1.3 %collective-permute-start.4 = (f32[512,256]{1,0:T(8,128)S(1)}, f32[512,256]{1,0:T(8,128)S(1)}, u32[]{:S(2)}, u32[]{:S(2)}) collective-permute-start(f32[512,256]{1,0:T(8,128)S(1)} %get-tuple-element.27.refs_0_), channel_id=1, source_target_pairs={{0,14},{1,19},{32,46},{33,51},{64,78},{65,83},{96,110},{97,115},{1... | collective-permute-start | bytes 1572872 | tf_op jit(solution)/shard_map/ppermute | solution.py:256
  27.6 1.3 %collective-permute-start.8 = (f32[2,16,256]{2,1,0:T(8,128)S(1)}, f32[2,16,256]{2,1,0:T(8,128)S(1)}, u32[]{:S(2)}, u32[]{:S(2)}) collective-permute-start(f32[2,16,256]{2,1,0:T(8,128)S(1)} %sum_kernel.5.refs_1_.refs_2_), channel_id=1, source_target_pairs={{0,4},{1,5},{8,12},{9,13},{16,20},{17,21},{24,28},{25,29},{32,36},... | collective-permute-start | bytes 98312 | tf_op jit(solution)/shard_map/ppermute | solution.py:256
  28.9 2.6 %collective-permute-start.7 = (f32[2,16,256]{2,1,0:T(8,128)S(1)}, f32[2,16,256]{2,1,0:T(8,128)S(1)}, u32[]{:S(2)}, u32[]{:S(2)}) collective-permute-start(f32[2,16,256]{2,1,0:T(8,128)S(1)} %sum_kernel.5.refs_1_.refs_2_), channel_id=1, source_target_pairs={{0,30},{1,31},{8,6},{9,7},{16,14},{17,15},{24,22},{25,23},{32,62},... | collective-permute-start | bytes 98312 | tf_op jit(solution)/shard_map/ppermute | solution.py:256
  31.5 1.3 %collective-permute-start.6 = (f32[2,16,256]{2,1,0:T(8,128)S(1)}, f32[2,16,256]{2,1,0:T(8,128)S(1)}, u32[]{:S(2)}, u32[]{:S(2)}) collective-permute-start(f32[2,16,256]{2,1,0:T(8,128)S(1)} %sum_kernel.5.refs_1_.refs_2_), channel_id=1, source_target_pairs={{0,2},{1,3},{8,10},{9,11},{16,18},{17,19},{24,26},{25,27},{32,34},... | collective-permute-start | bytes 98312 | tf_op jit(solution)/shard_map/ppermute | solution.py:256
  32.8 0.9 %collective-permute-done.4.refs_1_ = f32[512,256]{1,0:T(8,128)S(1)} collective-permute-done((f32[512,256]{1,0:T(8,128)S(1)}, f32[512,256]{1,0:T(8,128)S(1)}, u32[]{:S(2)}, u32[]{:S(2)}) %collective-permute-start.4) | collective-permute-done | bytes 524320 | tf_op jit(solution)/shard_map/ppermute | solution.py:256
  33.7 0.3 collective-permute-done.7.refs_4_
  34.0 1.1 %spread_kernel.1.refs_2_ = f32[16,4,16,256]{3,2,1,0:T(8,128)} custom-call(f32[2,16,256]{2,1,0:T(8,128)S(1)} %get-tuple-element.35.refs_4_.refs_0_, f32[2,16,256]{2,1,0:T(8,128)S(1)} %get-tuple-element.36.refs_1_, f32[2,16,256]{2,1,0:T(8,128)S(1)} %sum_kernel.5.refs_1_.refs_2_, f32[2,16,256]{2,1,0:T(8,128)S(1)} %collective-permute-done.6.refs_3_, ...), custom_call_target="tpu_custom_call" | custom-call | tf_op jit(solution)/shard_map/spread_kernel/pallas_call | solution.py:222
  35.1 3.7 %all-to-all-start.3 = ((f32[16,4,16,256]{3,2,1,0:T(8,128)}), f32[16,4,16,256]{3,2,1,0:T(8,128)S(1)}, u32[]{:S(2)}, u32[]{:S(2)}) async-start(f32[16,4,16,256]{3,2,1,0:T(8,128)} %spread_kernel.1.refs_2_), calls=%async_computation.3 | async-start | bytes 2097152 | tf_op jit(solution)/shard_map/all_to_all | solution.py:279
  38.8 7.1 %collective-permute-start.5 = (f32[512,256]{1,0:T(8,128)S(1)}, f32[512,256]{1,0:T(8,128)S(1)}, u32[]{:S(2)}, u32[]{:S(2)}) collective-permute-start(f32[512,256]{1,0:T(8,128)S(1)} %sum_kernel.6.refs_6_.refs_0_), channel_id=1, source_target_pairs={{0,8},{1,25},{14,22},{19,11},{32,40},{33,57},{46,54},{51,43},{64,7... | collective-permute-start | bytes 1572872 | tf_op jit(solution)/shard_map/ppermute | solution.py:256
  45.9 4.2 %collective-permute-start.10 = (f32[512,256]{1,0:T(8,128)S(1)}, f32[512,256]{1,0:T(8,128)S(1)}, u32[]{:S(2)}, u32[]{:S(2)}) collective-permute-start(f32[512,256]{1,0:T(8,128)S(1)} %get-tuple-element.26.refs_0_), channel_id=1, source_target_pairs={{0,1},{1,0},{32,33},{33,32},{64,65},{65,64},{96,97},{97,96},{128,1... | collective-permute-start | bytes 1572872 | tf_op jit(solution)/shard_map/ppermute | solution.py:244
  50.1 1.9 %collective-permute-done.5.refs_1_ = f32[512,256]{1,0:T(8,128)S(1)} collective-permute-done((f32[512,256]{1,0:T(8,128)S(1)}, f32[512,256]{1,0:T(8,128)S(1)}, u32[]{:S(2)}, u32[]{:S(2)}) %collective-permute-start.5) | collective-permute-done | bytes 524320 | tf_op jit(solution)/shard_map/ppermute | solution.py:256
  52.0 0.1 sum_kernel.7.refs_1_.refs_0_
  52.1 1.3 %collective-permute-start.9 = (f32[512,256]{1,0:T(8,128)S(1)}, f32[512,256]{1,0:T(8,128)S(1)}, u32[]{:S(2)}, u32[]{:S(2)}) collective-permute-start(f32[512,256]{1,0:T(8,128)S(1)} %sum_kernel.7.refs_1_.refs_0_), channel_id=1, source_target_pairs={{0,4},{1,29},{8,12},{25,21},{14,18},{19,15},{22,26},{11,7},{32,36}... | collective-permute-start | bytes 1572872 | tf_op jit(solution)/shard_map/ppermute | solution.py:256
  53.5 5.7 %collective-permute-start.12 = (f32[16,16,256]{2,1,0:T(8,128)S(1)}, f32[16,16,256]{2,1,0:T(8,128)S(1)}, u32[]{:S(2)}, u32[]{:S(2)}) collective-permute-start(f32[16,16,256]{2,1,0:T(8,128)S(1)} %pick_kernel.1), channel_id=1, source_target_pairs={{0,1},{1,0},{2,3},{3,2},{4,5},{5,4},{6,7},{7,6},{8,9},{9,8},{10,11... | collective-permute-start | bytes 786440 | tf_op jit(solution)/shard_map/ppermute | solution.py:244
  59.2 8.0 %first_kernel.1.refs_2_.refs_0_ = f32[256,256]{1,0:T(8,128)S(1)} custom-call(f32[16,4,16,256]{3,2,1,0:T(8,128)S(1)} %all-to-all-done.3.refs_0_.refs_1_, f32[512,256]{1,0:T(8,128)S(1)} %sum_kernel.7.refs_1_.refs_0_, f32[512,256]{1,0:T(8,128)S(1)} %collective-permute-done.10.refs_2_.refs_5_), custom_call_target="tpu_custom_call" | custom-call | flops 10000000000 | tf_op jit(solution)/shard_map/first_kernel/pallas_call | solution.py:222
  67.3 0.1 sum_kernel.8.refs_3_.refs_0_
  67.3 4.1 %collective-permute-start.11 = (f32[512,256]{1,0:T(8,128)S(1)}, f32[512,256]{1,0:T(8,128)S(1)}, u32[]{:S(2)}, u32[]{:S(2)}) collective-permute-start(f32[512,256]{1,0:T(8,128)S(1)} %sum_kernel.8.refs_3_.refs_0_), channel_id=1, source_target_pairs={{0,30},{1,3},{4,2},{29,31},{8,6},{25,27},{12,10},{21,23},{14,16},{... | collective-permute-start | bytes 1572872 | tf_op jit(solution)/shard_map/ppermute | solution.py:256
  71.4 8.8 %second_kernel.1 = (f32[256,256]{1,0:T(8,128)S(1)}, f32[256,256]{1,0:T(8,128)S(1)}, f32[256,256]{1,0:T(8,128)S(1)}, f32[256,256]{1,0:T(8,128)S(1)}) custom-call(f32[256,256]{1,0:T(8,128)S(1)} %first_kernel.1.refs_2_.refs_0_, f32[16,4,16,256]{3,2,1,0:T(8,128)S(1)} %all-to-all-done.3.refs_0_.refs_1_, f32[16,16,256]{2,1,0:T(8,128)S(1)} %collective-permute-done.12.refs_2_, ...), custom_call_target="tpu_custom_call" | custom-call | flops 10000000000 | tf_op jit(solution)/shard_map/second_kernel/pallas_call | solution.py:222
  80.3 0.1 sum_kernel.9.refs_5_.refs_1_
  80.3 0.7 collective-permute-start.13
  81.0 0.8 factors_kernel.1
  81.8 2.0 %final_kernel.1 = f32[512,256]{1,0:T(8,128)} custom-call(f32[512,256]{1,0:T(8,128)S(1)} %get-tuple-element.26.refs_0_, f32[512,256]{1,0:T(8,128)S(1)} %sum_kernel.9.refs_5_.refs_1_, f32[512,256]{1,0:T(8,128)S(1)} %collective-permute-done.13.refs_2_, f32[256,256]{1,0:T(8,128)S(1)} %get-tuple-element.32.refs_3_, f32[256,256]{1,0:T(8,128)S(1)} %get-tuple-element.33.refs_4_, ...), custom_call_target="tpu_custom_call" | custom-call | tf_op jit(solution)/shard_map/final_kernel/pallas_call | solution.py:222
  (22 shorter events, 0.3 us)
Async XLA Ops:
  15.9 10.2 %copy-start = (f32[512,256]{1,0:T(8,128)S(1)}, f32[512,256]{1,0:T(8,128)}, u32[]{:S(2)}) copy-start(f32[512,256]{1,0:T(8,128)} %refs_0_.1) | copy-start | bytes 1572868
  15.9 5.3 %collective-permute-start = (f32[16,256]{1,0:T(8,128)S(1)}, f32[16,256]{1,0:T(8,128)S(1)}, u32[]{:S(2)}, u32[]{:S(2)}) collective-permute-start(f32[16,256]{1,0:T(8,128)S(1)} %slice_bitcast_fusion), channel_id=1, source_target_pairs={{0,1},{32,33},{64,65},{96,97},{128,129},{160,161},{192,193},{224,2... | collective-permute-start | bytes 49160 | tf_op jit(solution)/shard_map/ppermute | solution.py:267
  21.3 3.9 %collective-permute-start.3 = (f32[2,16,256]{2,1,0:T(8,128)S(1)}, f32[2,16,256]{2,1,0:T(8,128)S(1)}, u32[]{:S(2)}, u32[]{:S(2)}) collective-permute-start(f32[2,16,256]{2,1,0:T(8,128)S(1)} %lead_kernel.1.refs_0_), channel_id=1, source_target_pairs={{0,16},{1,17},{32,48},{33,49},{64,80},{65,81},{96,112},{97,113},{1... | collective-permute-start | bytes 98312 | tf_op jit(solution)/shard_map/ppermute | solution.py:256
  22.6 2.7 %collective-permute-start.2 = (f32[2,16,256]{2,1,0:T(8,128)S(1)}, f32[2,16,256]{2,1,0:T(8,128)S(1)}, u32[]{:S(2)}, u32[]{:S(2)}) collective-permute-start(f32[2,16,256]{2,1,0:T(8,128)S(1)} %lead_kernel.1.refs_0_), channel_id=1, source_target_pairs={{0,8},{1,9},{32,40},{33,41},{64,72},{65,73},{96,104},{97,105},{128... | collective-permute-start | bytes 98312 | tf_op jit(solution)/shard_map/ppermute | solution.py:256
  23.9 2.3 %collective-permute-start.1 = (f32[2,16,256]{2,1,0:T(8,128)S(1)}, f32[2,16,256]{2,1,0:T(8,128)S(1)}, u32[]{:S(2)}, u32[]{:S(2)}) collective-permute-start(f32[2,16,256]{2,1,0:T(8,128)S(1)} %lead_kernel.1.refs_0_), channel_id=1, source_target_pairs={{0,24},{1,25},{32,56},{33,57},{64,88},{65,89},{96,120},{97,121},{1... | collective-permute-start | bytes 98312 | tf_op jit(solution)/shard_map/ppermute | solution.py:256
  26.3 7.4 %collective-permute-start.4 = (f32[512,256]{1,0:T(8,128)S(1)}, f32[512,256]{1,0:T(8,128)S(1)}, u32[]{:S(2)}, u32[]{:S(2)}) collective-permute-start(f32[512,256]{1,0:T(8,128)S(1)} %get-tuple-element.27.refs_0_), channel_id=1, source_target_pairs={{0,14},{1,19},{32,46},{33,51},{64,78},{65,83},{96,110},{97,115},{1... | collective-permute-start | bytes 1572872 | tf_op jit(solution)/shard_map/ppermute | solution.py:256
  27.6 6.1 %collective-permute-start.8 = (f32[2,16,256]{2,1,0:T(8,128)S(1)}, f32[2,16,256]{2,1,0:T(8,128)S(1)}, u32[]{:S(2)}, u32[]{:S(2)}) collective-permute-start(f32[2,16,256]{2,1,0:T(8,128)S(1)} %sum_kernel.5.refs_1_.refs_2_), channel_id=1, source_target_pairs={{0,4},{1,5},{8,12},{9,13},{16,20},{17,21},{24,28},{25,29},{32,36},... | collective-permute-start | bytes 98312 | tf_op jit(solution)/shard_map/ppermute | solution.py:256
  28.9 5.1 %collective-permute-start.7 = (f32[2,16,256]{2,1,0:T(8,128)S(1)}, f32[2,16,256]{2,1,0:T(8,128)S(1)}, u32[]{:S(2)}, u32[]{:S(2)}) collective-permute-start(f32[2,16,256]{2,1,0:T(8,128)S(1)} %sum_kernel.5.refs_1_.refs_2_), channel_id=1, source_target_pairs={{0,30},{1,31},{8,6},{9,7},{16,14},{17,15},{24,22},{25,23},{32,62},... | collective-permute-start | bytes 98312 | tf_op jit(solution)/shard_map/ppermute | solution.py:256
  31.5 2.6 %collective-permute-start.6 = (f32[2,16,256]{2,1,0:T(8,128)S(1)}, f32[2,16,256]{2,1,0:T(8,128)S(1)}, u32[]{:S(2)}, u32[]{:S(2)}) collective-permute-start(f32[2,16,256]{2,1,0:T(8,128)S(1)} %sum_kernel.5.refs_1_.refs_2_), channel_id=1, source_target_pairs={{0,2},{1,3},{8,10},{9,11},{16,18},{17,19},{24,26},{25,27},{32,34},... | collective-permute-start | bytes 98312 | tf_op jit(solution)/shard_map/ppermute | solution.py:256
  35.1 18.3 %all-to-all-start.3 = ((f32[16,4,16,256]{3,2,1,0:T(8,128)}), f32[16,4,16,256]{3,2,1,0:T(8,128)S(1)}, u32[]{:S(2)}, u32[]{:S(2)}) async-start(f32[16,4,16,256]{3,2,1,0:T(8,128)} %spread_kernel.1.refs_2_), calls=%async_computation.3 | async-start | bytes 2097152 | tf_op jit(solution)/shard_map/all_to_all | solution.py:279
  38.8 13.2 %collective-permute-start.5 = (f32[512,256]{1,0:T(8,128)S(1)}, f32[512,256]{1,0:T(8,128)S(1)}, u32[]{:S(2)}, u32[]{:S(2)}) collective-permute-start(f32[512,256]{1,0:T(8,128)S(1)} %sum_kernel.6.refs_6_.refs_0_), channel_id=1, source_target_pairs={{0,8},{1,25},{14,22},{19,11},{32,40},{33,57},{46,54},{51,43},{64,7... | collective-permute-start | bytes 1572872 | tf_op jit(solution)/shard_map/ppermute | solution.py:256
  45.9 13.3 %collective-permute-start.10 = (f32[512,256]{1,0:T(8,128)S(1)}, f32[512,256]{1,0:T(8,128)S(1)}, u32[]{:S(2)}, u32[]{:S(2)}) collective-permute-start(f32[512,256]{1,0:T(8,128)S(1)} %get-tuple-element.26.refs_0_), channel_id=1, source_target_pairs={{0,1},{1,0},{32,33},{33,32},{64,65},{65,64},{96,97},{97,96},{128,1... | collective-permute-start | bytes 1572872 | tf_op jit(solution)/shard_map/ppermute | solution.py:244
  52.1 15.2 %collective-permute-start.9 = (f32[512,256]{1,0:T(8,128)S(1)}, f32[512,256]{1,0:T(8,128)S(1)}, u32[]{:S(2)}, u32[]{:S(2)}) collective-permute-start(f32[512,256]{1,0:T(8,128)S(1)} %sum_kernel.7.refs_1_.refs_0_), channel_id=1, source_target_pairs={{0,4},{1,29},{8,12},{25,21},{14,18},{19,15},{22,26},{11,7},{32,36}... | collective-permute-start | bytes 1572872 | tf_op jit(solution)/shard_map/ppermute | solution.py:256
  53.5 17.9 %collective-permute-start.12 = (f32[16,16,256]{2,1,0:T(8,128)S(1)}, f32[16,16,256]{2,1,0:T(8,128)S(1)}, u32[]{:S(2)}, u32[]{:S(2)}) collective-permute-start(f32[16,16,256]{2,1,0:T(8,128)S(1)} %pick_kernel.1), channel_id=1, source_target_pairs={{0,1},{1,0},{2,3},{3,2},{4,5},{5,4},{6,7},{7,6},{8,9},{9,8},{10,11... | collective-permute-start | bytes 786440 | tf_op jit(solution)/shard_map/ppermute | solution.py:244
  67.3 12.9 %collective-permute-start.11 = (f32[512,256]{1,0:T(8,128)S(1)}, f32[512,256]{1,0:T(8,128)S(1)}, u32[]{:S(2)}, u32[]{:S(2)}) collective-permute-start(f32[512,256]{1,0:T(8,128)S(1)} %sum_kernel.8.refs_3_.refs_0_), channel_id=1, source_target_pairs={{0,30},{1,3},{4,2},{29,31},{8,6},{25,27},{12,10},{21,23},{14,16},{... | collective-permute-start | bytes 1572872 | tf_op jit(solution)/shard_map/ppermute | solution.py:256
  80.3 1.5 %collective-permute-start.13 = (f32[512,256]{1,0:T(8,128)S(1)}, f32[512,256]{1,0:T(8,128)S(1)}, u32[]{:S(2)}, u32[]{:S(2)}) collective-permute-start(f32[512,256]{1,0:T(8,128)S(1)} %sum_kernel.9.refs_5_.refs_1_), channel_id=1, source_target_pairs={{2,3},{3,2},{4,5},{5,4},{6,7},{7,6},{8,9},{9,8},{10,11},{11,10},{1... | collective-permute-start | bytes 1572872 | tf_op jit(solution)/shard_map/ppermute | solution.py:244

commit v7 on v6

--- a/solution.py
+++ b/solution.py
@@ -15,8 +15,8 @@
 PANEL_TREE = (
     ((0, 7),),
     ((0, 4), (7, 11)),
-    ((0, 2), (4, 6), (7, 9), (11, 13)),
-    ((0, 15), (2, 1), (4, 3), (6, 5), (7, 8), (9, 10), (11, 12), (13, 14)),
+    ((0, 2), (7, 6), (4, 8), (11, 13)),
+    ((0, 15), (2, 1), (4, 3), (6, 5), (7, 10), (8, 9), (11, 12), (13, 14)),
 )
 PIECE_TREE = (
     (((0, 12),), ((0, 4),), ((0, 8),)),

time: 84.5 us -> 84.5 us (level)
  no operation moved by 1% of the time
where the time goes in v7:
time: 84.5 us; the launch traced here: 84 us
  starting transfers between devices  38.5 us (46%)
  Pallas kernels  21.1 us (25%)
  blocking collectives  14.9 us (18%)
  waiting for transfers between devices  7.99 us (9%)
  local copies, waits for them, and re-layouts  0.98 us (1%)
    ppermute x10, starting transfers between devices, along_z(): return lax.ppermute(value, 'col', both_cores(pairs, mirror))  22.9 us
    pallas_call x13, Pallas kernels, call(): pl.pallas_call(whole, out_shape=outs, in_specs=[pl.BlockSpec(memory_space...  21.1 us
    all_to_all x1, blocking collectives, scatter_rows(): return lax.all_to_all(top.reshape(16, 16, NB), 'row', 0, 0)[:2]  14.9 us
    ppermute x3, starting transfers between devices, swap_cores(): lax.ppermute(value, 'col', [(2 * z + c, 2 * z + 1 - c) for z in chips for...  10.6 us
    ppermute x10, waiting for transfers between devices, along_z(): return lax.ppermute(value, 'col', both_cores(pairs, mirror))  4.04 us
    ppermute x1, waiting for transfers between devices, local(): lax.ppermute(first[0], 'col', [(0, 1)])  3.89 us
    all_to_all x1, starting transfers between devices, local(): lead = lax.all_to_all(spread, 'row', 0, 0)  3.65 us
  transfers between devices with their start and end apart: 15, of which 5 were waited for; matrix products, arithmetic and copies ran while one was open for 0% of the time, Pallas kernels for 21%

profile of v7, /device:TPU:1, one launch (start us, length us, event | category | flops | bytes accessed | tf_op | source)
XLA Modules:
  0.0 84.0 jit_solution(7980171499009566836)
XLA Ops:
  0.0 1.0 %slice.24 = f32[256,256]{1,0:T(8,128)S(1)} slice(f32[512,256]{1,0:T(8,128)} %refs_0_.1), slice={[0:256], [0:256]} | slice | bytes 524288 | tf_op jit(solution)/shard_map/slice | solution.py:261
  1.0 15.0 %conditional.3 = (f32[2,16,256]{2,1,0:T(8,128)S(1)}) conditional(s32[]{:T(128)} %convert_element_type.9, () %tuple.23, f32[256,256]{1,0:T(8,128)S(1)} %slice.24), branch_computations={%region_0.1_spmd, %region_1.2_spmd} | conditional | bytes 589832 | solution.py:266
  1.0 14.9 %all_to_all.17 = f32[16,16,256]{2,1,0:T(8,128)S(1)} all-to-all(f32[16,16,256]{2,1,0:T(8,128)S(1)} %bitcast.5), channel_id=1, replica_groups=mesh['row'=16,'col'=32] {'row'}, dimensions={0} | all-to-all | bytes 524288 | tf_op jit(solution)/shard_map/cond/branch_1_fun/all_to_all | solution.py:248
  15.9 1.4 %collective-permute-start = (f32[16,256]{1,0:T(8,128)S(1)}, f32[16,256]{1,0:T(8,128)S(1)}, u32[]{:S(2)}, u32[]{:S(2)}) collective-permute-start(f32[16,256]{1,0:T(8,128)S(1)} %slice_bitcast_fusion), channel_id=1, source_target_pairs={{0,1},{32,33},{64,65},{96,97},{128,129},{160,161},{192,193},{224,2... | collective-permute-start | bytes 49160 | tf_op jit(solution)/shard_map/ppermute | solution.py:267
  17.4 3.9 %collective-permute-done.refs_1_ = f32[16,256]{1,0:T(8,128)S(1)} collective-permute-done((f32[16,256]{1,0:T(8,128)S(1)}, f32[16,256]{1,0:T(8,128)S(1)}, u32[]{:S(2)}, u32[]{:S(2)}) %collective-permute-start) | collective-permute-done | bytes 16416 | tf_op jit(solution)/shard_map/ppermute | solution.py:267
  21.3 1.3 %collective-permute-start.3 = (f32[2,16,256]{2,1,0:T(8,128)S(1)}, f32[2,16,256]{2,1,0:T(8,128)S(1)}, u32[]{:S(2)}, u32[]{:S(2)}) collective-permute-start(f32[2,16,256]{2,1,0:T(8,128)S(1)} %lead_kernel.1.refs_0_), channel_id=1, source_target_pairs={{0,16},{1,17},{32,48},{33,49},{64,80},{65,81},{96,112},{97,113},{1... | collective-permute-start | bytes 98312 | tf_op jit(solution)/shard_map/ppermute | solution.py:256
  22.6 1.3 %collective-permute-start.2 = (f32[2,16,256]{2,1,0:T(8,128)S(1)}, f32[2,16,256]{2,1,0:T(8,128)S(1)}, u32[]{:S(2)}, u32[]{:S(2)}) collective-permute-start(f32[2,16,256]{2,1,0:T(8,128)S(1)} %lead_kernel.1.refs_0_), channel_id=1, source_target_pairs={{0,8},{1,9},{32,40},{33,41},{64,72},{65,73},{96,104},{97,105},{128... | collective-permute-start | bytes 98312 | tf_op jit(solution)/shard_map/ppermute | solution.py:256
  23.9 1.3 %collective-permute-start.1 = (f32[2,16,256]{2,1,0:T(8,128)S(1)}, f32[2,16,256]{2,1,0:T(8,128)S(1)}, u32[]{:S(2)}, u32[]{:S(2)}) collective-permute-start(f32[2,16,256]{2,1,0:T(8,128)S(1)} %lead_kernel.1.refs_0_), channel_id=1, source_target_pairs={{0,24},{1,25},{32,56},{33,57},{64,88},{65,89},{96,120},{97,121},{1... | collective-permute-start | bytes 98312 | tf_op jit(solution)/shard_map/ppermute | solution.py:256
  25.2 0.9 %collective-permute-done.1.refs_1_ = f32[2,16,256]{2,1,0:T(8,128)S(1)} collective-permute-done((f32[2,16,256]{2,1,0:T(8,128)S(1)}, f32[2,16,256]{2,1,0:T(8,128)S(1)}, u32[]{:S(2)}, u32[]{:S(2)}) %collective-permute-start.1) | collective-permute-done | bytes 32800 | tf_op jit(solution)/shard_map/ppermute | solution.py:256
  26.2 0.1 panel_kernel.1
  26.3 1.3 %collective-permute-start.4 = (f32[512,256]{1,0:T(8,128)S(1)}, f32[512,256]{1,0:T(8,128)S(1)}, u32[]{:S(2)}, u32[]{:S(2)}) collective-permute-start(f32[512,256]{1,0:T(8,128)S(1)} %get-tuple-element.27.refs_0_), channel_id=1, source_target_pairs={{0,14},{1,19},{32,46},{33,51},{64,78},{65,83},{96,110},{97,115},{1... | collective-permute-start | bytes 1572872 | tf_op jit(solution)/shard_map/ppermute | solution.py:256
  27.6 1.3 %collective-permute-start.8 = (f32[2,16,256]{2,1,0:T(8,128)S(1)}, f32[2,16,256]{2,1,0:T(8,128)S(1)}, u32[]{:S(2)}, u32[]{:S(2)}) collective-permute-start(f32[2,16,256]{2,1,0:T(8,128)S(1)} %sum_kernel.5.refs_1_.refs_2_), channel_id=1, source_target_pairs={{0,4},{1,5},{8,12},{9,13},{16,20},{17,21},{24,28},{25,29},{32,36},... | collective-permute-start | bytes 98312 | tf_op jit(solution)/shard_map/ppermute | solution.py:256
  28.9 2.6 %collective-permute-start.7 = (f32[2,16,256]{2,1,0:T(8,128)S(1)}, f32[2,16,256]{2,1,0:T(8,128)S(1)}, u32[]{:S(2)}, u32[]{:S(2)}) collective-permute-start(f32[2,16,256]{2,1,0:T(8,128)S(1)} %sum_kernel.5.refs_1_.refs_2_), channel_id=1, source_target_pairs={{0,30},{1,31},{8,6},{9,7},{16,14},{17,15},{24,22},{25,23},{32,62},... | collective-permute-start | bytes 98312 | tf_op jit(solution)/shard_map/ppermute | solution.py:256
  31.5 1.3 %collective-permute-start.6 = (f32[2,16,256]{2,1,0:T(8,128)S(1)}, f32[2,16,256]{2,1,0:T(8,128)S(1)}, u32[]{:S(2)}, u32[]{:S(2)}) collective-permute-start(f32[2,16,256]{2,1,0:T(8,128)S(1)} %sum_kernel.5.refs_1_.refs_2_), channel_id=1, source_target_pairs={{0,2},{1,3},{8,10},{9,11},{16,18},{17,19},{24,26},{25,27},{32,34},... | collective-permute-start | bytes 98312 | tf_op jit(solution)/shard_map/ppermute | solution.py:256
  32.8 0.9 %collective-permute-done.4.refs_1_ = f32[512,256]{1,0:T(8,128)S(1)} collective-permute-done((f32[512,256]{1,0:T(8,128)S(1)}, f32[512,256]{1,0:T(8,128)S(1)}, u32[]{:S(2)}, u32[]{:S(2)}) %collective-permute-start.4) | collective-permute-done | bytes 524320 | tf_op jit(solution)/shard_map/ppermute | solution.py:256
  33.7 0.1 sum_kernel.6.refs_6_.refs_0_
  33.7 0.3 collective-permute-done.7.refs_4_
  34.0 1.1 %spread_kernel.1.refs_2_ = f32[16,4,16,256]{3,2,1,0:T(8,128)} custom-call(f32[2,16,256]{2,1,0:T(8,128)S(1)} %get-tuple-element.35.refs_4_.refs_0_, f32[2,16,256]{2,1,0:T(8,128)S(1)} %get-tuple-element.36.refs_1_, f32[2,16,256]{2,1,0:T(8,128)S(1)} %sum_kernel.5.refs_1_.refs_2_, f32[2,16,256]{2,1,0:T(8,128)S(1)} %collective-permute-done.6.refs_3_, ...), custom_call_target="tpu_custom_call" | custom-call | tf_op jit(solution)/shard_map/spread_kernel/pallas_call | solution.py:222
  35.1 3.7 %all-to-all-start.3 = ((f32[16,4,16,256]{3,2,1,0:T(8,128)}), f32[16,4,16,256]{3,2,1,0:T(8,128)S(1)}, u32[]{:S(2)}, u32[]{:S(2)}) async-start(f32[16,4,16,256]{3,2,1,0:T(8,128)} %spread_kernel.1.refs_2_), calls=%async_computation.3 | async-start | bytes 2097152 | tf_op jit(solution)/shard_map/all_to_all | solution.py:279
  38.8 7.1 %collective-permute-start.5 = (f32[512,256]{1,0:T(8,128)S(1)}, f32[512,256]{1,0:T(8,128)S(1)}, u32[]{:S(2)}, u32[]{:S(2)}) collective-permute-start(f32[512,256]{1,0:T(8,128)S(1)} %sum_kernel.6.refs_6_.refs_0_), channel_id=1, source_target_pairs={{0,8},{1,25},{14,22},{19,11},{32,40},{33,57},{46,54},{51,43},{64,7... | collective-permute-start | bytes 1572872 | tf_op jit(solution)/shard_map/ppermute | solution.py:256
  45.9 4.2 %collective-permute-start.10 = (f32[512,256]{1,0:T(8,128)S(1)}, f32[512,256]{1,0:T(8,128)S(1)}, u32[]{:S(2)}, u32[]{:S(2)}) collective-permute-start(f32[512,256]{1,0:T(8,128)S(1)} %get-tuple-element.26.refs_0_), channel_id=1, source_target_pairs={{0,1},{1,0},{32,33},{33,32},{64,65},{65,64},{96,97},{97,96},{128,1... | collective-permute-start | bytes 1572872 | tf_op jit(solution)/shard_map/ppermute | solution.py:244
  50.1 1.9 %collective-permute-done.5.refs_1_ = f32[512,256]{1,0:T(8,128)S(1)} collective-permute-done((f32[512,256]{1,0:T(8,128)S(1)}, f32[512,256]{1,0:T(8,128)S(1)}, u32[]{:S(2)}, u32[]{:S(2)}) %collective-permute-start.5) | collective-permute-done | bytes 524320 | tf_op jit(solution)/shard_map/ppermute | solution.py:256
  52.1 1.3 %collective-permute-start.9 = (f32[512,256]{1,0:T(8,128)S(1)}, f32[512,256]{1,0:T(8,128)S(1)}, u32[]{:S(2)}, u32[]{:S(2)}) collective-permute-start(f32[512,256]{1,0:T(8,128)S(1)} %sum_kernel.7.refs_1_.refs_0_), channel_id=1, source_target_pairs={{0,4},{1,29},{14,12},{19,21},{8,16},{25,17},{22,26},{11,7},{32,36}... | collective-permute-start | bytes 1572872 | tf_op jit(solution)/shard_map/ppermute | solution.py:256
  53.5 5.7 %collective-permute-start.12 = (f32[16,16,256]{2,1,0:T(8,128)S(1)}, f32[16,16,256]{2,1,0:T(8,128)S(1)}, u32[]{:S(2)}, u32[]{:S(2)}) collective-permute-start(f32[16,16,256]{2,1,0:T(8,128)S(1)} %pick_kernel.1), channel_id=1, source_target_pairs={{0,1},{1,0},{2,3},{3,2},{4,5},{5,4},{6,7},{7,6},{8,9},{9,8},{10,11... | collective-permute-start | bytes 786440 | tf_op jit(solution)/shard_map/ppermute | solution.py:244
  59.2 8.0 %first_kernel.1.refs_2_.refs_0_ = f32[256,256]{1,0:T(8,128)S(1)} custom-call(f32[16,4,16,256]{3,2,1,0:T(8,128)S(1)} %all-to-all-done.3.refs_0_.refs_1_, f32[512,256]{1,0:T(8,128)S(1)} %sum_kernel.7.refs_1_.refs_0_, f32[512,256]{1,0:T(8,128)S(1)} %collective-permute-done.10.refs_2_.refs_5_), custom_call_target="tpu_custom_call" | custom-call | flops 10000000000 | tf_op jit(solution)/shard_map/first_kernel/pallas_call | solution.py:222
  67.3 0.1 sum_kernel.8.refs_3_.refs_0_
  67.3 4.1 %collective-permute-start.11 = (f32[512,256]{1,0:T(8,128)S(1)}, f32[512,256]{1,0:T(8,128)S(1)}, u32[]{:S(2)}, u32[]{:S(2)}) collective-permute-start(f32[512,256]{1,0:T(8,128)S(1)} %sum_kernel.8.refs_3_.refs_0_), channel_id=1, source_target_pairs={{0,30},{1,3},{4,2},{29,31},{8,6},{25,27},{12,10},{21,23},{14,20},{... | collective-permute-start | bytes 1572872 | tf_op jit(solution)/shard_map/ppermute | solution.py:256
  71.4 8.8 %second_kernel.1 = (f32[256,256]{1,0:T(8,128)S(1)}, f32[256,256]{1,0:T(8,128)S(1)}, f32[256,256]{1,0:T(8,128)S(1)}, f32[256,256]{1,0:T(8,128)S(1)}) custom-call(f32[256,256]{1,0:T(8,128)S(1)} %first_kernel.1.refs_2_.refs_0_, f32[16,4,16,256]{3,2,1,0:T(8,128)S(1)} %all-to-all-done.3.refs_0_.refs_1_, f32[16,16,256]{2,1,0:T(8,128)S(1)} %collective-permute-done.12.refs_2_, ...), custom_call_target="tpu_custom_call" | custom-call | flops 10000000000 | tf_op jit(solution)/shard_map/second_kernel/pallas_call | solution.py:222
  80.3 0.1 sum_kernel.9.refs_5_.refs_1_
  80.3 0.7 collective-permute-start.13
  81.0 0.8 factors_kernel.1
  81.8 2.0 %final_kernel.1 = f32[512,256]{1,0:T(8,128)} custom-call(f32[512,256]{1,0:T(8,128)S(1)} %get-tuple-element.26.refs_0_, f32[512,256]{1,0:T(8,128)S(1)} %sum_kernel.9.refs_5_.refs_1_, f32[512,256]{1,0:T(8,128)S(1)} %collective-permute-done.13.refs_2_, f32[256,256]{1,0:T(8,128)S(1)} %get-tuple-element.32.refs_3_, f32[256,256]{1,0:T(8,128)S(1)} %get-tuple-element.33.refs_4_, ...), custom_call_target="tpu_custom_call" | custom-call | tf_op jit(solution)/shard_map/final_kernel/pallas_call | solution.py:222
  (22 shorter events, 0.3 us)
Async XLA Ops:
  15.9 10.2 %copy-start = (f32[512,256]{1,0:T(8,128)S(1)}, f32[512,256]{1,0:T(8,128)}, u32[]{:S(2)}) copy-start(f32[512,256]{1,0:T(8,128)} %refs_0_.1) | copy-start | bytes 1572868
  15.9 5.3 %collective-permute-start = (f32[16,256]{1,0:T(8,128)S(1)}, f32[16,256]{1,0:T(8,128)S(1)}, u32[]{:S(2)}, u32[]{:S(2)}) collective-permute-start(f32[16,256]{1,0:T(8,128)S(1)} %slice_bitcast_fusion), channel_id=1, source_target_pairs={{0,1},{32,33},{64,65},{96,97},{128,129},{160,161},{192,193},{224,2... | collective-permute-start | bytes 49160 | tf_op jit(solution)/shard_map/ppermute | solution.py:267
  21.3 3.9 %collective-permute-start.3 = (f32[2,16,256]{2,1,0:T(8,128)S(1)}, f32[2,16,256]{2,1,0:T(8,128)S(1)}, u32[]{:S(2)}, u32[]{:S(2)}) collective-permute-start(f32[2,16,256]{2,1,0:T(8,128)S(1)} %lead_kernel.1.refs_0_), channel_id=1, source_target_pairs={{0,16},{1,17},{32,48},{33,49},{64,80},{65,81},{96,112},{97,113},{1... | collective-permute-start | bytes 98312 | tf_op jit(solution)/shard_map/ppermute | solution.py:256
  22.6 2.7 %collective-permute-start.2 = (f32[2,16,256]{2,1,0:T(8,128)S(1)}, f32[2,16,256]{2,1,0:T(8,128)S(1)}, u32[]{:S(2)}, u32[]{:S(2)}) collective-permute-start(f32[2,16,256]{2,1,0:T(8,128)S(1)} %lead_kernel.1.refs_0_), channel_id=1, source_target_pairs={{0,8},{1,9},{32,40},{33,41},{64,72},{65,73},{96,104},{97,105},{128... | collective-permute-start | bytes 98312 | tf_op jit(solution)/shard_map/ppermute | solution.py:256
  23.9 2.3 %collective-permute-start.1 = (f32[2,16,256]{2,1,0:T(8,128)S(1)}, f32[2,16,256]{2,1,0:T(8,128)S(1)}, u32[]{:S(2)}, u32[]{:S(2)}) collective-permute-start(f32[2,16,256]{2,1,0:T(8,128)S(1)} %lead_kernel.1.refs_0_), channel_id=1, source_target_pairs={{0,24},{1,25},{32,56},{33,57},{64,88},{65,89},{96,120},{97,121},{1... | collective-permute-start | bytes 98312 | tf_op jit(solution)/shard_map/ppermute | solution.py:256
  26.3 7.4 %collective-permute-start.4 = (f32[512,256]{1,0:T(8,128)S(1)}, f32[512,256]{1,0:T(8,128)S(1)}, u32[]{:S(2)}, u32[]{:S(2)}) collective-permute-start(f32[512,256]{1,0:T(8,128)S(1)} %get-tuple-element.27.refs_0_), channel_id=1, source_target_pairs={{0,14},{1,19},{32,46},{33,51},{64,78},{65,83},{96,110},{97,115},{1... | collective-permute-start | bytes 1572872 | tf_op jit(solution)/shard_map/ppermute | solution.py:256
  27.6 6.1 %collective-permute-start.8 = (f32[2,16,256]{2,1,0:T(8,128)S(1)}, f32[2,16,256]{2,1,0:T(8,128)S(1)}, u32[]{:S(2)}, u32[]{:S(2)}) collective-permute-start(f32[2,16,256]{2,1,0:T(8,128)S(1)} %sum_kernel.5.refs_1_.refs_2_), channel_id=1, source_target_pairs={{0,4},{1,5},{8,12},{9,13},{16,20},{17,21},{24,28},{25,29},{32,36},... | collective-permute-start | bytes 98312 | tf_op jit(solution)/shard_map/ppermute | solution.py:256
  28.9 5.1 %collective-permute-start.7 = (f32[2,16,256]{2,1,0:T(8,128)S(1)}, f32[2,16,256]{2,1,0:T(8,128)S(1)}, u32[]{:S(2)}, u32[]{:S(2)}) collective-permute-start(f32[2,16,256]{2,1,0:T(8,128)S(1)} %sum_kernel.5.refs_1_.refs_2_), channel_id=1, source_target_pairs={{0,30},{1,31},{8,6},{9,7},{16,14},{17,15},{24,22},{25,23},{32,62},... | collective-permute-start | bytes 98312 | tf_op jit(solution)/shard_map/ppermute | solution.py:256
  31.5 2.6 %collective-permute-start.6 = (f32[2,16,256]{2,1,0:T(8,128)S(1)}, f32[2,16,256]{2,1,0:T(8,128)S(1)}, u32[]{:S(2)}, u32[]{:S(2)}) collective-permute-start(f32[2,16,256]{2,1,0:T(8,128)S(1)} %sum_kernel.5.refs_1_.refs_2_), channel_id=1, source_target_pairs={{0,2},{1,3},{8,10},{9,11},{16,18},{17,19},{24,26},{25,27},{32,34},... | collective-permute-start | bytes 98312 | tf_op jit(solution)/shard_map/ppermute | solution.py:256
  35.1 18.3 %all-to-all-start.3 = ((f32[16,4,16,256]{3,2,1,0:T(8,128)}), f32[16,4,16,256]{3,2,1,0:T(8,128)S(1)}, u32[]{:S(2)}, u32[]{:S(2)}) async-start(f32[16,4,16,256]{3,2,1,0:T(8,128)} %spread_kernel.1.refs_2_), calls=%async_computation.3 | async-start | bytes 2097152 | tf_op jit(solution)/shard_map/all_to_all | solution.py:279
  38.8 13.2 %collective-permute-start.5 = (f32[512,256]{1,0:T(8,128)S(1)}, f32[512,256]{1,0:T(8,128)S(1)}, u32[]{:S(2)}, u32[]{:S(2)}) collective-permute-start(f32[512,256]{1,0:T(8,128)S(1)} %sum_kernel.6.refs_6_.refs_0_), channel_id=1, source_target_pairs={{0,8},{1,25},{14,22},{19,11},{32,40},{33,57},{46,54},{51,43},{64,7... | collective-permute-start | bytes 1572872 | tf_op jit(solution)/shard_map/ppermute | solution.py:256
  45.9 13.3 %collective-permute-start.10 = (f32[512,256]{1,0:T(8,128)S(1)}, f32[512,256]{1,0:T(8,128)S(1)}, u32[]{:S(2)}, u32[]{:S(2)}) collective-permute-start(f32[512,256]{1,0:T(8,128)S(1)} %get-tuple-element.26.refs_0_), channel_id=1, source_target_pairs={{0,1},{1,0},{32,33},{33,32},{64,65},{65,64},{96,97},{97,96},{128,1... | collective-permute-start | bytes 1572872 | tf_op jit(solution)/shard_map/ppermute | solution.py:244
  52.1 15.2 %collective-permute-start.9 = (f32[512,256]{1,0:T(8,128)S(1)}, f32[512,256]{1,0:T(8,128)S(1)}, u32[]{:S(2)}, u32[]{:S(2)}) collective-permute-start(f32[512,256]{1,0:T(8,128)S(1)} %sum_kernel.7.refs_1_.refs_0_), channel_id=1, source_target_pairs={{0,4},{1,29},{14,12},{19,21},{8,16},{25,17},{22,26},{11,7},{32,36}... | collective-permute-start | bytes 1572872 | tf_op jit(solution)/shard_map/ppermute | solution.py:256
  53.5 17.9 %collective-permute-start.12 = (f32[16,16,256]{2,1,0:T(8,128)S(1)}, f32[16,16,256]{2,1,0:T(8,128)S(1)}, u32[]{:S(2)}, u32[]{:S(2)}) collective-permute-start(f32[16,16,256]{2,1,0:T(8,128)S(1)} %pick_kernel.1), channel_id=1, source_target_pairs={{0,1},{1,0},{2,3},{3,2},{4,5},{5,4},{6,7},{7,6},{8,9},{9,8},{10,11... | collective-permute-start | bytes 786440 | tf_op jit(solution)/shard_map/ppermute | solution.py:244
  67.3 12.9 %collective-permute-start.11 = (f32[512,256]{1,0:T(8,128)S(1)}, f32[512,256]{1,0:T(8,128)S(1)}, u32[]{:S(2)}, u32[]{:S(2)}) collective-permute-start(f32[512,256]{1,0:T(8,128)S(1)} %sum_kernel.8.refs_3_.refs_0_), channel_id=1, source_target_pairs={{0,30},{1,3},{4,2},{29,31},{8,6},{25,27},{12,10},{21,23},{14,20},{... | collective-permute-start | bytes 1572872 | tf_op jit(solution)/shard_map/ppermute | solution.py:256
  80.3 1.5 %collective-permute-start.13 = (f32[512,256]{1,0:T(8,128)S(1)}, f32[512,256]{1,0:T(8,128)S(1)}, u32[]{:S(2)}, u32[]{:S(2)}) collective-permute-start(f32[512,256]{1,0:T(8,128)S(1)} %sum_kernel.9.refs_5_.refs_1_), channel_id=1, source_target_pairs={{2,3},{3,2},{4,5},{5,4},{6,7},{7,6},{8,9},{9,8},{10,11},{11,10},{1... | collective-permute-start | bytes 1572872 | tf_op jit(solution)/shard_map/ppermute | solution.py:244

commit v8 on v6

--- a/solution.py
+++ b/solution.py
@@ -148,12 +148,26 @@
     refs[-1][...] = total
 
 
-def spread_kernel(early_ref, late_ref, base_ref, a_ref, b_ref, c_ref, out_ref):
-    total = base_ref[...] + a_ref[...] + b_ref[...] + c_ref[...]
-    pieces = early_ref[...] + late_ref[...]
-    for target in range(out_ref.shape[0]):
-        out_ref[target, :2] = total
-        out_ref[target, 2:] = pieces
+def spread_kernel(early_ref, late_ref, base_ref, a_ref, b_ref, c_ref, order_ref, out_ref, held, sems):
+    held[:2] = base_ref[...] + a_ref[...] + b_ref[...] + c_ref[...]
+    held[2:] = early_ref[...] + late_ref[...]
+    copies = [pltpu.make_async_copy(held, out_ref.at[t], sems.at[t]) for t in range(16)]
+    for copy in copies:
+        copy.start()
+    for copy in copies:
+        copy.wait()
+
+
+def spread_pieces(early, late, lead, sent, order):
+    return pl.pallas_call(
+        spread_kernel,
+        out_shape=jax.ShapeDtypeStruct((16, 4, 16, NB), jnp.float32),
+        in_specs=[pl.BlockSpec(memory_space=pltpu.VMEM)] * 6 + [pl.BlockSpec(memory_space=pl.ANY)],
+        out_specs=pl.BlockSpec(memory_space=pl.ANY),
+        scratch_shapes=[pltpu.VMEM((4, 16, NB), jnp.float32), pltpu.SemaphoreType.DMA((16,))],
+        compiler_params=pltpu.CompilerParams(vmem_limit_bytes=VMEM_LIMIT),
+        name="spread_kernel",
+    )(early, late, lead, *sent, order)
 
 
 def factors_kernel(right_ref, below_ref, inv0_ref, turned_ref, inv1_ref, x0_ref, x1_ref):
@@ -275,7 +289,7 @@
     panel = call(sum_kernel, kernel.shape, panel, along_z(panel, PANEL_TREE[0], True))
     late = lax.cond(waits, lambda t, l: scatter_rows(t), lambda t, l: no_rows(t), top, lead)
     sent = [along_z(lead, p) for p in PIECE_TREE[1]]
-    spread = call(spread_kernel, (16, 4, 16, NB), early, late, lead, *sent, order=(panel,))
+    spread = spread_pieces(early, late, lead, sent, panel)
     lead = lax.all_to_all(spread, "row", 0, 0)
     panel = call(sum_kernel, kernel.shape, panel, along_z(panel, PANEL_TREE[1], True), order=(spread,))
     swapped = swap_cores(call(pick_kernel, (16, 16, NB), lead, order=(panel,)), range(CHIPS_Z))

time: 84.5 us -> 84.6 us (level)
    pallas_call x0 -> x1, Pallas kernels: none -> 1.15 us  [spread_pieces(): pl.pallas_call(spread_kernel, out_shape=jax.ShapeDtypeStruct((16, 4, 16,...]
    pallas_call x13 -> x12, Pallas kernels: 21.1 us -> 19.9 us  [call(): pl.pallas_call(whole, out_shape=outs, in_specs=[pl.BlockSpec(memory_space...]
where the time goes in v8:
time: 84.6 us; the launch traced here: 84 us
  starting transfers between devices  38.5 us (46%)
  Pallas kernels  21.1 us (25%)
  blocking collectives  14.9 us (18%)
  waiting for transfers between devices  7.99 us (9%)
  local copies, waits for them, and re-layouts  0.98 us (1%)
    ppermute x10, starting transfers between devices, along_z(): return lax.ppermute(value, 'col', both_cores(pairs, mirror))  22.9 us
    pallas_call x12, Pallas kernels, call(): pl.pallas_call(whole, out_shape=outs, in_specs=[pl.BlockSpec(memory_space...  19.9 us
    all_to_all x1, blocking collectives, scatter_rows(): return lax.all_to_all(top.reshape(16, 16, NB), 'row', 0, 0)[:2]  14.9 us
    ppermute x3, starting transfers between devices, swap_cores(): lax.ppermute(value, 'col', [(2 * z + c, 2 * z + 1 - c) for z in chips for...  10.6 us
    ppermute x10, waiting for transfers between devices, along_z(): return lax.ppermute(value, 'col', both_cores(pairs, mirror))  4.04 us
    ppermute x1, waiting for transfers between devices, local(): lax.ppermute(first[0], 'col', [(0, 1)])  3.89 us
    all_to_all x1, starting transfers between devices, local(): lead = lax.all_to_all(spread, 'row', 0, 0)  3.66 us
  transfers between devices with their start and end apart: 15, of which 5 were waited for; matrix products, arithmetic and copies ran while one was open for 0% of the time, Pallas kernels for 21%

profile of v8, /device:TPU:1, one launch (start us, length us, event | category | flops | bytes accessed | tf_op | source)
XLA Modules:
  0.0 84.0 jit_solution(11788292577467500043)
XLA Ops:
  0.0 1.0 %slice.24 = f32[256,256]{1,0:T(8,128)S(1)} slice(f32[512,256]{1,0:T(8,128)} %refs_0_.1), slice={[0:256], [0:256]} | slice | bytes 524288 | tf_op jit(solution)/shard_map/slice | solution.py:275
  1.0 15.0 %conditional.3 = (f32[2,16,256]{2,1,0:T(8,128)S(1)}) conditional(s32[]{:T(128)} %convert_element_type.9, () %tuple.23, f32[256,256]{1,0:T(8,128)S(1)} %slice.24), branch_computations={%region_0.1_spmd, %region_1.2_spmd} | conditional | bytes 589832 | solution.py:280
  1.0 14.9 %all_to_all.17 = f32[16,16,256]{2,1,0:T(8,128)S(1)} all-to-all(f32[16,16,256]{2,1,0:T(8,128)S(1)} %bitcast.5), channel_id=1, replica_groups=mesh['row'=16,'col'=32] {'row'}, dimensions={0} | all-to-all | bytes 524288 | tf_op jit(solution)/shard_map/cond/branch_1_fun/all_to_all | solution.py:262
  15.9 1.4 %collective-permute-start = (f32[16,256]{1,0:T(8,128)S(1)}, f32[16,256]{1,0:T(8,128)S(1)}, u32[]{:S(2)}, u32[]{:S(2)}) collective-permute-start(f32[16,256]{1,0:T(8,128)S(1)} %slice_bitcast_fusion), channel_id=1, source_target_pairs={{0,1},{32,33},{64,65},{96,97},{128,129},{160,161},{192,193},{224,2... | collective-permute-start | bytes 49160 | tf_op jit(solution)/shard_map/ppermute | solution.py:281
  17.4 3.9 %collective-permute-done.refs_1_ = f32[16,256]{1,0:T(8,128)S(1)} collective-permute-done((f32[16,256]{1,0:T(8,128)S(1)}, f32[16,256]{1,0:T(8,128)S(1)}, u32[]{:S(2)}, u32[]{:S(2)}) %collective-permute-start) | collective-permute-done | bytes 16416 | tf_op jit(solution)/shard_map/ppermute | solution.py:281
  21.3 1.3 %collective-permute-start.3 = (f32[2,16,256]{2,1,0:T(8,128)S(1)}, f32[2,16,256]{2,1,0:T(8,128)S(1)}, u32[]{:S(2)}, u32[]{:S(2)}) collective-permute-start(f32[2,16,256]{2,1,0:T(8,128)S(1)} %lead_kernel.1.refs_0_), channel_id=1, source_target_pairs={{0,16},{1,17},{32,48},{33,49},{64,80},{65,81},{96,112},{97,113},{1... | collective-permute-start | bytes 98312 | tf_op jit(solution)/shard_map/ppermute | solution.py:270
  22.6 1.3 %collective-permute-start.2 = (f32[2,16,256]{2,1,0:T(8,128)S(1)}, f32[2,16,256]{2,1,0:T(8,128)S(1)}, u32[]{:S(2)}, u32[]{:S(2)}) collective-permute-start(f32[2,16,256]{2,1,0:T(8,128)S(1)} %lead_kernel.1.refs_0_), channel_id=1, source_target_pairs={{0,8},{1,9},{32,40},{33,41},{64,72},{65,73},{96,104},{97,105},{128... | collective-permute-start | bytes 98312 | tf_op jit(solution)/shard_map/ppermute | solution.py:270
  23.9 1.3 %collective-permute-start.1 = (f32[2,16,256]{2,1,0:T(8,128)S(1)}, f32[2,16,256]{2,1,0:T(8,128)S(1)}, u32[]{:S(2)}, u32[]{:S(2)}) collective-permute-start(f32[2,16,256]{2,1,0:T(8,128)S(1)} %lead_kernel.1.refs_0_), channel_id=1, source_target_pairs={{0,24},{1,25},{32,56},{33,57},{64,88},{65,89},{96,120},{97,121},{1... | collective-permute-start | bytes 98312 | tf_op jit(solution)/shard_map/ppermute | solution.py:270
  25.2 0.9 %collective-permute-done.1.refs_1_ = f32[2,16,256]{2,1,0:T(8,128)S(1)} collective-permute-done((f32[2,16,256]{2,1,0:T(8,128)S(1)}, f32[2,16,256]{2,1,0:T(8,128)S(1)}, u32[]{:S(2)}, u32[]{:S(2)}) %collective-permute-start.1) | collective-permute-done | bytes 32800 | tf_op jit(solution)/shard_map/ppermute | solution.py:270
  26.2 0.1 panel_kernel.1
  26.3 1.3 %collective-permute-start.4 = (f32[512,256]{1,0:T(8,128)S(1)}, f32[512,256]{1,0:T(8,128)S(1)}, u32[]{:S(2)}, u32[]{:S(2)}) collective-permute-start(f32[512,256]{1,0:T(8,128)S(1)} %get-tuple-element.27.refs_0_), channel_id=1, source_target_pairs={{0,14},{1,19},{32,46},{33,51},{64,78},{65,83},{96,110},{97,115},{1... | collective-permute-start | bytes 1572872 | tf_op jit(solution)/shard_map/ppermute | solution.py:270
  27.6 1.3 %collective-permute-start.8 = (f32[2,16,256]{2,1,0:T(8,128)S(1)}, f32[2,16,256]{2,1,0:T(8,128)S(1)}, u32[]{:S(2)}, u32[]{:S(2)}) collective-permute-start(f32[2,16,256]{2,1,0:T(8,128)S(1)} %sum_kernel.5.refs_1_.base_ref), channel_id=1, source_target_pairs={{0,4},{1,5},{8,12},{9,13},{16,20},{17,21},{24,28},{25,29},{32,36},... | collective-permute-start | bytes 98312 | tf_op jit(solution)/shard_map/ppermute | solution.py:270
  28.9 2.6 %collective-permute-start.7 = (f32[2,16,256]{2,1,0:T(8,128)S(1)}, f32[2,16,256]{2,1,0:T(8,128)S(1)}, u32[]{:S(2)}, u32[]{:S(2)}) collective-permute-start(f32[2,16,256]{2,1,0:T(8,128)S(1)} %sum_kernel.5.refs_1_.base_ref), channel_id=1, source_target_pairs={{0,30},{1,31},{8,6},{9,7},{16,14},{17,15},{24,22},{25,23},{32,62},... | collective-permute-start | bytes 98312 | tf_op jit(solution)/shard_map/ppermute | solution.py:270
  31.5 1.3 %collective-permute-start.6 = (f32[2,16,256]{2,1,0:T(8,128)S(1)}, f32[2,16,256]{2,1,0:T(8,128)S(1)}, u32[]{:S(2)}, u32[]{:S(2)}) collective-permute-start(f32[2,16,256]{2,1,0:T(8,128)S(1)} %sum_kernel.5.refs_1_.base_ref), channel_id=1, source_target_pairs={{0,2},{1,3},{8,10},{9,11},{16,18},{17,19},{24,26},{25,27},{32,34},... | collective-permute-start | bytes 98312 | tf_op jit(solution)/shard_map/ppermute | solution.py:270
  32.8 0.9 %collective-permute-done.4.refs_1_ = f32[512,256]{1,0:T(8,128)S(1)} collective-permute-done((f32[512,256]{1,0:T(8,128)S(1)}, f32[512,256]{1,0:T(8,128)S(1)}, u32[]{:S(2)}, u32[]{:S(2)}) %collective-permute-start.4) | collective-permute-done | bytes 524320 | tf_op jit(solution)/shard_map/ppermute | solution.py:270
  33.7 0.3 collective-permute-done.7.b_ref
  34.0 1.2 %spread_kernel.1.refs_2_ = f32[16,4,16,256]{3,2,1,0:T(8,128)} custom-call(f32[2,16,256]{2,1,0:T(8,128)S(1)} %get-tuple-element.35.refs_4_.early_ref, f32[2,16,256]{2,1,0:T(8,128)S(1)} %get-tuple-element.36.late_ref, f32[2,16,256]{2,1,0:T(8,128)S(1)} %sum_kernel.5.refs_1_.base_ref, f32[2,16,256]{2,1,0:T(8,128)S(1)} %collective-permute-done.6.a_ref, ...), custom_call_target="tpu_custom_call" | custom-call | tf_op jit(solution)/shard_map/spread_kernel/pallas_call | solution.py:162
  35.2 3.7 %all-to-all-start.3 = ((f32[16,4,16,256]{3,2,1,0:T(8,128)}), f32[16,4,16,256]{3,2,1,0:T(8,128)S(1)}, u32[]{:S(2)}, u32[]{:S(2)}) async-start(f32[16,4,16,256]{3,2,1,0:T(8,128)} %spread_kernel.1.refs_2_), calls=%async_computation.3 | async-start | bytes 2097152 | tf_op jit(solution)/shard_map/all_to_all | solution.py:293
  38.9 7.1 %collective-permute-start.5 = (f32[512,256]{1,0:T(8,128)S(1)}, f32[512,256]{1,0:T(8,128)S(1)}, u32[]{:S(2)}, u32[]{:S(2)}) collective-permute-start(f32[512,256]{1,0:T(8,128)S(1)} %sum_kernel.6.order_ref.refs_0_), channel_id=1, source_target_pairs={{0,8},{1,25},{14,22},{19,11},{32,40},{33,57},{46,54},{51,43},{64,7... | collective-permute-start | bytes 1572872 | tf_op jit(solution)/shard_map/ppermute | solution.py:270
  46.0 4.2 %collective-permute-start.10 = (f32[512,256]{1,0:T(8,128)S(1)}, f32[512,256]{1,0:T(8,128)S(1)}, u32[]{:S(2)}, u32[]{:S(2)}) collective-permute-start(f32[512,256]{1,0:T(8,128)S(1)} %get-tuple-element.26.refs_0_), channel_id=1, source_target_pairs={{0,1},{1,0},{32,33},{33,32},{64,65},{65,64},{96,97},{97,96},{128,1... | collective-permute-start | bytes 1572872 | tf_op jit(solution)/shard_map/ppermute | solution.py:258
  50.2 1.9 %collective-permute-done.5.refs_1_ = f32[512,256]{1,0:T(8,128)S(1)} collective-permute-done((f32[512,256]{1,0:T(8,128)S(1)}, f32[512,256]{1,0:T(8,128)S(1)}, u32[]{:S(2)}, u32[]{:S(2)}) %collective-permute-start.5) | collective-permute-done | bytes 524320 | tf_op jit(solution)/shard_map/ppermute | solution.py:270
  52.1 0.1 sum_kernel.7.refs_1_.refs_0_
  52.1 1.3 %collective-permute-start.9 = (f32[512,256]{1,0:T(8,128)S(1)}, f32[512,256]{1,0:T(8,128)S(1)}, u32[]{:S(2)}, u32[]{:S(2)}) collective-permute-start(f32[512,256]{1,0:T(8,128)S(1)} %sum_kernel.7.refs_1_.refs_0_), channel_id=1, source_target_pairs={{0,4},{1,29},{8,12},{25,21},{14,18},{19,15},{22,26},{11,7},{32,36}... | collective-permute-start | bytes 1572872 | tf_op jit(solution)/shard_map/ppermute | solution.py:270
  53.5 5.7 %collective-permute-start.12 = (f32[16,16,256]{2,1,0:T(8,128)S(1)}, f32[16,16,256]{2,1,0:T(8,128)S(1)}, u32[]{:S(2)}, u32[]{:S(2)}) collective-permute-start(f32[16,16,256]{2,1,0:T(8,128)S(1)} %pick_kernel.1), channel_id=1, source_target_pairs={{0,1},{1,0},{2,3},{3,2},{4,5},{5,4},{6,7},{7,6},{8,9},{9,8},{10,11... | collective-permute-start | bytes 786440 | tf_op jit(solution)/shard_map/ppermute | solution.py:258
  59.3 8.0 %first_kernel.1.refs_2_.refs_0_ = f32[256,256]{1,0:T(8,128)S(1)} custom-call(f32[16,4,16,256]{3,2,1,0:T(8,128)S(1)} %all-to-all-done.3.refs_0_.refs_1_, f32[512,256]{1,0:T(8,128)S(1)} %sum_kernel.7.refs_1_.refs_0_, f32[512,256]{1,0:T(8,128)S(1)} %collective-permute-done.10.refs_2_.refs_5_), custom_call_target="tpu_custom_call" | custom-call | flops 10000000000 | tf_op jit(solution)/shard_map/first_kernel/pallas_call | solution.py:236
  67.3 0.1 sum_kernel.8.refs_3_.refs_0_
  67.4 4.1 %collective-permute-start.11 = (f32[512,256]{1,0:T(8,128)S(1)}, f32[512,256]{1,0:T(8,128)S(1)}, u32[]{:S(2)}, u32[]{:S(2)}) collective-permute-start(f32[512,256]{1,0:T(8,128)S(1)} %sum_kernel.8.refs_3_.refs_0_), channel_id=1, source_target_pairs={{0,30},{1,3},{4,2},{29,31},{8,6},{25,27},{12,10},{21,23},{14,16},{... | collective-permute-start | bytes 1572872 | tf_op jit(solution)/shard_map/ppermute | solution.py:270
  71.5 8.8 %second_kernel.1 = (f32[256,256]{1,0:T(8,128)S(1)}, f32[256,256]{1,0:T(8,128)S(1)}, f32[256,256]{1,0:T(8,128)S(1)}, f32[256,256]{1,0:T(8,128)S(1)}) custom-call(f32[256,256]{1,0:T(8,128)S(1)} %first_kernel.1.refs_2_.refs_0_, f32[16,4,16,256]{3,2,1,0:T(8,128)S(1)} %all-to-all-done.3.refs_0_.refs_1_, f32[16,16,256]{2,1,0:T(8,128)S(1)} %collective-permute-done.12.refs_2_, ...), custom_call_target="tpu_custom_call" | custom-call | flops 10000000000 | tf_op jit(solution)/shard_map/second_kernel/pallas_call | solution.py:236
  80.3 0.1 sum_kernel.9.refs_5_.refs_1_
  80.4 0.7 collective-permute-start.13
  81.1 0.8 factors_kernel.1
  81.9 2.0 %final_kernel.1 = f32[512,256]{1,0:T(8,128)} custom-call(f32[512,256]{1,0:T(8,128)S(1)} %get-tuple-element.26.refs_0_, f32[512,256]{1,0:T(8,128)S(1)} %sum_kernel.9.refs_5_.refs_1_, f32[512,256]{1,0:T(8,128)S(1)} %collective-permute-done.13.refs_2_, f32[256,256]{1,0:T(8,128)S(1)} %get-tuple-element.32.refs_3_, f32[256,256]{1,0:T(8,128)S(1)} %get-tuple-element.33.refs_4_, ...), custom_call_target="tpu_custom_call" | custom-call | tf_op jit(solution)/shard_map/final_kernel/pallas_call | solution.py:236
  (22 shorter events, 0.3 us)
Async XLA Ops:
  15.9 10.2 %copy-start = (f32[512,256]{1,0:T(8,128)S(1)}, f32[512,256]{1,0:T(8,128)}, u32[]{:S(2)}) copy-start(f32[512,256]{1,0:T(8,128)} %refs_0_.1) | copy-start | bytes 1572868
  15.9 5.3 %collective-permute-start = (f32[16,256]{1,0:T(8,128)S(1)}, f32[16,256]{1,0:T(8,128)S(1)}, u32[]{:S(2)}, u32[]{:S(2)}) collective-permute-start(f32[16,256]{1,0:T(8,128)S(1)} %slice_bitcast_fusion), channel_id=1, source_target_pairs={{0,1},{32,33},{64,65},{96,97},{128,129},{160,161},{192,193},{224,2... | collective-permute-start | bytes 49160 | tf_op jit(solution)/shard_map/ppermute | solution.py:281
  21.3 3.9 %collective-permute-start.3 = (f32[2,16,256]{2,1,0:T(8,128)S(1)}, f32[2,16,256]{2,1,0:T(8,128)S(1)}, u32[]{:S(2)}, u32[]{:S(2)}) collective-permute-start(f32[2,16,256]{2,1,0:T(8,128)S(1)} %lead_kernel.1.refs_0_), channel_id=1, source_target_pairs={{0,16},{1,17},{32,48},{33,49},{64,80},{65,81},{96,112},{97,113},{1... | collective-permute-start | bytes 98312 | tf_op jit(solution)/shard_map/ppermute | solution.py:270
  22.6 2.7 %collective-permute-start.2 = (f32[2,16,256]{2,1,0:T(8,128)S(1)}, f32[2,16,256]{2,1,0:T(8,128)S(1)}, u32[]{:S(2)}, u32[]{:S(2)}) collective-permute-start(f32[2,16,256]{2,1,0:T(8,128)S(1)} %lead_kernel.1.refs_0_), channel_id=1, source_target_pairs={{0,8},{1,9},{32,40},{33,41},{64,72},{65,73},{96,104},{97,105},{128... | collective-permute-start | bytes 98312 | tf_op jit(solution)/shard_map/ppermute | solution.py:270
  23.9 2.3 %collective-permute-start.1 = (f32[2,16,256]{2,1,0:T(8,128)S(1)}, f32[2,16,256]{2,1,0:T(8,128)S(1)}, u32[]{:S(2)}, u32[]{:S(2)}) collective-permute-start(f32[2,16,256]{2,1,0:T(8,128)S(1)} %lead_kernel.1.refs_0_), channel_id=1, source_target_pairs={{0,24},{1,25},{32,56},{33,57},{64,88},{65,89},{96,120},{97,121},{1... | collective-permute-start | bytes 98312 | tf_op jit(solution)/shard_map/ppermute | solution.py:270
  26.3 7.4 %collective-permute-start.4 = (f32[512,256]{1,0:T(8,128)S(1)}, f32[512,256]{1,0:T(8,128)S(1)}, u32[]{:S(2)}, u32[]{:S(2)}) collective-permute-start(f32[512,256]{1,0:T(8,128)S(1)} %get-tuple-element.27.refs_0_), channel_id=1, source_target_pairs={{0,14},{1,19},{32,46},{33,51},{64,78},{65,83},{96,110},{97,115},{1... | collective-permute-start | bytes 1572872 | tf_op jit(solution)/shard_map/ppermute | solution.py:270
  27.6 6.1 %collective-permute-start.8 = (f32[2,16,256]{2,1,0:T(8,128)S(1)}, f32[2,16,256]{2,1,0:T(8,128)S(1)}, u32[]{:S(2)}, u32[]{:S(2)}) collective-permute-start(f32[2,16,256]{2,1,0:T(8,128)S(1)} %sum_kernel.5.refs_1_.base_ref), channel_id=1, source_target_pairs={{0,4},{1,5},{8,12},{9,13},{16,20},{17,21},{24,28},{25,29},{32,36},... | collective-permute-start | bytes 98312 | tf_op jit(solution)/shard_map/ppermute | solution.py:270
  28.9 5.1 %collective-permute-start.7 = (f32[2,16,256]{2,1,0:T(8,128)S(1)}, f32[2,16,256]{2,1,0:T(8,128)S(1)}, u32[]{:S(2)}, u32[]{:S(2)}) collective-permute-start(f32[2,16,256]{2,1,0:T(8,128)S(1)} %sum_kernel.5.refs_1_.base_ref), channel_id=1, source_target_pairs={{0,30},{1,31},{8,6},{9,7},{16,14},{17,15},{24,22},{25,23},{32,62},... | collective-permute-start | bytes 98312 | tf_op jit(solution)/shard_map/ppermute | solution.py:270
  31.5 2.6 %collective-permute-start.6 = (f32[2,16,256]{2,1,0:T(8,128)S(1)}, f32[2,16,256]{2,1,0:T(8,128)S(1)}, u32[]{:S(2)}, u32[]{:S(2)}) collective-permute-start(f32[2,16,256]{2,1,0:T(8,128)S(1)} %sum_kernel.5.refs_1_.base_ref), channel_id=1, source_target_pairs={{0,2},{1,3},{8,10},{9,11},{16,18},{17,19},{24,26},{25,27},{32,34},... | collective-permute-start | bytes 98312 | tf_op jit(solution)/shard_map/ppermute | solution.py:270
  35.2 18.3 %all-to-all-start.3 = ((f32[16,4,16,256]{3,2,1,0:T(8,128)}), f32[16,4,16,256]{3,2,1,0:T(8,128)S(1)}, u32[]{:S(2)}, u32[]{:S(2)}) async-start(f32[16,4,16,256]{3,2,1,0:T(8,128)} %spread_kernel.1.refs_2_), calls=%async_computation.3 | async-start | bytes 2097152 | tf_op jit(solution)/shard_map/all_to_all | solution.py:293
  38.9 13.2 %collective-permute-start.5 = (f32[512,256]{1,0:T(8,128)S(1)}, f32[512,256]{1,0:T(8,128)S(1)}, u32[]{:S(2)}, u32[]{:S(2)}) collective-permute-start(f32[512,256]{1,0:T(8,128)S(1)} %sum_kernel.6.order_ref.refs_0_), channel_id=1, source_target_pairs={{0,8},{1,25},{14,22},{19,11},{32,40},{33,57},{46,54},{51,43},{64,7... | collective-permute-start | bytes 1572872 | tf_op jit(solution)/shard_map/ppermute | solution.py:270
  46.0 13.3 %collective-permute-start.10 = (f32[512,256]{1,0:T(8,128)S(1)}, f32[512,256]{1,0:T(8,128)S(1)}, u32[]{:S(2)}, u32[]{:S(2)}) collective-permute-start(f32[512,256]{1,0:T(8,128)S(1)} %get-tuple-element.26.refs_0_), channel_id=1, source_target_pairs={{0,1},{1,0},{32,33},{33,32},{64,65},{65,64},{96,97},{97,96},{128,1... | collective-permute-start | bytes 1572872 | tf_op jit(solution)/shard_map/ppermute | solution.py:258
  52.1 15.2 %collective-permute-start.9 = (f32[512,256]{1,0:T(8,128)S(1)}, f32[512,256]{1,0:T(8,128)S(1)}, u32[]{:S(2)}, u32[]{:S(2)}) collective-permute-start(f32[512,256]{1,0:T(8,128)S(1)} %sum_kernel.7.refs_1_.refs_0_), channel_id=1, source_target_pairs={{0,4},{1,29},{8,12},{25,21},{14,18},{19,15},{22,26},{11,7},{32,36}... | collective-permute-start | bytes 1572872 | tf_op jit(solution)/shard_map/ppermute | solution.py:270
  53.5 17.9 %collective-permute-start.12 = (f32[16,16,256]{2,1,0:T(8,128)S(1)}, f32[16,16,256]{2,1,0:T(8,128)S(1)}, u32[]{:S(2)}, u32[]{:S(2)}) collective-permute-start(f32[16,16,256]{2,1,0:T(8,128)S(1)} %pick_kernel.1), channel_id=1, source_target_pairs={{0,1},{1,0},{2,3},{3,2},{4,5},{5,4},{6,7},{7,6},{8,9},{9,8},{10,11... | collective-permute-start | bytes 786440 | tf_op jit(solution)/shard_map/ppermute | solution.py:258
  67.4 12.9 %collective-permute-start.11 = (f32[512,256]{1,0:T(8,128)S(1)}, f32[512,256]{1,0:T(8,128)S(1)}, u32[]{:S(2)}, u32[]{:S(2)}) collective-permute-start(f32[512,256]{1,0:T(8,128)S(1)} %sum_kernel.8.refs_3_.refs_0_), channel_id=1, source_target_pairs={{0,30},{1,3},{4,2},{29,31},{8,6},{25,27},{12,10},{21,23},{14,16},{... | collective-permute-start | bytes 1572872 | tf_op jit(solution)/shard_map/ppermute | solution.py:270
  80.4 1.5 %collective-permute-start.13 = (f32[512,256]{1,0:T(8,128)S(1)}, f32[512,256]{1,0:T(8,128)S(1)}, u32[]{:S(2)}, u32[]{:S(2)}) collective-permute-start(f32[512,256]{1,0:T(8,128)S(1)} %sum_kernel.9.refs_5_.refs_1_), channel_id=1, source_target_pairs={{2,3},{3,2},{4,5},{5,4},{6,7},{7,6},{8,9},{9,8},{10,11},{11,10},{1... | collective-permute-start | bytes 1572872 | tf_op jit(solution)/shard_map/ppermute | solution.py:258

commit v9 on v8

--- a/solution.py
+++ b/solution.py
@@ -15,8 +15,8 @@
 PANEL_TREE = (
     ((0, 7),),
     ((0, 4), (7, 11)),
-    ((0, 2), (4, 6), (7, 9), (11, 13)),
-    ((0, 15), (2, 1), (4, 3), (6, 5), (7, 8), (9, 10), (11, 12), (13, 14)),
+    ((0, 2), (7, 6), (4, 8), (11, 13)),
+    ((0, 15), (2, 1), (4, 3), (6, 5), (7, 10), (8, 9), (11, 12), (13, 14)),
 )
 PIECE_TREE = (
     (((0, 12),), ((0, 4),), ((0, 8),)),

time: 84.6 us -> 84.6 us (level)
  no operation moved by 1% of the time
where the time goes in v9:
time: 84.6 us; the launch traced here: 84 us
  starting transfers between devices  38.5 us (46%)
  Pallas kernels  21.1 us (25%)
  blocking collectives  14.9 us (18%)
  waiting for transfers between devices  7.99 us (9%)
  local copies, waits for them, and re-layouts  0.98 us (1%)
    ppermute x10, starting transfers between devices, along_z(): return lax.ppermute(value, 'col', both_cores(pairs, mirror))  22.9 us
    pallas_call x12, Pallas kernels, call(): pl.pallas_call(whole, out_shape=outs, in_specs=[pl.BlockSpec(memory_space...  19.9 us
    all_to_all x1, blocking collectives, scatter_rows(): return lax.all_to_all(top.reshape(16, 16, NB), 'row', 0, 0)[:2]  14.9 us
    ppermute x3, starting transfers between devices, swap_cores(): lax.ppermute(value, 'col', [(2 * z + c, 2 * z + 1 - c) for z in chips for...  10.6 us
    ppermute x10, waiting for transfers between devices, along_z(): return lax.ppermute(value, 'col', both_cores(pairs, mirror))  4.04 us
    ppermute x1, waiting for transfers between devices, local(): lax.ppermute(first[0], 'col', [(0, 1)])  3.89 us
    all_to_all x1, starting transfers between devices, local(): lead = lax.all_to_all(spread, 'row', 0, 0)  3.66 us
  transfers between devices with their start and end apart: 15, of which 5 were waited for; matrix products, arithmetic and copies ran while one was open for 0% of the time, Pallas kernels for 21%

profile of v9, /device:TPU:1, one launch (start us, length us, event | category | flops | bytes accessed | tf_op | source)
XLA Modules:
  0.0 84.0 jit_solution(9958153751959300131)
XLA Ops:
  0.0 1.0 %slice.24 = f32[256,256]{1,0:T(8,128)S(1)} slice(f32[512,256]{1,0:T(8,128)} %refs_0_.1), slice={[0:256], [0:256]} | slice | bytes 524288 | tf_op jit(solution)/shard_map/slice | solution.py:275
  1.0 15.0 %conditional.3 = (f32[2,16,256]{2,1,0:T(8,128)S(1)}) conditional(s32[]{:T(128)} %convert_element_type.9, () %tuple.23, f32[256,256]{1,0:T(8,128)S(1)} %slice.24), branch_computations={%region_0.1_spmd, %region_1.2_spmd} | conditional | bytes 589832 | solution.py:280
  1.0 14.9 %all_to_all.17 = f32[16,16,256]{2,1,0:T(8,128)S(1)} all-to-all(f32[16,16,256]{2,1,0:T(8,128)S(1)} %bitcast.5), channel_id=1, replica_groups=mesh['row'=16,'col'=32] {'row'}, dimensions={0} | all-to-all | bytes 524288 | tf_op jit(solution)/shard_map/cond/branch_1_fun/all_to_all | solution.py:262
  15.9 1.4 %collective-permute-start = (f32[16,256]{1,0:T(8,128)S(1)}, f32[16,256]{1,0:T(8,128)S(1)}, u32[]{:S(2)}, u32[]{:S(2)}) collective-permute-start(f32[16,256]{1,0:T(8,128)S(1)} %slice_bitcast_fusion), channel_id=1, source_target_pairs={{0,1},{32,33},{64,65},{96,97},{128,129},{160,161},{192,193},{224,2... | collective-permute-start | bytes 49160 | tf_op jit(solution)/shard_map/ppermute | solution.py:281
  17.4 3.9 %collective-permute-done.refs_1_ = f32[16,256]{1,0:T(8,128)S(1)} collective-permute-done((f32[16,256]{1,0:T(8,128)S(1)}, f32[16,256]{1,0:T(8,128)S(1)}, u32[]{:S(2)}, u32[]{:S(2)}) %collective-permute-start) | collective-permute-done | bytes 16416 | tf_op jit(solution)/shard_map/ppermute | solution.py:281
  21.3 1.3 %collective-permute-start.3 = (f32[2,16,256]{2,1,0:T(8,128)S(1)}, f32[2,16,256]{2,1,0:T(8,128)S(1)}, u32[]{:S(2)}, u32[]{:S(2)}) collective-permute-start(f32[2,16,256]{2,1,0:T(8,128)S(1)} %lead_kernel.1.refs_0_), channel_id=1, source_target_pairs={{0,16},{1,17},{32,48},{33,49},{64,80},{65,81},{96,112},{97,113},{1... | collective-permute-start | bytes 98312 | tf_op jit(solution)/shard_map/ppermute | solution.py:270
  22.6 1.3 %collective-permute-start.2 = (f32[2,16,256]{2,1,0:T(8,128)S(1)}, f32[2,16,256]{2,1,0:T(8,128)S(1)}, u32[]{:S(2)}, u32[]{:S(2)}) collective-permute-start(f32[2,16,256]{2,1,0:T(8,128)S(1)} %lead_kernel.1.refs_0_), channel_id=1, source_target_pairs={{0,8},{1,9},{32,40},{33,41},{64,72},{65,73},{96,104},{97,105},{128... | collective-permute-start | bytes 98312 | tf_op jit(solution)/shard_map/ppermute | solution.py:270
  23.9 1.3 %collective-permute-start.1 = (f32[2,16,256]{2,1,0:T(8,128)S(1)}, f32[2,16,256]{2,1,0:T(8,128)S(1)}, u32[]{:S(2)}, u32[]{:S(2)}) collective-permute-start(f32[2,16,256]{2,1,0:T(8,128)S(1)} %lead_kernel.1.refs_0_), channel_id=1, source_target_pairs={{0,24},{1,25},{32,56},{33,57},{64,88},{65,89},{96,120},{97,121},{1... | collective-permute-start | bytes 98312 | tf_op jit(solution)/shard_map/ppermute | solution.py:270
  25.2 0.9 %collective-permute-done.1.refs_1_ = f32[2,16,256]{2,1,0:T(8,128)S(1)} collective-permute-done((f32[2,16,256]{2,1,0:T(8,128)S(1)}, f32[2,16,256]{2,1,0:T(8,128)S(1)}, u32[]{:S(2)}, u32[]{:S(2)}) %collective-permute-start.1) | collective-permute-done | bytes 32800 | tf_op jit(solution)/shard_map/ppermute | solution.py:270
  26.2 0.1 panel_kernel.1
  26.3 1.3 %collective-permute-start.4 = (f32[512,256]{1,0:T(8,128)S(1)}, f32[512,256]{1,0:T(8,128)S(1)}, u32[]{:S(2)}, u32[]{:S(2)}) collective-permute-start(f32[512,256]{1,0:T(8,128)S(1)} %get-tuple-element.27.refs_0_), channel_id=1, source_target_pairs={{0,14},{1,19},{32,46},{33,51},{64,78},{65,83},{96,110},{97,115},{1... | collective-permute-start | bytes 1572872 | tf_op jit(solution)/shard_map/ppermute | solution.py:270
  27.6 1.3 %collective-permute-start.8 = (f32[2,16,256]{2,1,0:T(8,128)S(1)}, f32[2,16,256]{2,1,0:T(8,128)S(1)}, u32[]{:S(2)}, u32[]{:S(2)}) collective-permute-start(f32[2,16,256]{2,1,0:T(8,128)S(1)} %sum_kernel.5.refs_1_.base_ref), channel_id=1, source_target_pairs={{0,4},{1,5},{8,12},{9,13},{16,20},{17,21},{24,28},{25,29},{32,36},... | collective-permute-start | bytes 98312 | tf_op jit(solution)/shard_map/ppermute | solution.py:270
  28.9 2.6 %collective-permute-start.7 = (f32[2,16,256]{2,1,0:T(8,128)S(1)}, f32[2,16,256]{2,1,0:T(8,128)S(1)}, u32[]{:S(2)}, u32[]{:S(2)}) collective-permute-start(f32[2,16,256]{2,1,0:T(8,128)S(1)} %sum_kernel.5.refs_1_.base_ref), channel_id=1, source_target_pairs={{0,30},{1,31},{8,6},{9,7},{16,14},{17,15},{24,22},{25,23},{32,62},... | collective-permute-start | bytes 98312 | tf_op jit(solution)/shard_map/ppermute | solution.py:270
  31.5 1.3 %collective-permute-start.6 = (f32[2,16,256]{2,1,0:T(8,128)S(1)}, f32[2,16,256]{2,1,0:T(8,128)S(1)}, u32[]{:S(2)}, u32[]{:S(2)}) collective-permute-start(f32[2,16,256]{2,1,0:T(8,128)S(1)} %sum_kernel.5.refs_1_.base_ref), channel_id=1, source_target_pairs={{0,2},{1,3},{8,10},{9,11},{16,18},{17,19},{24,26},{25,27},{32,34},... | collective-permute-start | bytes 98312 | tf_op jit(solution)/shard_map/ppermute | solution.py:270
  32.8 0.9 %collective-permute-done.4.refs_1_ = f32[512,256]{1,0:T(8,128)S(1)} collective-permute-done((f32[512,256]{1,0:T(8,128)S(1)}, f32[512,256]{1,0:T(8,128)S(1)}, u32[]{:S(2)}, u32[]{:S(2)}) %collective-permute-start.4) | collective-permute-done | bytes 524320 | tf_op jit(solution)/shard_map/ppermute | solution.py:270
  33.7 0.1 sum_kernel.6.order_ref.refs_0_
  33.7 0.3 collective-permute-done.7.b_ref
  34.0 1.2 %spread_kernel.1.refs_2_ = f32[16,4,16,256]{3,2,1,0:T(8,128)} custom-call(f32[2,16,256]{2,1,0:T(8,128)S(1)} %get-tuple-element.35.refs_4_.early_ref, f32[2,16,256]{2,1,0:T(8,128)S(1)} %get-tuple-element.36.late_ref, f32[2,16,256]{2,1,0:T(8,128)S(1)} %sum_kernel.5.refs_1_.base_ref, f32[2,16,256]{2,1,0:T(8,128)S(1)} %collective-permute-done.6.a_ref, ...), custom_call_target="tpu_custom_call" | custom-call | tf_op jit(solution)/shard_map/spread_kernel/pallas_call | solution.py:162
  35.2 3.7 %all-to-all-start.3 = ((f32[16,4,16,256]{3,2,1,0:T(8,128)}), f32[16,4,16,256]{3,2,1,0:T(8,128)S(1)}, u32[]{:S(2)}, u32[]{:S(2)}) async-start(f32[16,4,16,256]{3,2,1,0:T(8,128)} %spread_kernel.1.refs_2_), calls=%async_computation.3 | async-start | bytes 2097152 | tf_op jit(solution)/shard_map/all_to_all | solution.py:293
  38.9 7.1 %collective-permute-start.5 = (f32[512,256]{1,0:T(8,128)S(1)}, f32[512,256]{1,0:T(8,128)S(1)}, u32[]{:S(2)}, u32[]{:S(2)}) collective-permute-start(f32[512,256]{1,0:T(8,128)S(1)} %sum_kernel.6.order_ref.refs_0_), channel_id=1, source_target_pairs={{0,8},{1,25},{14,22},{19,11},{32,40},{33,57},{46,54},{51,43},{64,7... | collective-permute-start | bytes 1572872 | tf_op jit(solution)/shard_map/ppermute | solution.py:270
  46.0 4.2 %collective-permute-start.10 = (f32[512,256]{1,0:T(8,128)S(1)}, f32[512,256]{1,0:T(8,128)S(1)}, u32[]{:S(2)}, u32[]{:S(2)}) collective-permute-start(f32[512,256]{1,0:T(8,128)S(1)} %get-tuple-element.26.refs_0_), channel_id=1, source_target_pairs={{0,1},{1,0},{32,33},{33,32},{64,65},{65,64},{96,97},{97,96},{128,1... | collective-permute-start | bytes 1572872 | tf_op jit(solution)/shard_map/ppermute | solution.py:258
  50.2 1.9 %collective-permute-done.5.refs_1_ = f32[512,256]{1,0:T(8,128)S(1)} collective-permute-done((f32[512,256]{1,0:T(8,128)S(1)}, f32[512,256]{1,0:T(8,128)S(1)}, u32[]{:S(2)}, u32[]{:S(2)}) %collective-permute-start.5) | collective-permute-done | bytes 524320 | tf_op jit(solution)/shard_map/ppermute | solution.py:270
  52.1 1.3 %collective-permute-start.9 = (f32[512,256]{1,0:T(8,128)S(1)}, f32[512,256]{1,0:T(8,128)S(1)}, u32[]{:S(2)}, u32[]{:S(2)}) collective-permute-start(f32[512,256]{1,0:T(8,128)S(1)} %sum_kernel.7.refs_1_.refs_0_), channel_id=1, source_target_pairs={{0,4},{1,29},{14,12},{19,21},{8,16},{25,17},{22,26},{11,7},{32,36}... | collective-permute-start | bytes 1572872 | tf_op jit(solution)/shard_map/ppermute | solution.py:270
  53.5 5.7 %collective-permute-start.12 = (f32[16,16,256]{2,1,0:T(8,128)S(1)}, f32[16,16,256]{2,1,0:T(8,128)S(1)}, u32[]{:S(2)}, u32[]{:S(2)}) collective-permute-start(f32[16,16,256]{2,1,0:T(8,128)S(1)} %pick_kernel.1), channel_id=1, source_target_pairs={{0,1},{1,0},{2,3},{3,2},{4,5},{5,4},{6,7},{7,6},{8,9},{9,8},{10,11... | collective-permute-start | bytes 786440 | tf_op jit(solution)/shard_map/ppermute | solution.py:258
  59.3 8.0 %first_kernel.1.refs_2_.refs_0_ = f32[256,256]{1,0:T(8,128)S(1)} custom-call(f32[16,4,16,256]{3,2,1,0:T(8,128)S(1)} %all-to-all-done.3.refs_0_.refs_1_, f32[512,256]{1,0:T(8,128)S(1)} %sum_kernel.7.refs_1_.refs_0_, f32[512,256]{1,0:T(8,128)S(1)} %collective-permute-done.10.refs_2_.refs_5_), custom_call_target="tpu_custom_call" | custom-call | flops 10000000000 | tf_op jit(solution)/shard_map/first_kernel/pallas_call | solution.py:236
  67.3 0.1 sum_kernel.8.refs_3_.refs_0_
  67.4 4.1 %collective-permute-start.11 = (f32[512,256]{1,0:T(8,128)S(1)}, f32[512,256]{1,0:T(8,128)S(1)}, u32[]{:S(2)}, u32[]{:S(2)}) collective-permute-start(f32[512,256]{1,0:T(8,128)S(1)} %sum_kernel.8.refs_3_.refs_0_), channel_id=1, source_target_pairs={{0,30},{1,3},{4,2},{29,31},{8,6},{25,27},{12,10},{21,23},{14,20},{... | collective-permute-start | bytes 1572872 | tf_op jit(solution)/shard_map/ppermute | solution.py:270
  71.5 8.8 %second_kernel.1 = (f32[256,256]{1,0:T(8,128)S(1)}, f32[256,256]{1,0:T(8,128)S(1)}, f32[256,256]{1,0:T(8,128)S(1)}, f32[256,256]{1,0:T(8,128)S(1)}) custom-call(f32[256,256]{1,0:T(8,128)S(1)} %first_kernel.1.refs_2_.refs_0_, f32[16,4,16,256]{3,2,1,0:T(8,128)S(1)} %all-to-all-done.3.refs_0_.refs_1_, f32[16,16,256]{2,1,0:T(8,128)S(1)} %collective-permute-done.12.refs_2_, ...), custom_call_target="tpu_custom_call" | custom-call | flops 10000000000 | tf_op jit(solution)/shard_map/second_kernel/pallas_call | solution.py:236
  80.3 0.1 sum_kernel.9.refs_5_.refs_1_
  80.4 0.7 collective-permute-start.13
  81.1 0.8 factors_kernel.1
  81.9 2.0 %final_kernel.1 = f32[512,256]{1,0:T(8,128)} custom-call(f32[512,256]{1,0:T(8,128)S(1)} %get-tuple-element.26.refs_0_, f32[512,256]{1,0:T(8,128)S(1)} %sum_kernel.9.refs_5_.refs_1_, f32[512,256]{1,0:T(8,128)S(1)} %collective-permute-done.13.refs_2_, f32[256,256]{1,0:T(8,128)S(1)} %get-tuple-element.32.refs_3_, f32[256,256]{1,0:T(8,128)S(1)} %get-tuple-element.33.refs_4_, ...), custom_call_target="tpu_custom_call" | custom-call | tf_op jit(solution)/shard_map/final_kernel/pallas_call | solution.py:236
  (22 shorter events, 0.3 us)
Async XLA Ops:
  15.9 10.2 %copy-start = (f32[512,256]{1,0:T(8,128)S(1)}, f32[512,256]{1,0:T(8,128)}, u32[]{:S(2)}) copy-start(f32[512,256]{1,0:T(8,128)} %refs_0_.1) | copy-start | bytes 1572868
  15.9 5.3 %collective-permute-start = (f32[16,256]{1,0:T(8,128)S(1)}, f32[16,256]{1,0:T(8,128)S(1)}, u32[]{:S(2)}, u32[]{:S(2)}) collective-permute-start(f32[16,256]{1,0:T(8,128)S(1)} %slice_bitcast_fusion), channel_id=1, source_target_pairs={{0,1},{32,33},{64,65},{96,97},{128,129},{160,161},{192,193},{224,2... | collective-permute-start | bytes 49160 | tf_op jit(solution)/shard_map/ppermute | solution.py:281
  21.3 3.9 %collective-permute-start.3 = (f32[2,16,256]{2,1,0:T(8,128)S(1)}, f32[2,16,256]{2,1,0:T(8,128)S(1)}, u32[]{:S(2)}, u32[]{:S(2)}) collective-permute-start(f32[2,16,256]{2,1,0:T(8,128)S(1)} %lead_kernel.1.refs_0_), channel_id=1, source_target_pairs={{0,16},{1,17},{32,48},{33,49},{64,80},{65,81},{96,112},{97,113},{1... | collective-permute-start | bytes 98312 | tf_op jit(solution)/shard_map/ppermute | solution.py:270
  22.6 2.7 %collective-permute-start.2 = (f32[2,16,256]{2,1,0:T(8,128)S(1)}, f32[2,16,256]{2,1,0:T(8,128)S(1)}, u32[]{:S(2)}, u32[]{:S(2)}) collective-permute-start(f32[2,16,256]{2,1,0:T(8,128)S(1)} %lead_kernel.1.refs_0_), channel_id=1, source_target_pairs={{0,8},{1,9},{32,40},{33,41},{64,72},{65,73},{96,104},{97,105},{128... | collective-permute-start | bytes 98312 | tf_op jit(solution)/shard_map/ppermute | solution.py:270
  23.9 2.3 %collective-permute-start.1 = (f32[2,16,256]{2,1,0:T(8,128)S(1)}, f32[2,16,256]{2,1,0:T(8,128)S(1)}, u32[]{:S(2)}, u32[]{:S(2)}) collective-permute-start(f32[2,16,256]{2,1,0:T(8,128)S(1)} %lead_kernel.1.refs_0_), channel_id=1, source_target_pairs={{0,24},{1,25},{32,56},{33,57},{64,88},{65,89},{96,120},{97,121},{1... | collective-permute-start | bytes 98312 | tf_op jit(solution)/shard_map/ppermute | solution.py:270
  26.3 7.4 %collective-permute-start.4 = (f32[512,256]{1,0:T(8,128)S(1)}, f32[512,256]{1,0:T(8,128)S(1)}, u32[]{:S(2)}, u32[]{:S(2)}) collective-permute-start(f32[512,256]{1,0:T(8,128)S(1)} %get-tuple-element.27.refs_0_), channel_id=1, source_target_pairs={{0,14},{1,19},{32,46},{33,51},{64,78},{65,83},{96,110},{97,115},{1... | collective-permute-start | bytes 1572872 | tf_op jit(solution)/shard_map/ppermute | solution.py:270
  27.6 6.1 %collective-permute-start.8 = (f32[2,16,256]{2,1,0:T(8,128)S(1)}, f32[2,16,256]{2,1,0:T(8,128)S(1)}, u32[]{:S(2)}, u32[]{:S(2)}) collective-permute-start(f32[2,16,256]{2,1,0:T(8,128)S(1)} %sum_kernel.5.refs_1_.base_ref), channel_id=1, source_target_pairs={{0,4},{1,5},{8,12},{9,13},{16,20},{17,21},{24,28},{25,29},{32,36},... | collective-permute-start | bytes 98312 | tf_op jit(solution)/shard_map/ppermute | solution.py:270
  28.9 5.1 %collective-permute-start.7 = (f32[2,16,256]{2,1,0:T(8,128)S(1)}, f32[2,16,256]{2,1,0:T(8,128)S(1)}, u32[]{:S(2)}, u32[]{:S(2)}) collective-permute-start(f32[2,16,256]{2,1,0:T(8,128)S(1)} %sum_kernel.5.refs_1_.base_ref), channel_id=1, source_target_pairs={{0,30},{1,31},{8,6},{9,7},{16,14},{17,15},{24,22},{25,23},{32,62},... | collective-permute-start | bytes 98312 | tf_op jit(solution)/shard_map/ppermute | solution.py:270
  31.5 2.6 %collective-permute-start.6 = (f32[2,16,256]{2,1,0:T(8,128)S(1)}, f32[2,16,256]{2,1,0:T(8,128)S(1)}, u32[]{:S(2)}, u32[]{:S(2)}) collective-permute-start(f32[2,16,256]{2,1,0:T(8,128)S(1)} %sum_kernel.5.refs_1_.base_ref), channel_id=1, source_target_pairs={{0,2},{1,3},{8,10},{9,11},{16,18},{17,19},{24,26},{25,27},{32,34},... | collective-permute-start | bytes 98312 | tf_op jit(solution)/shard_map/ppermute | solution.py:270
  35.2 18.3 %all-to-all-start.3 = ((f32[16,4,16,256]{3,2,1,0:T(8,128)}), f32[16,4,16,256]{3,2,1,0:T(8,128)S(1)}, u32[]{:S(2)}, u32[]{:S(2)}) async-start(f32[16,4,16,256]{3,2,1,0:T(8,128)} %spread_kernel.1.refs_2_), calls=%async_computation.3 | async-start | bytes 2097152 | tf_op jit(solution)/shard_map/all_to_all | solution.py:293
  38.9 13.2 %collective-permute-start.5 = (f32[512,256]{1,0:T(8,128)S(1)}, f32[512,256]{1,0:T(8,128)S(1)}, u32[]{:S(2)}, u32[]{:S(2)}) collective-permute-start(f32[512,256]{1,0:T(8,128)S(1)} %sum_kernel.6.order_ref.refs_0_), channel_id=1, source_target_pairs={{0,8},{1,25},{14,22},{19,11},{32,40},{33,57},{46,54},{51,43},{64,7... | collective-permute-start | bytes 1572872 | tf_op jit(solution)/shard_map/ppermute | solution.py:270
  46.0 13.3 %collective-permute-start.10 = (f32[512,256]{1,0:T(8,128)S(1)}, f32[512,256]{1,0:T(8,128)S(1)}, u32[]{:S(2)}, u32[]{:S(2)}) collective-permute-start(f32[512,256]{1,0:T(8,128)S(1)} %get-tuple-element.26.refs_0_), channel_id=1, source_target_pairs={{0,1},{1,0},{32,33},{33,32},{64,65},{65,64},{96,97},{97,96},{128,1... | collective-permute-start | bytes 1572872 | tf_op jit(solution)/shard_map/ppermute | solution.py:258
  52.1 15.2 %collective-permute-start.9 = (f32[512,256]{1,0:T(8,128)S(1)}, f32[512,256]{1,0:T(8,128)S(1)}, u32[]{:S(2)}, u32[]{:S(2)}) collective-permute-start(f32[512,256]{1,0:T(8,128)S(1)} %sum_kernel.7.refs_1_.refs_0_), channel_id=1, source_target_pairs={{0,4},{1,29},{14,12},{19,21},{8,16},{25,17},{22,26},{11,7},{32,36}... | collective-permute-start | bytes 1572872 | tf_op jit(solution)/shard_map/ppermute | solution.py:270
  53.5 17.9 %collective-permute-start.12 = (f32[16,16,256]{2,1,0:T(8,128)S(1)}, f32[16,16,256]{2,1,0:T(8,128)S(1)}, u32[]{:S(2)}, u32[]{:S(2)}) collective-permute-start(f32[16,16,256]{2,1,0:T(8,128)S(1)} %pick_kernel.1), channel_id=1, source_target_pairs={{0,1},{1,0},{2,3},{3,2},{4,5},{5,4},{6,7},{7,6},{8,9},{9,8},{10,11... | collective-permute-start | bytes 786440 | tf_op jit(solution)/shard_map/ppermute | solution.py:258
  67.4 12.9 %collective-permute-start.11 = (f32[512,256]{1,0:T(8,128)S(1)}, f32[512,256]{1,0:T(8,128)S(1)}, u32[]{:S(2)}, u32[]{:S(2)}) collective-permute-start(f32[512,256]{1,0:T(8,128)S(1)} %sum_kernel.8.refs_3_.refs_0_), channel_id=1, source_target_pairs={{0,30},{1,3},{4,2},{29,31},{8,6},{25,27},{12,10},{21,23},{14,20},{... | collective-permute-start | bytes 1572872 | tf_op jit(solution)/shard_map/ppermute | solution.py:270
  80.4 1.5 %collective-permute-start.13 = (f32[512,256]{1,0:T(8,128)S(1)}, f32[512,256]{1,0:T(8,128)S(1)}, u32[]{:S(2)}, u32[]{:S(2)}) collective-permute-start(f32[512,256]{1,0:T(8,128)S(1)} %sum_kernel.9.refs_5_.refs_1_), channel_id=1, source_target_pairs={{2,3},{3,2},{4,5},{5,4},{6,7},{7,6},{8,9},{9,8},{10,11},{11,10},{1... | collective-permute-start | bytes 1572872 | tf_op jit(solution)/shard_map/ppermute | solution.py:258
